TPU v7x, 128 devices: a whole 4x4x4 slice. The times are simulated.
128 devices in a mesh: dp: 2 (over core), expert: 64 (over z, y, x).
Axes of the slice: x: 4, y: 4, z: 4, core: 2. Of those that a mesh axis runs over, the one named last changes fastest.
Arguments:
- tokens: bfloat16 [16384, 4096], P(('dp', 'expert')), may hold values from -6 to 6
- cotangent: bfloat16 [16384, 4096], P(('dp', 'expert')), may hold values from -6 to 6
- routing: int32 [16384, 2], P(('dp', 'expert')), may hold values from 0 to 63, as said below
- combine_weights: float32 [16384, 2], P(('dp', 'expert')), may hold values from 0.05 to 0.3
- w_gate: bfloat16 [64, 4096, 768], P('expert', None, 'dp'), may hold values from -0.09375 to 0.09375
- w_up: bfloat16 [64, 4096, 768], P('expert', None, 'dp'), may hold values from -0.09375 to 0.09375
- w_down: bfloat16 [64, 768, 4096], P('expert', 'dp'), may hold values from -0.21875 to 0.21875
Outputs:
- combined: bfloat16 [16384, 4096], P(('dp', 'expert'))
- token_grad: bfloat16 [16384, 4096], P(('dp', 'expert'))
- gate_weight_grad: bfloat16 [64, 4096, 768], P('expert', None, 'dp')
- up_weight_grad: bfloat16 [64, 4096, 768], P('expert', None, 'dp')
- down_weight_grad: bfloat16 [64, 768, 4096], P('expert', 'dp')
Inputs may be any that keep to these rules, and one draw needn't show every extreme that they name: `routing`: each row names 2 different experts. The same 4 experts are named by exactly 8 of the 128 rows of every device; each of the other 60 experts is named by 3 or 4 rows of every device.
All inputs are finite; a program needn't handle non-finite values.
Results may differ from a plain program's by a relative error of at most 0.0065.
Values may be sent and summed in bfloat16 or wider, within the bound.
No kernel may reach another device: no remote copies, remote signals or barrier semaphores. Data moves between devices by JAX's collectives and lax.ppermute only.
A program may use at most 256 MiB of HBM per device.

v0:
```python
import jax
import jax.numpy as jnp
from jax import lax
from jax.sharding import PartitionSpec as P

HOT = 4


def silu_parts(gate_pre):
    sig_gate = jax.nn.sigmoid(gate_pre)
    return (gate_pre * sig_gate, sig_gate)


def expert_pass(row_tokens, route_grad, gate_matrix, up_matrix, down_matrix):
    gate_pre = jnp.dot(row_tokens, gate_matrix, preferred_element_type=jnp.float32)
    up_pre = jnp.dot(row_tokens, up_matrix, preferred_element_type=jnp.float32)
    activated, sig_gate = silu_parts(gate_pre)
    hidden = (activated * up_pre).astype(jnp.bfloat16)
    expert_out = jnp.dot(hidden, down_matrix, preferred_element_type=jnp.float32)
    hidden_grad = jnp.dot(route_grad, down_matrix.T, preferred_element_type=jnp.float32)
    up_grad = (hidden_grad * activated).astype(jnp.bfloat16)
    gate_grad = (hidden_grad * up_pre * sig_gate * (1.0 + gate_pre * (1.0 - sig_gate))).astype(
        jnp.bfloat16
    )
    input_grad = jnp.dot(gate_grad, gate_matrix.T, preferred_element_type=jnp.float32) + jnp.dot(
        up_grad, up_matrix.T, preferred_element_type=jnp.float32
    )
    gate_wgrad = jnp.dot(row_tokens.T, gate_grad, preferred_element_type=jnp.float32)
    up_wgrad = jnp.dot(row_tokens.T, up_grad, preferred_element_type=jnp.float32)
    down_wgrad = jnp.dot(hidden.T, route_grad, preferred_element_type=jnp.float32)
    return (expert_out, input_grad, gate_wgrad, up_wgrad, down_wgrad)


def local(tokens, cotangent, routing, combine_weights, w_gate, w_up, w_down):
    tok_rows, features = tokens.shape
    top_count = routing.shape[1]
    experts = lax.axis_size("expert")
    cold_count = experts - HOT
    hot_cap = 2 * tok_rows * top_count // experts
    cold_cap = (tok_rows * top_count - HOT * hot_cap + cold_count - 1) // cold_count
    capacity = max(hot_cap, cold_cap)
    local_rows = experts * capacity
    flat_ids = routing.reshape(-1)
    expert_ids = jnp.arange(experts, dtype=jnp.int32)
    matches = (flat_ids[:, None] == expert_ids[None, :]).astype(jnp.int32)
    before = jnp.cumsum(matches, axis=0) - matches
    slot_ids = jnp.sum(before * matches, axis=1)
    position = (flat_ids * capacity + slot_ids).reshape(tok_rows, top_count)
    targets = jnp.arange(local_rows, dtype=jnp.int32)
    selected = position[None, :, :] == targets[:, None, None]
    picker = jnp.any(selected, axis=2).astype(jnp.bfloat16)
    slot_weight = jnp.sum(jnp.where(selected, combine_weights[None, :, :], 0.0), axis=(1, 2))
    send_rows = jnp.dot(picker, tokens, preferred_element_type=jnp.float32).astype(jnp.bfloat16)
    picked_grads = jnp.dot(picker, cotangent, preferred_element_type=jnp.float32)
    send_grads = (slot_weight[:, None] * picked_grads).astype(jnp.bfloat16)
    rows_in, grads_in = (
        lax.all_to_all(
            send_rows.reshape(experts, capacity, features),
            "expert",
            split_axis=0,
            concat_axis=0,
            tiled=True,
        ),
        lax.all_to_all(
            send_grads.reshape(experts, capacity, features),
            "expert",
            split_axis=0,
            concat_axis=0,
            tiled=True,
        ),
    )
    rows_in = rows_in.reshape(local_rows, features)
    grads_in = grads_in.reshape(local_rows, features)
    rows_all, grads_all = (
        lax.all_gather(rows_in, "dp", axis=0, tiled=True),
        lax.all_gather(grads_in, "dp", axis=0, tiled=True),
    )
    out_part, input_part, gate_wgrad, up_wgrad, down_wgrad = expert_pass(
        rows_all, grads_all, w_gate[0], w_up[0], w_down[0]
    )
    out_sum, input_sum = (
        lax.psum_scatter(out_part, "dp", scatter_dimension=0, tiled=True),
        lax.psum_scatter(input_part, "dp", scatter_dimension=0, tiled=True),
    )
    out_rows = out_sum.astype(jnp.bfloat16).reshape(experts, capacity, features)
    input_rows = input_sum.astype(jnp.bfloat16).reshape(experts, capacity, features)
    out_back, input_back = (
        lax.all_to_all(out_rows, "expert", split_axis=0, concat_axis=0, tiled=True),
        lax.all_to_all(input_rows, "expert", split_axis=0, concat_axis=0, tiled=True),
    )
    out_flat = out_back.reshape(local_rows, features)
    combined = jnp.zeros((tok_rows, features), jnp.float32)
    for column in range(top_count):
        column_pick = (position[:, column][:, None] == targets[None, :]).astype(jnp.bfloat16)
        column_rows = jnp.dot(column_pick, out_flat, preferred_element_type=jnp.float32)
        combined = combined + combine_weights[:, column][:, None] * column_rows
    token_grad = jnp.dot(
        picker.T, input_back.reshape(local_rows, features), preferred_element_type=jnp.float32
    ).astype(jnp.bfloat16)
    return (
        combined.astype(jnp.bfloat16),
        token_grad,
        gate_wgrad.astype(jnp.bfloat16)[None],
        up_wgrad.astype(jnp.bfloat16)[None],
        down_wgrad.astype(jnp.bfloat16)[None],
    )


def solution(mesh):
    in_specs = (
        P(("dp", "expert"), None),
        P(("dp", "expert"), None),
        P(("dp", "expert"), None),
        P(("dp", "expert"), None),
        P("expert", None, "dp"),
        P("expert", None, "dp"),
        P("expert", "dp", None),
    )
    out_specs = (
        P(("dp", "expert"), None),
        P(("dp", "expert"), None),
        P("expert", None, "dp"),
        P("expert", None, "dp"),
        P("expert", "dp", None),
    )
    return jax.shard_map(local, mesh=mesh, in_specs=in_specs, out_specs=out_specs, check_vma=False)
```

profile of v0, /device:TPU:0, one launch (start us, length us, event | category | flops | bytes accessed | tf_op | source)
XLA Modules:
  0.0 366.3 jit_solution(15104058964655476949)
XLA Ops:
  7.2 0.0 copy-start
  7.2 0.0 all-gather.3.cloned.1.call-start
  7.2 0.9 copy.32
  8.2 0.1 eq.72
  8.3 0.1 eq.68
  8.5 0.6 reduce-window.6
  9.1 0.2 slice_reduce_fusion
  9.3 0.1 fusion.27
  9.4 0.1 reduce_sum.21
  9.6 0.1 copy.35
  9.6 0.7 multiply_add_fusion
  10.3 0.1 fusion.22
  10.4 2.5 fusion.1
  12.9 64.0 %all_to_all.20 = bf16[64,8,4096]{2,1,0:T(8,128)(2,1)} all-to-all(bf16[64,8,4096]{2,1,0:T(8,128)(2,1)S(1)} %fusion.1), channel_id=1, replica_groups=mesh['dp'=2,'expert'=64] {'expert'}, dimensions={0} | all-to-all | bytes 8388608 | tf_op jit(solution)/shard_map/all_to_all | solution.py:57
  76.8 0.0 all-gather.3.cloned.1.call-update
  76.8 0.0 all-gather.5.cloned.1.call-start
  76.9 0.6 copy-done.10
  77.5 0.2 select_reduce_fusion
  77.7 2.5 fusion
  80.1 58.5 %all_to_all.21 = bf16[64,8,4096]{2,1,0:T(8,128)(2,1)} all-to-all(bf16[64,8,4096]{2,1,0:T(8,128)(2,1)S(1)} %fusion), channel_id=1, replica_groups=mesh['dp'=2,'expert'=64] {'expert'}, dimensions={0} | all-to-all | bytes 8388608 | tf_op jit(solution)/shard_map/all_to_all | solution.py:64
  138.6 0.0 all-gather.5.cloned.1.call-update
  138.6 0.2 reduce-scatter.5.cloned.1.call-start
  138.9 0.0 all-gather.3.cloned.1.call-done
  138.9 0.0 copy-start.2
  138.9 0.0 copy-start.11
  138.9 10.0 %fusion.15 = f32[1024,384]{1,0:T(8,128)} fusion(bf16[1024,4096]{1,0:T(8,128)(2,1)} %all-gather.3.cloned.1.call-done, bf16[1,4096,384]{2,1,0:T(8,128)(2,1)} %param.12), kind=kOutput, calls=%fused_computation.26 | convolution fusion | flops 3221225472 | bytes 13107200 | tf_op jit(solution)/shard_map/dot_general | solution.py:16
  149.0 0.0 copy-done.2
  149.0 0.0 copy-done.11
  149.0 5.6 %fusion.19 = f32[1024,384]{1,0:T(8,128)} fusion(bf16[1024,4096]{1,0:T(8,128)(2,1)S(1)} %copy-done.11, bf16[1,4096,384]{2,1,0:T(8,128)(2,1)S(1)} %copy-done.2), kind=kOutput, calls=%fused_computation.30 | convolution fusion | flops 3221225472 | bytes 13107200 | tf_op jit(solution)/shard_map/dot_general | solution.py:15
  154.6 3.6 all-gather.5.cloned.1.call-done
  158.2 0.0 copy-done
  158.2 10.3 %multiply_convert_fusion.1 = (bf16[1024,384]{1,0:T(8,128)(2,1)S(1)}, bf16[1024,384]{1,0:T(8,128)(2,1)S(1)}, bf16[1024,384]{1,0:T(8,128)(2,1)}) fusion(f32[1024,384]{1,0:T(8,128)} %fusion.19, f32[1024,384]{1,0:T(8,128)} %fusion.15, bf16[1024,4096]{1,0:T(8,128)(2,1)} %all-gather.5.cloned.1.call-done, bf16[1,384,4096]{2,1,0:T(8,128)(2,1)S(1)} %copy-done), kind=kOutput, calls=%fused_computation.32 | convolution fusion | flops 3227123712 | bytes 17039360 | tf_op jit(solution)/shard_map/dot_general | solution.py:20
  168.4 0.0 copy-done.3
  168.5 8.3 %fusion.17 = f32[1024,4096]{1,0:T(8,128)} fusion(bf16[1024,384]{1,0:T(8,128)(2,1)S(1)} %get-tuple-element.6, bf16[1,4096,384]{2,1,0:T(8,128)(2,1)S(1)} %copy-done.3), kind=kOutput, calls=%fused_computation.28 | convolution fusion | flops 3221225472 | bytes 20709376 | tf_op jit(solution)/shard_map/dot_general | solution.py:25
  176.8 0.0 copy-done.7
  176.8 0.0 copy-done.5
  176.8 0.0 copy-done.4
  176.8 11.5 %convolution_add_fusion = f32[1024,4096]{1,0:T(8,128)} fusion(f32[1024,4096]{1,0:T(8,128)} %fusion.17, bf16[1024,384]{1,0:T(8,128)(2,1)S(1)} %get-tuple-element.5, bf16[1,4096,384]{2,1,0:T(8,128)(2,1)S(1)} %copy-done.4), kind=kOutput, calls=%fused_computation.1 | convolution fusion | flops 3225419776 | bytes 37486592 | tf_op jit(solution)/shard_map/dot_general | solution.py:25
  188.2 0.0 reduce-scatter.5.cloned.1.call-update
  188.3 0.0 reduce-scatter.3.cloned.1.call-start
  188.3 9.2 %fusion.12 = f32[1024,4096]{1,0:T(8,128)} fusion(bf16[1024,384]{1,0:T(8,128)(2,1)} %get-tuple-element.7, bf16[1,384,4096]{2,1,0:T(8,128)(2,1)S(1)} %copy-done), kind=kOutput, calls=%fused_computation.23 | convolution fusion | flops 3221225472 | bytes 20709376 | tf_op jit(solution)/shard_map/dot_general | solution.py:19
  197.5 0.0 reduce-scatter.3.cloned.1.call-update
  197.5 21.2 %reduce-scatter.5.cloned.1.call-done = f32[512,4096]{1,0:T(8,128)} async-done(((f32[1024,4096]{1,0:T(8,128)}), f32[512,4096]{1,0:T(8,128)}) %reduce-scatter.5.cloned.1.call-update) | async-done | bytes 8388624 | tf_op jit(solution)/shard_map/reduce_scatter | solution.py:83
  218.8 6.0 %convert_bitcast_fusion = bf16[64,8,4096]{2,1,0:T(8,128)(2,1)} fusion(f32[512,4096]{1,0:T(8,128)} %reduce-scatter.5.cloned.1.call-done), kind=kLoop, calls=%fused_computation.19 | loop fusion | flops 2097152 | bytes 12582912 | tf_op jit(solution)/shard_map/reshape | solution.py:86
  224.7 10.7 %all-to-all-start.3 = ((bf16[64,8,4096]{2,1,0:T(8,128)(2,1)}), bf16[64,8,4096]{2,1,0:T(8,128)(2,1)}, u32[]{:S(2)}, u32[]{:S(2)}) async-start(bf16[64,8,4096]{2,1,0:T(8,128)(2,1)} %convert_bitcast_fusion), calls=%async_computation.5 | async-start | bytes 8388608 | tf_op jit(solution)/shard_map/all_to_all | solution.py:89
  235.4 16.1 %reduce-scatter.3.cloned.1.call-done = f32[512,4096]{1,0:T(8,128)} async-done(((f32[1024,4096]{1,0:T(8,128)}), f32[512,4096]{1,0:T(8,128)}) %reduce-scatter.3.cloned.1.call-update) | async-done | bytes 8388624 | tf_op jit(solution)/shard_map/reduce_scatter | solution.py:82
  251.5 6.0 %convert_bitcast_fusion.1 = bf16[64,8,4096]{2,1,0:T(8,128)(2,1)} fusion(f32[512,4096]{1,0:T(8,128)} %reduce-scatter.3.cloned.1.call-done), kind=kLoop, calls=%fused_computation.20 | loop fusion | flops 2097152 | bytes 12582912 | tf_op jit(solution)/shard_map/reshape | solution.py:85
  257.5 32.5 %all-to-all-done.3 = bf16[64,8,4096]{2,1,0:T(8,128)(2,1)} async-done(((bf16[64,8,4096]{2,1,0:T(8,128)(2,1)}), bf16[64,8,4096]{2,1,0:T(8,128)(2,1)}, u32[]{:S(2)}, u32[]{:S(2)}) %all-to-all-start.3) | async-done | bytes 4194336 | tf_op jit(solution)/shard_map/all_to_all | solution.py:89
  290.0 9.7 %all-to-all-start.1 = ((bf16[64,8,4096]{2,1,0:T(8,128)(2,1)}), bf16[64,8,4096]{2,1,0:T(8,128)(2,1)}, u32[]{:S(2)}, u32[]{:S(2)}) async-start(bf16[64,8,4096]{2,1,0:T(8,128)(2,1)} %convert_bitcast_fusion.1), calls=%async_computation.2 | async-start | bytes 8388608 | tf_op jit(solution)/shard_map/all_to_all | solution.py:88
  299.7 0.0 copy-done.9
  299.7 0.0 copy-start.6
  299.7 0.0 slice-start
  299.7 8.7 %fusion.4 = bf16[1,384,4096]{2,1,0:T(8,128)(2,1)} fusion(bf16[1024,384]{1,0:T(8,128)(2,1)S(1)} %copy-done.9, bf16[1024,4096]{1,0:T(8,128)(2,1)} %all-gather.5.cloned.1.call-done), kind=kOutput, calls=%fused_computation.10 | convolution fusion | flops 3222798336 | bytes 12320768 | tf_op jit(solution)/shard_map/dot_general | solution.py:30
  308.4 0.0 copy-done.6
  308.4 9.5 %fusion.3 = bf16[1,4096,384]{2,1,0:T(8,128)(2,1)} fusion(bf16[1024,4096]{1,0:T(8,128)(2,1)} %all-gather.3.cloned.1.call-done, bf16[1024,384]{1,0:T(8,128)(2,1)S(1)} %copy-done.6), kind=kOutput, calls=%fused_computation.9 | convolution fusion | flops 3222798336 | bytes 12320768 | tf_op jit(solution)/shard_map/dot_general | solution.py:29
  317.9 0.0 slice-done
  317.9 0.0 copy-done.8
  317.9 0.0 slice-done.1
  317.9 6.1 %fusion.2 = bf16[1,4096,384]{2,1,0:T(8,128)(2,1)} fusion(bf16[1024,4096]{1,0:T(8,128)(2,1)S(1)} %bitcast.88, bf16[1024,384]{1,0:T(8,128)(2,1)S(1)} %copy-done.8), kind=kOutput, calls=%fused_computation.8 | convolution fusion | flops 3222798336 | bytes 12320768 | tf_op jit(solution)/shard_map/dot_general | solution.py:28
  324.0 3.9 %convolution_convert_fusion.4 = bf16[128,4096]{1,0:T(8,128)(2,1)} fusion(pred[512,128]{1,0:T(8,128)(4,1)S(1)} %fusion.22, bf16[64,8,4096]{2,1,0:T(8,128)(2,1)} %all-to-all-done.3), kind=kOutput, calls=%fused_computation.15 | convolution fusion | flops 537395200 | bytes 5308416 | tf_op jit(solution)/shard_map/dot_general | solution.py:97
  327.9 24.7 %all-to-all-done.1 = bf16[64,8,4096]{2,1,0:T(8,128)(2,1)} async-done(((bf16[64,8,4096]{2,1,0:T(8,128)(2,1)}), bf16[64,8,4096]{2,1,0:T(8,128)(2,1)}, u32[]{:S(2)}, u32[]{:S(2)}) %all-to-all-start.1) | async-done | bytes 4194336 | tf_op jit(solution)/shard_map/all_to_all | solution.py:88
  352.6 3.1 convolution_multiply_fusion.1
  355.7 4.0 %fusion.6 = bf16[128,4096]{1,0:T(8,128)(2,1)} fusion(f32[128,4096]{1,0:T(8,128)S(1)} %convolution_multiply_fusion.1, bf16[64,8,4096]{2,1,0:T(8,128)(2,1)} %all-to-all-done.1, f32[128]{0:T(128)S(1)} %get-tuple-element.10, s32[128]{0:T(128)S(1)} %get-tuple-element.8), kind=kOutput, calls=%fused_computation.14 | convolution fusion | flops 538509312 | bytes 7341056 | tf_op jit(solution)/shard_map/dot_general | solution.py:95
  359.8 0.0 copy-done.1
  (15 shorter events, 0.1 us)
Async XLA Ops:
  7.2 151.0 %copy-start = (bf16[1,384,4096]{2,1,0:T(8,128)(2,1)S(1)}, bf16[1,384,4096]{2,1,0:T(8,128)(2,1)}, u32[]{:S(2)}) copy-start(bf16[1,384,4096]{2,1,0:T(8,128)(2,1)} %param.13) | copy-start | bytes 9437188
  7.2 131.7 %all-gather.3.cloned.1.call-start = ((), (), s32[]{:S(2)}) async-start(), calls=%async_computation.6 | async-start | bytes 12582912 | tf_op jit(solution)/shard_map/all_gather | solution.py:75
  76.8 0.7 copy-start.10
  76.8 81.3 %all-gather.5.cloned.1.call-start = ((), (), s32[]{:S(2)}) async-start(), calls=%async_computation.8 | async-start | bytes 12582912 | tf_op jit(solution)/shard_map/all_gather | solution.py:76
  138.6 80.1 %reduce-scatter.5.cloned.1.call-start = ((), (), s32[]{:S(2)}) async-start(), calls=%async_computation.9 | async-start | bytes 25165824 | tf_op jit(solution)/shard_map/reduce_scatter | solution.py:83
  138.9 10.1 %copy-start.2 = (bf16[1,4096,384]{2,1,0:T(8,128)(2,1)S(1)}, bf16[1,4096,384]{2,1,0:T(8,128)(2,1)}, u32[]{:S(2)}) copy-start(bf16[1,4096,384]{2,1,0:T(8,128)(2,1)} %param.11) | copy-start | bytes 9437188
  138.9 10.1 %copy-start.11 = (bf16[1024,4096]{1,0:T(8,128)(2,1)S(1)}, bf16[1024,4096]{1,0:T(8,128)(2,1)}, u32[]{:S(2)}) copy-start(bf16[1024,4096]{1,0:T(8,128)(2,1)} %all-gather.3.cloned.1.call-done) | copy-start | bytes 25165828
  158.2 10.3 %copy-start.3 = (bf16[1,4096,384]{2,1,0:T(8,128)(2,1)S(1)}, bf16[1,4096,384]{2,1,0:T(8,128)(2,1)}, u32[]{:S(2)}) copy-start(bf16[1,4096,384]{2,1,0:T(8,128)(2,1)} %param.11) | copy-start | bytes 9437188
  168.4 8.3 %copy-start.7 = (bf16[1024,384]{1,0:T(8,128)(2,1)}, bf16[1024,384]{1,0:T(8,128)(2,1)S(1)}, u32[]{:S(2)}) copy-start(bf16[1024,384]{1,0:T(8,128)(2,1)S(1)} %get-tuple-element.6) | copy-start | bytes 2359300
  168.4 8.3 %copy-start.5 = (bf16[1024,384]{1,0:T(8,128)(2,1)}, bf16[1024,384]{1,0:T(8,128)(2,1)S(1)}, u32[]{:S(2)}) copy-start(bf16[1024,384]{1,0:T(8,128)(2,1)S(1)} %get-tuple-element.5) | copy-start | bytes 2359300
  168.4 8.3 %copy-start.4 = (bf16[1,4096,384]{2,1,0:T(8,128)(2,1)S(1)}, bf16[1,4096,384]{2,1,0:T(8,128)(2,1)}, u32[]{:S(2)}) copy-start(bf16[1,4096,384]{2,1,0:T(8,128)(2,1)} %param.12) | copy-start | bytes 9437188
  188.3 63.3 %reduce-scatter.3.cloned.1.call-start = ((), (), s32[]{:S(2)}) async-start(), calls=%async_computation.7 | async-start | bytes 25165824 | tf_op jit(solution)/shard_map/reduce_scatter | solution.py:82
  224.7 65.2 %all-to-all-start.3 = ((bf16[64,8,4096]{2,1,0:T(8,128)(2,1)}), bf16[64,8,4096]{2,1,0:T(8,128)(2,1)}, u32[]{:S(2)}, u32[]{:S(2)}) async-start(bf16[64,8,4096]{2,1,0:T(8,128)(2,1)} %convert_bitcast_fusion), calls=%async_computation.5 | async-start | bytes 8388608 | tf_op jit(solution)/shard_map/all_to_all | solution.py:89
  257.5 42.2 %copy-start.9 = (bf16[1024,384]{1,0:T(8,128)(2,1)S(1)}, bf16[1024,384]{1,0:T(8,128)(2,1)}, u32[]{:S(2)}) copy-start(bf16[1024,384]{1,0:T(8,128)(2,1)} %get-tuple-element.7) | copy-start | bytes 2359300
  290.0 62.6 %all-to-all-start.1 = ((bf16[64,8,4096]{2,1,0:T(8,128)(2,1)}), bf16[64,8,4096]{2,1,0:T(8,128)(2,1)}, u32[]{:S(2)}, u32[]{:S(2)}) async-start(bf16[64,8,4096]{2,1,0:T(8,128)(2,1)} %convert_bitcast_fusion.1), calls=%async_computation.2 | async-start | bytes 8388608 | tf_op jit(solution)/shard_map/all_to_all | solution.py:88
  299.7 8.7 %copy-start.6 = (bf16[1024,384]{1,0:T(8,128)(2,1)S(1)}, bf16[1024,384]{1,0:T(8,128)(2,1)}, u32[]{:S(2)}) copy-start(bf16[1024,384]{1,0:T(8,128)(2,1)} %copy-done.5) | copy-start | bytes 2359300
  299.7 18.2 %slice-start = ((s8[8388608]{0:T(1024)(128)(4,1)}), s8[4194304]{0:T(1024)(128)(4,1)S(1)}, s32[]{:S(2)}) async-start(s8[8388608]{0:T(1024)(128)(4,1)} %bitcast.87), calls=%async_computation.10 | async-start | bytes 8388608
  308.4 9.5 %copy-start.8 = (bf16[1024,384]{1,0:T(8,128)(2,1)S(1)}, bf16[1024,384]{1,0:T(8,128)(2,1)}, u32[]{:S(2)}) copy-start(bf16[1024,384]{1,0:T(8,128)(2,1)} %copy-done.7) | copy-start | bytes 2359300
  308.4 9.5 %slice-start.1 = ((s8[8388608]{0:T(1024)(128)(4,1)}), s8[4194304]{0:T(1024)(128)(4,1)S(1)}, s32[]{:S(2)}) async-start(s8[8388608]{0:T(1024)(128)(4,1)} %bitcast.87), calls=%async_computation.11 | async-start | bytes 8388608
  352.6 7.1 %copy-start.1 = (bf16[1,384,4096]{2,1,0:T(8,128)(2,1)S(1)}, bf16[1,384,4096]{2,1,0:T(8,128)(2,1)}, u32[]{:S(2)}) copy-start(bf16[1,384,4096]{2,1,0:T(8,128)(2,1)} %param.13) | copy-start | bytes 9437188
Sparse Core Ops, SparseCore 0:
  77.0 19.3 all-gather.2
  138.8 19.3 all-gather.4
  188.4 30.3 reduce-scatter.4
  221.2 30.3 reduce-scatter.2
where the time goes:
time: 367 us; the launch traced here: 366 us
  blocking collectives  122 us (33%)
  waiting for transfers between devices  98.2 us (27%)
  matrix products  95.1 us (26%)
  starting transfers between devices  20.7 us (6%)
  between operations  13.9 us (4%)
  other arithmetic  13.6 us (4%)
    all_to_all x1, blocking collectives, local(): lax.all_to_all(send_rows.reshape(experts, capacity, features), 'expert',...  64 us
    all_to_all x1, blocking collectives, local(): lax.all_to_all(send_grads.reshape(experts, capacity, features), 'expert',...  58.5 us
    all_to_all x1, waiting for transfers between devices, local(): lax.all_to_all(input_rows, 'expert', split_axis=0, concat_axis=0, tiled=T...  32.5 us
    all_to_all x1, waiting for transfers between devices, local(): lax.all_to_all(out_rows, 'expert', split_axis=0, concat_axis=0, tiled=True)  24.7 us
    reduce_scatter x1, waiting for transfers between devices, local(): lax.psum_scatter(input_part, 'dp', scatter_dimension=0, tiled=True)  21.2 us
    reduce_scatter x1, waiting for transfers between devices, local(): lax.psum_scatter(out_part, 'dp', scatter_dimension=0, tiled=True)  16.1 us
    dot_general x1, matrix products, expert_pass(): jnp.dot(up_grad, up_matrix.T, preferred_element_type=jnp.float32)  11.5 us
    all_to_all x1, starting transfers between devices, local(): lax.all_to_all(input_rows, 'expert', split_axis=0, concat_axis=0, tiled=T...  10.7 us
  transfers between devices with their start and end apart: 6, of which 5 were waited for; matrix products, arithmetic and copies ran while one was open for 18% of the time, Pallas kernels for 0%

commit v1 on v0

v1 whole, which is shorter than its diff:
```python
import jax
import jax.numpy as jnp
from jax import lax
from jax.experimental import pallas as pl
from jax.experimental.pallas import tpu as pltpu
from jax.sharding import PartitionSpec as P

HOT = 4
BLOCK = 256
BF16 = jnp.bfloat16
F32 = jnp.float32


def dot(left, right, dims):
    return lax.dot_general(left, right, (dims, ((), ())), preferred_element_type=F32)


def swap(value):
    return lax.ppermute(value, "dp", [(0, 1), (1, 0)])


def exchange(value, experts):
    rows, features = value.shape
    parts = value.reshape(experts, rows // experts, features)
    moved = lax.all_to_all(parts, "expert", split_axis=0, concat_axis=0, tiled=True)
    return moved.reshape(rows, features)


def hidden_parts(rows, gate_matrix, up_matrix):
    gate_pre = dot(rows, gate_matrix, ((1,), (0,)))
    up_pre = dot(rows, up_matrix, ((1,), (0,)))
    sig_gate = jax.nn.sigmoid(gate_pre)
    activated = gate_pre * sig_gate
    hidden = (activated * up_pre).astype(BF16)
    gate_slope = up_pre * sig_gate * (1.0 + gate_pre * (1.0 - sig_gate))
    return hidden, activated, gate_slope


def hidden_kernel(rows_ref, gate_ref, up_ref, hidden_ref, act_ref, slope_ref):
    hidden_ref[...], act_ref[...], slope_ref[...] = hidden_parts(rows_ref[...], gate_ref[...], up_ref[...])


def forward_kernel(rows_ref, gate_ref, up_ref, down_ref, hidden_ref, act_ref, slope_ref, out_ref):
    hidden, act_ref[...], slope_ref[...] = hidden_parts(rows_ref[...], gate_ref[...], up_ref[...])
    hidden_ref[...] = hidden
    out_ref[...] = dot(hidden, down_ref[...], ((1,), (0,))).astype(BF16)


def out_kernel(hidden_ref, peer_ref, down_ref, out_ref):
    total = dot(hidden_ref[...], down_ref[...], ((1,), (0,))) + peer_ref[...].astype(F32)
    out_ref[...] = total.astype(BF16)


def grad_parts(grads, act, slope, down_matrix):
    hidden_grad = dot(grads, down_matrix, ((1,), (1,)))
    return (hidden_grad * slope).astype(BF16), (hidden_grad * act).astype(BF16)


def input_parts(gate_grad, up_grad, gate_matrix, up_matrix):
    return dot(gate_grad, gate_matrix, ((1,), (1,))) + dot(up_grad, up_matrix, ((1,), (1,)))


def grad_kernel(grads_ref, act_ref, slope_ref, down_ref, gate_grad_ref, up_grad_ref):
    gate_grad_ref[...], up_grad_ref[...] = grad_parts(grads_ref[...], act_ref[...], slope_ref[...], down_ref[...])


def backward_kernel(grads_ref, act_ref, slope_ref, gate_ref, up_ref, down_ref, gate_grad_ref, up_grad_ref, input_ref):
    gate_grad, up_grad = grad_parts(grads_ref[...], act_ref[...], slope_ref[...], down_ref[...])
    gate_grad_ref[...] = gate_grad
    up_grad_ref[...] = up_grad
    input_ref[...] = input_parts(gate_grad, up_grad, gate_ref[...], up_ref[...]).astype(BF16)


def input_kernel(gate_grad_ref, up_grad_ref, peer_ref, gate_ref, up_ref, input_ref):
    total = input_parts(gate_grad_ref[...], up_grad_ref[...], gate_ref[...], up_ref[...])
    input_ref[...] = (total + peer_ref[...].astype(F32)).astype(BF16)


def by_rows(kernel, row_args, matrices, outs):
    rows = row_args[0].shape[0]
    in_specs = [pl.BlockSpec((BLOCK, arg.shape[1]), lambda i: (i, 0)) for arg in row_args]
    in_specs += [
        pl.BlockSpec(matrix.shape, lambda i: (0, 0), pipeline_mode=pl.Buffered(1)) for matrix in matrices
    ]
    return pl.pallas_call(
        kernel,
        grid=(rows // BLOCK,),
        in_specs=in_specs,
        out_specs=[pl.BlockSpec((BLOCK, columns), lambda i: (i, 0)) for columns, _ in outs],
        out_shape=[jax.ShapeDtypeStruct((rows, columns), kind) for columns, kind in outs],
        compiler_params=pltpu.CompilerParams(vmem_limit_bytes=48 * 1024 * 1024),
        cost_estimate=pl.CostEstimate(flops=1000, bytes_accessed=1000, transcendentals=0),
    )(*row_args, *matrices)


def local(tokens, cotangent, routing, combine_weights, w_gate, w_up, w_down):
    tok_rows, features = tokens.shape
    top_count = routing.shape[1]
    experts = lax.axis_size("expert")
    cold_count = experts - HOT
    hot_cap = 2 * tok_rows * top_count // experts
    cold_cap = (tok_rows * top_count - HOT * hot_cap + cold_count - 1) // cold_count
    capacity = max(hot_cap, cold_cap)
    local_rows = experts * capacity
    gate_matrix, up_matrix, down_matrix = w_gate[0], w_up[0], w_down[0]
    width = gate_matrix.shape[1]

    flat_ids = routing.reshape(-1)
    expert_ids = jnp.arange(experts, dtype=jnp.int32)
    matches = (flat_ids[:, None] == expert_ids[None, :]).astype(jnp.int32)
    before = jnp.cumsum(matches, axis=0) - matches
    slot_ids = jnp.sum(before * matches, axis=1)
    position = (flat_ids * capacity + slot_ids).reshape(tok_rows, top_count)
    targets = jnp.arange(local_rows, dtype=jnp.int32)
    selected = position[None, :, :] == targets[:, None, None]
    picker = jnp.any(selected, axis=2).astype(BF16)
    slot_weight = jnp.sum(jnp.where(selected, combine_weights[None, :, :], 0.0), axis=(1, 2))

    send_rows = dot(picker, tokens, ((1,), (0,))).astype(BF16)
    rows_own = exchange(send_rows, experts)
    send_grads = (slot_weight[:, None] * dot(picker, cotangent, ((1,), (0,)))).astype(BF16)
    rows_own, send_grads = lax.optimization_barrier((rows_own, send_grads))
    grads_own = exchange(send_grads, experts)

    kept = [(width, BF16), (width, F32), (width, F32)]
    rows_other = swap(rows_own)
    hidden_own, act_own, slope_own = by_rows(hidden_kernel, [rows_own], [gate_matrix, up_matrix], kept)
    hidden_other, act_other, slope_other, out_other = by_rows(
        forward_kernel, [rows_other], [gate_matrix, up_matrix, down_matrix], kept + [(features, BF16)]
    )
    out_peer = swap(out_other)
    (out_send,) = by_rows(out_kernel, [hidden_own, out_peer], [down_matrix], [(features, BF16)])
    grads_own, out_send = lax.optimization_barrier((grads_own, out_send))
    out_back = exchange(out_send, experts)

    pair = [(width, BF16), (width, BF16)]
    grads_other = swap(grads_own)
    gate_own, up_own = by_rows(grad_kernel, [grads_own, act_own, slope_own], [down_matrix], pair)
    gate_other, up_other, input_other = by_rows(
        backward_kernel,
        [grads_other, act_other, slope_other],
        [gate_matrix, up_matrix, down_matrix],
        pair + [(features, BF16)],
    )
    input_peer = swap(input_other)
    (input_send,) = by_rows(
        input_kernel, [gate_own, up_own, input_peer], [gate_matrix, up_matrix], [(features, BF16)]
    )
    out_back, input_send = lax.optimization_barrier((out_back, input_send))
    input_back = exchange(input_send, experts)

    rows_all = jnp.concatenate([rows_own, rows_other])
    grads_all = jnp.concatenate([grads_own, grads_other])
    gate_wgrad = dot(rows_all, jnp.concatenate([gate_own, gate_other]), ((0,), (0,)))
    up_wgrad = dot(rows_all, jnp.concatenate([up_own, up_other]), ((0,), (0,)))
    down_wgrad = dot(jnp.concatenate([hidden_own, hidden_other]), grads_all, ((0,), (0,)))

    combined = jnp.zeros((tok_rows, features), F32)
    for column in range(top_count):
        column_pick = (position[:, column][:, None] == targets[None, :]).astype(BF16)
        column_rows = dot(column_pick, out_back, ((1,), (0,)))
        combined = combined + combine_weights[:, column][:, None] * column_rows
    gate_wgrad, up_wgrad, down_wgrad, combined, input_back = lax.optimization_barrier(
        (gate_wgrad.astype(BF16), up_wgrad.astype(BF16), down_wgrad.astype(BF16), combined.astype(BF16), input_back)
    )
    token_grad = dot(picker, input_back, ((0,), (0,))).astype(BF16)
    return combined, token_grad, gate_wgrad[None], up_wgrad[None], down_wgrad[None]


def solution(mesh):
    in_specs = (
        P(("dp", "expert"), None),
        P(("dp", "expert"), None),
        P(("dp", "expert"), None),
        P(("dp", "expert"), None),
        P("expert", None, "dp"),
        P("expert", None, "dp"),
        P("expert", "dp", None),
    )
    out_specs = (
        P(("dp", "expert"), None),
        P(("dp", "expert"), None),
        P("expert", None, "dp"),
        P("expert", None, "dp"),
        P("expert", "dp", None),
    )
    return jax.shard_map(local, mesh=mesh, in_specs=in_specs, out_specs=out_specs, check_vma=False)
```

time: 367 us -> 317 us (0.86)
  blocking collectives: 122 us -> 0 us
  waiting for transfers between devices: 98.2 us -> 164 us
  matrix products: 95.1 us -> 38.5 us
  Pallas kernels: 0 us -> 49.7 us
  local copies, waits for them, and re-layouts: 2.28 us -> 23.5 us
  starting transfers between devices: 20.7 us -> 38.2 us
  between operations: 13.9 us -> 0.9 us
  other arithmetic: 13.6 us -> 1.68 us
    all_to_all x2 -> x0, blocking collectives: 122 us -> none  [the longest x1 64 us: local(): lax.all_to_all(send_rows.reshape(experts, capacity, features), 'expert',...]
    all_to_all x2 -> x4, waiting for transfers between devices: 57.2 us -> 149 us  [exchange(): lax.all_to_all(parts, 'expert', split_axis=0, concat_axis=0, tiled=True)]
    dot_general x14 -> x8, matrix products: 95.1 us -> 38.5 us  [dot(): lax.dot_general(left, right, (dims, ((), ())), preferred_element_type=F32)]
    pallas_call x0 -> x6, Pallas kernels: none -> 49.7 us  [by_rows(): pl.pallas_call(kernel, grid=(rows // BLOCK,), in_specs=in_specs, out_spec...]
    reduce_scatter x2 -> x0, waiting for transfers between devices: 37.3 us -> none  [the longest x1 21.2 us: local(): lax.psum_scatter(input_part, 'dp', scatter_dimension=0, tiled=True)]
    all_to_all x2 -> x4, starting transfers between devices: 20.4 us -> 38 us  [exchange(): lax.all_to_all(parts, 'expert', split_axis=0, concat_axis=0, tiled=True)]
    unnamed x29 -> x50, local copies, waits for them, and re-layouts: 1.6 us -> 18 us
    ppermute x0 -> x4, waiting for transfers between devices: none -> 14.9 us  [swap(): return lax.ppermute(value, 'dp', [(0, 1), (1, 0)])]
  transfers between devices with their start and end apart: 6 -> 8, of which waited for: 5 -> 6; matrix products, arithmetic and copies ran while one was open for 18% -> 13% of each run, Pallas kernels for 0% -> 8%
where the time goes in v1:
time: 317 us; the launch traced here: 316 us
  waiting for transfers between devices  164 us (52%)
  Pallas kernels  49.7 us (16%)
  matrix products  38.5 us (12%)
  starting transfers between devices  38.2 us (12%)
  local copies, waits for them, and re-layouts  23.5 us (7%)
    all_to_all x4, waiting for transfers between devices, exchange(): lax.all_to_all(parts, 'expert', split_axis=0, concat_axis=0, tiled=True)  149 us
    pallas_call x6, Pallas kernels, by_rows(): pl.pallas_call(kernel, grid=(rows // BLOCK,), in_specs=in_specs, out_spec...  49.7 us
    dot_general x8, matrix products, dot(): lax.dot_general(left, right, (dims, ((), ())), preferred_element_type=F32)  38.5 us
    all_to_all x4, starting transfers between devices, exchange(): lax.all_to_all(parts, 'expert', split_axis=0, concat_axis=0, tiled=True)  38 us
    unnamed x50, local copies, waits for them, and re-layouts  18 us
    ppermute x4, waiting for transfers between devices, swap(): return lax.ppermute(value, 'dp', [(0, 1), (1, 0)])  14.9 us
  transfers between devices with their start and end apart: 8, of which 6 were waited for; matrix products, arithmetic and copies ran while one was open for 13% of the time, Pallas kernels for 8%

profile of v1, /device:TPU:0, one launch (start us, length us, event | category | flops | bytes accessed | tf_op | source)
XLA Modules:
  0.0 316.3 jit_solution(6410738234775106857)
XLA Ops:
  0.6 0.0 copy-start
  0.6 0.9 copy.32
  1.5 0.1 eq.72
  1.7 0.1 eq.68
  1.8 0.6 reduce-window.6
  2.4 0.2 slice_reduce_fusion
  2.7 0.1 fusion.24
  2.8 0.1 reduce_sum.21
  2.9 0.1 copy.35
  3.0 0.7 multiply_add_fusion
  3.7 0.1 fusion.19
  3.8 3.2 %fusion.7 = bf16[64,8,4096]{2,1,0:T(8,128)(2,1)} fusion(pred[512,128]{1,0:T(8,128)(4,1)S(1)} %fusion.19, bf16[128,4096]{1,0:T(8,128)(2,1)S(1)} %copy-done), kind=kOutput, calls=%fused_computation.9 | convolution fusion | flops 538968064 | bytes 5308416 | tf_op jit(solution)/shard_map/dot_general | solution.py:15
  7.0 11.9 %all-to-all-start = ((bf16[64,8,4096]{2,1,0:T(8,128)(2,1)}), bf16[64,8,4096]{2,1,0:T(8,128)(2,1)}, u32[]{:S(2)}, u32[]{:S(2)}) async-start(bf16[64,8,4096]{2,1,0:T(8,128)(2,1)} %fusion.7), calls=%async_computation | async-start | bytes 8388608 | tf_op jit(solution)/shard_map/all_to_all | solution.py:25
  18.9 0.0 copy-done.23
  18.9 0.0 copy-start.4
  18.9 0.1 select_reduce_fusion
  19.1 4.6 %multiply_convert_fusion = bf16[512,4096]{1,0:T(8,128)(2,1)} fusion(pred[512,128]{1,0:T(8,128)(4,1)S(1)} %fusion.19, bf16[128,4096]{1,0:T(8,128)(2,1)} %param.8, f32[512]{0:T(512)S(1)} %select_reduce_fusion), kind=kOutput, calls=%fused_computation.4 | convolution fusion | flops 541065216 | bytes 5310464 | tf_op jit(solution)/shard_map/dot_general | solution.py:15
  23.7 50.0 %all-to-all-done = bf16[64,8,4096]{2,1,0:T(8,128)(2,1)} async-done(((bf16[64,8,4096]{2,1,0:T(8,128)(2,1)}), bf16[64,8,4096]{2,1,0:T(8,128)(2,1)}, u32[]{:S(2)}, u32[]{:S(2)}) %all-to-all-start) | async-done | bytes 4194336 | tf_op jit(solution)/shard_map/all_to_all | solution.py:25
  73.6 0.0 collective-permute-start
  73.6 7.5 %collective-permute-done.rows_ref = bf16[512,4096]{1,0:T(8,128)(2,1)} collective-permute-done((bf16[512,4096]{1,0:T(8,128)(2,1)}, bf16[512,4096]{1,0:T(8,128)(2,1)}, u32[]{:S(2)}, u32[]{:S(2)}) %collective-permute-start) | collective-permute-done | bytes 4194336 | tf_op jit(solution)/shard_map/ppermute | solution.py:19
  81.1 11.9 %shard_map.111 = (bf16[512,384]{1,0:T(8,128)(2,1)S(1)}, f32[512,384]{1,0:T(8,128)S(1)}, f32[512,384]{1,0:T(8,128)S(1)}, bf16[512,4096]{1,0:T(8,128)(2,1)}) custom-call(bf16[512,4096]{1,0:T(8,128)(2,1)} %collective-permute-done.rows_ref, bf16[4096,384]{1,0:T(8,128)(2,1)S(1)} %bitcast.56, bf16[4096,384]{1,0:T(8,128)(2,1)} %bitcast.60, bf16[384,4096]{1,0:T(8,128)(2,1)} %bitcast.52), custom_call_target="tpu_custom_call" | custom-call | flops 1000 | bytes 1000 | tf_op jit(solution)/shard_map/pallas_call | solution.py:85
  93.0 0.9 copy-done.12
  93.9 0.9 copy-done.14
  94.8 0.7 copy-done.16
  95.5 0.1 collective-permute-start.1
  95.7 7.9 %all-to-all-start.1 = ((bf16[64,8,4096]{2,1,0:T(8,128)(2,1)}), bf16[64,8,4096]{2,1,0:T(8,128)(2,1)}, u32[]{:S(2)}, u32[]{:S(2)}) async-start(bf16[64,8,4096]{2,1,0:T(8,128)(2,1)} %bitcast.64), calls=%async_computation.1 | async-start | bytes 8388608 | tf_op jit(solution)/shard_map/all_to_all | solution.py:25
  103.6 0.0 copy-start.5
  103.6 1.9 copy-done.5
  105.5 7.5 %shard_map.110 = (bf16[512,384]{1,0:T(8,128)(2,1)S(1)}, f32[512,384]{1,0:T(8,128)S(1)}, f32[512,384]{1,0:T(8,128)S(1)}) custom-call(bf16[512,4096]{1,0:T(8,128)(2,1)} %bitcast.2.rows_ref, bf16[4096,384]{1,0:T(8,128)(2,1)S(1)} %bitcast.57, bf16[4096,384]{1,0:T(8,128)(2,1)} %bitcast.61), custom_call_target="tpu_custom_call" | custom-call | flops 1000 | bytes 1000 | tf_op jit(solution)/shard_map/pallas_call | solution.py:85
  112.9 0.0 copy-start.8
  112.9 0.9 copy-done.8
  113.8 0.9 copy-done.10
  114.7 0.0 collective-permute-done.1.peer_ref
  114.7 5.4 %shard_map.112 = bf16[512,4096]{1,0:T(8,128)(2,1)} custom-call(bf16[512,384]{1,0:T(8,128)(2,1)S(1)} %get-tuple-element.30.hidden_ref, bf16[512,4096]{1,0:T(8,128)(2,1)} %collective-permute-done.1.peer_ref, bf16[384,4096]{1,0:T(8,128)(2,1)S(1)} %bitcast.54), custom_call_target="tpu_custom_call" | custom-call | flops 1000 | bytes 1000 | tf_op jit(solution)/shard_map/pallas_call | solution.py:85
  120.1 38.3 %all-to-all-done.1 = bf16[64,8,4096]{2,1,0:T(8,128)(2,1)} async-done(((bf16[64,8,4096]{2,1,0:T(8,128)(2,1)}), bf16[64,8,4096]{2,1,0:T(8,128)(2,1)}, u32[]{:S(2)}, u32[]{:S(2)}) %all-to-all-start.1) | async-done | bytes 4194336 | tf_op jit(solution)/shard_map/all_to_all | solution.py:25
  158.5 0.0 collective-permute-start.2
  158.5 7.4 %collective-permute-done.2.grads_ref = bf16[512,4096]{1,0:T(8,128)(2,1)S(1)} collective-permute-done((bf16[512,4096]{1,0:T(8,128)(2,1)}, bf16[512,4096]{1,0:T(8,128)(2,1)S(1)}, u32[]{:S(2)}, u32[]{:S(2)}) %collective-permute-start.2) | collective-permute-done | bytes 4194336 | tf_op jit(solution)/shard_map/ppermute | solution.py:19
  165.8 2.0 copy-done.18
  167.8 1.9 copy-done.6
  169.7 1.1 copy-done.13
  170.8 1.1 copy-done.15
  172.0 12.0 %shard_map.114 = (bf16[512,384]{1,0:T(8,128)(2,1)S(1)}, bf16[512,384]{1,0:T(8,128)(2,1)S(1)}, bf16[512,4096]{1,0:T(8,128)(2,1)}) custom-call(bf16[512,4096]{1,0:T(8,128)(2,1)} %copy-done.18, f32[512,384]{1,0:T(8,128)S(1)} %copy-done.13, f32[512,384]{1,0:T(8,128)S(1)} %copy-done.15, bf16[4096,384]{1,0:T(8,128)(2,1)S(1)} %bitcast.58, ...), custom_call_target="tpu_custom_call" | custom-call | flops 1000 | bytes 1000 | tf_op jit(solution)/shard_map/pallas_call | solution.py:85
  183.9 0.1 collective-permute-start.3
  184.1 9.0 %all-to-all-start.2 = ((bf16[64,8,4096]{2,1,0:T(8,128)(2,1)}), bf16[64,8,4096]{2,1,0:T(8,128)(2,1)}, u32[]{:S(2)}, u32[]{:S(2)}) async-start(bf16[64,8,4096]{2,1,0:T(8,128)(2,1)} %bitcast.65), calls=%async_computation.2 | async-start | bytes 8388608 | tf_op jit(solution)/shard_map/all_to_all | solution.py:25
  193.1 0.0 copy-start.3
  193.1 0.0 copy-start.9
  193.1 0.0 copy-start.11
  193.1 4.8 %constant_dynamic-update-slice_fusion.1 = bf16[1024,4096]{1,0:T(8,128)(2,1)} fusion(bf16[512,4096]{1,0:T(8,128)(2,1)} %bitcast.2.rows_ref), kind=kLoop, calls=%fused_computation.41 | loop fusion | bytes 8388608
  197.9 0.0 copy-start.7
  197.9 4.3 %shard_map.113 = (bf16[512,384]{1,0:T(8,128)(2,1)S(1)}, bf16[512,384]{1,0:T(8,128)(2,1)S(1)}) custom-call(bf16[512,4096]{1,0:T(8,128)(2,1)} %bitcast.4.grads_ref, f32[512,384]{1,0:T(8,128)S(1)} %copy-done.9, f32[512,384]{1,0:T(8,128)S(1)} %copy-done.11, bf16[384,4096]{1,0:T(8,128)(2,1)S(1)} %bitcast.55), custom_call_target="tpu_custom_call" | custom-call | flops 1000 | bytes 1000 | tf_op jit(solution)/shard_map/pallas_call | solution.py:85
  202.3 0.0 collective-permute-done.3.peer_ref
  202.3 8.6 %shard_map.115 = bf16[512,4096]{1,0:T(8,128)(2,1)} custom-call(bf16[512,384]{1,0:T(8,128)(2,1)S(1)} %get-tuple-element.35.gate_grad_ref, bf16[512,384]{1,0:T(8,128)(2,1)S(1)} %get-tuple-element.39.up_grad_ref, bf16[512,4096]{1,0:T(8,128)(2,1)} %collective-permute-done.3.peer_ref, bf16[4096,384]{1,0:T(8,128)(2,1)S(1)} %bitcast.59, bf16[4096,384]{1,0:T(8,128)(2,1)} %bitcast.63), custom_call_target="tpu_custom_call" | custom-call | flops 1000 | bytes 1000 | tf_op jit(solution)/shard_map/pallas_call | solution.py:85
  210.9 37.2 %all-to-all-done.2 = bf16[64,8,4096]{2,1,0:T(8,128)(2,1)} async-done(((bf16[64,8,4096]{2,1,0:T(8,128)(2,1)}), bf16[64,8,4096]{2,1,0:T(8,128)(2,1)}, u32[]{:S(2)}, u32[]{:S(2)}) %all-to-all-start.2) | async-done | bytes 4194336 | tf_op jit(solution)/shard_map/all_to_all | solution.py:25
  248.1 9.2 %all-to-all-start.3 = ((bf16[64,8,4096]{2,1,0:T(8,128)(2,1)}), bf16[64,8,4096]{2,1,0:T(8,128)(2,1)}, u32[]{:S(2)}, u32[]{:S(2)}) async-start(bf16[64,8,4096]{2,1,0:T(8,128)(2,1)} %bitcast.66), calls=%async_computation.3 | async-start | bytes 8388608 | tf_op jit(solution)/shard_map/all_to_all | solution.py:25
  257.3 0.0 copy-start.17
  257.4 4.8 %constant_dynamic-update-slice_fusion = bf16[1024,4096]{1,0:T(8,128)(2,1)} fusion(bf16[1024,4096]{1,0:T(8,128)(2,1)} %constant_dynamic-update-slice_fusion.1, bf16[512,4096]{1,0:T(8,128)(2,1)} %collective-permute-done.rows_ref), kind=kLoop, calls=%fused_computation.40 | loop fusion | bytes 8388608 | tf_op jit(solution)/shard_map/concatenate | solution.py:152
  262.2 7.6 %fusion.4 = bf16[384,4096]{1,0:T(8,128)(2,1)} fusion(bf16[512,4096]{1,0:T(8,128)(2,1)S(1)} %copy-done.19, bf16[512,4096]{1,0:T(8,128)(2,1)} %bitcast.4.grads_ref, bf16[512,384]{1,0:T(8,128)(2,1)S(1)} %copy-done.17, bf16[512,384]{1,0:T(8,128)(2,1)S(1)} %get-tuple-element.30.hidden_ref), kind=kOutput, calls=%fused_computation.6 | convolution fusion | flops 3241148416 | bytes 12320768 | tf_op jit(solution)/shard_map/dot_general | solution.py:15
  269.8 6.0 %convolution_convert_fusion.1 = bf16[4096,384]{1,0:T(8,128)(2,1)} fusion(bf16[1024,4096]{1,0:T(8,128)(2,1)S(1)} %copy-done.20, bf16[512,384]{1,0:T(8,128)(2,1)S(1)} %get-tuple-element.40, bf16[512,384]{1,0:T(8,128)(2,1)S(1)} %get-tuple-element.39.up_grad_ref), kind=kOutput, calls=%fused_computation.7 | convolution fusion | flops 3224371200 | bytes 12320768 | tf_op jit(solution)/shard_map/dot_general | solution.py:15
  275.9 6.0 %convolution_convert_fusion.2 = bf16[4096,384]{1,0:T(8,128)(2,1)} fusion(bf16[1024,4096]{1,0:T(8,128)(2,1)S(1)} %copy-done.20, bf16[512,384]{1,0:T(8,128)(2,1)S(1)} %get-tuple-element.38, bf16[512,384]{1,0:T(8,128)(2,1)S(1)} %get-tuple-element.35.gate_grad_ref), kind=kOutput, calls=%fused_computation.8 | convolution fusion | flops 3224371200 | bytes 12320768 | tf_op jit(solution)/shard_map/dot_general | solution.py:15
  281.9 2.9 convolution_multiply_fusion.1
  284.8 0.0 copy-start.1
  284.9 4.1 %fusion.9 = bf16[128,4096]{1,0:T(8,128)(2,1)} fusion(f32[128,4096]{1,0:T(8,128)S(1)} %convolution_multiply_fusion.1, bf16[512,4096]{1,0:T(8,128)(2,1)} %bitcast.11, f32[128]{0:T(128)S(1)} %get-tuple-element.53, s32[128]{0:T(128)S(1)} %get-tuple-element.51), kind=kOutput, calls=%fused_computation.13 | convolution fusion | flops 538509312 | bytes 7341056 | tf_op jit(solution)/shard_map/dot_general | solution.py:15
  289.0 23.3 %all-to-all-done.3 = bf16[64,8,4096]{2,1,0:T(8,128)(2,1)} async-done(((bf16[64,8,4096]{2,1,0:T(8,128)(2,1)}), bf16[64,8,4096]{2,1,0:T(8,128)(2,1)}, u32[]{:S(2)}, u32[]{:S(2)}) %all-to-all-start.3) | async-done | bytes 4194336 | tf_op jit(solution)/shard_map/all_to_all | solution.py:25
  312.3 3.9 %convolution_convert_fusion.3 = bf16[128,4096]{1,0:T(8,128)(2,1)} fusion(pred[512,128]{1,0:T(8,128)(4,1)S(1)} %copy-done.22, bf16[512,4096]{1,0:T(8,128)(2,1)} %bitcast.15), kind=kOutput, calls=%fused_computation.14 | convolution fusion | flops 537395200 | bytes 5308416 | tf_op jit(solution)/shard_map/dot_general | solution.py:15
  (32 shorter events, 0.1 us)
Async XLA Ops:
  0.6 3.1 copy-start
  3.8 15.3 %copy-start.21 = (pred[512,128]{1,0:T(8,128)(4,1)}, pred[512,128]{1,0:T(8,128)(4,1)S(1)}, u32[]{:S(2)}) copy-start(pred[512,128]{1,0:T(8,128)(4,1)S(1)} %fusion.19) | copy-start | bytes 196612
  7.0 11.9 %copy-start.23 = (f32[128,2]{0,1:T(2,128)S(1)}, f32[128,2]{0,1:T(2,128)}, u32[]{:S(2)}) copy-start(f32[128,2]{0,1:T(2,128)} %param.10) | copy-start | bytes 3076
  7.0 66.6 %all-to-all-start = ((bf16[64,8,4096]{2,1,0:T(8,128)(2,1)}), bf16[64,8,4096]{2,1,0:T(8,128)(2,1)}, u32[]{:S(2)}, u32[]{:S(2)}) async-start(bf16[64,8,4096]{2,1,0:T(8,128)(2,1)} %fusion.7), calls=%async_computation | async-start | bytes 8388608 | tf_op jit(solution)/shard_map/all_to_all | solution.py:25
  18.9 62.2 %copy-start.4 = (bf16[1,4096,384]{2,1,0:T(8,128)(2,1)S(1)}, bf16[1,4096,384]{2,1,0:T(8,128)(2,1)}, u32[]{:S(2)}) copy-start(bf16[1,4096,384]{2,1,0:T(8,128)(2,1)} %param.11) | copy-start | bytes 9437188
  73.6 7.5 %collective-permute-start = (bf16[512,4096]{1,0:T(8,128)(2,1)}, bf16[512,4096]{1,0:T(8,128)(2,1)}, u32[]{:S(2)}, u32[]{:S(2)}) collective-permute-start(bf16[512,4096]{1,0:T(8,128)(2,1)} %bitcast.2.rows_ref), channel_id=1, source_target_pairs={{0,64},{64,0},{1,65},{65,1},{2,66},{66,2},{3,67},{67,3},{4,68},{68... | collective-permute-start | bytes 12582920 | tf_op jit(solution)/shard_map/ppermute | solution.py:19
  93.0 0.9 copy-start.12
  93.9 0.9 copy-start.14
  94.8 0.7 copy-start.16
  95.5 19.2 %collective-permute-start.1 = (bf16[512,4096]{1,0:T(8,128)(2,1)}, bf16[512,4096]{1,0:T(8,128)(2,1)}, u32[]{:S(2)}, u32[]{:S(2)}) collective-permute-start(bf16[512,4096]{1,0:T(8,128)(2,1)} %get-tuple-element.31), channel_id=1, source_target_pairs={{0,64},{64,0},{1,65},{65,1},{2,66},{66,2},{3,67},{67,3},{4,68},{68... | collective-permute-start | bytes 12582920 | tf_op jit(solution)/shard_map/ppermute | solution.py:19
  95.7 62.8 %all-to-all-start.1 = ((bf16[64,8,4096]{2,1,0:T(8,128)(2,1)}), bf16[64,8,4096]{2,1,0:T(8,128)(2,1)}, u32[]{:S(2)}, u32[]{:S(2)}) async-start(bf16[64,8,4096]{2,1,0:T(8,128)(2,1)} %bitcast.64), calls=%async_computation.1 | async-start | bytes 8388608 | tf_op jit(solution)/shard_map/all_to_all | solution.py:25
  103.6 1.9 copy-start.5
  105.5 9.2 %copy-start.2 = (bf16[1,384,4096]{2,1,0:T(8,128)(2,1)S(1)}, bf16[1,384,4096]{2,1,0:T(8,128)(2,1)}, u32[]{:S(2)}) copy-start(bf16[1,384,4096]{2,1,0:T(8,128)(2,1)} %param.13) | copy-start | bytes 9437188
  112.9 0.9 copy-start.8
  113.8 0.9 copy-start.10
  158.5 7.4 %collective-permute-start.2 = (bf16[512,4096]{1,0:T(8,128)(2,1)}, bf16[512,4096]{1,0:T(8,128)(2,1)S(1)}, u32[]{:S(2)}, u32[]{:S(2)}) collective-permute-start(bf16[512,4096]{1,0:T(8,128)(2,1)} %bitcast.4.grads_ref), channel_id=1, source_target_pairs={{0,64},{64,0},{1,65},{65,1},{2,66},{66,2},{3,67},{67,3},{4,68},{68... | collective-permute-start | bytes 12582920 | tf_op jit(solution)/shard_map/ppermute | solution.py:19
  165.8 2.0 copy-start.18
  167.8 1.9 copy-start.6
  169.7 1.1 copy-start.13
  170.8 1.1 copy-start.15
  183.9 18.3 %collective-permute-start.3 = (bf16[512,4096]{1,0:T(8,128)(2,1)}, bf16[512,4096]{1,0:T(8,128)(2,1)}, u32[]{:S(2)}, u32[]{:S(2)}) collective-permute-start(bf16[512,4096]{1,0:T(8,128)(2,1)} %get-tuple-element.43), channel_id=1, source_target_pairs={{0,64},{64,0},{1,65},{65,1},{2,66},{66,2},{3,67},{67,3},{4,68},{68... | collective-permute-start | bytes 12582920 | tf_op jit(solution)/shard_map/ppermute | solution.py:19
  184.1 64.1 %all-to-all-start.2 = ((bf16[64,8,4096]{2,1,0:T(8,128)(2,1)}), bf16[64,8,4096]{2,1,0:T(8,128)(2,1)}, u32[]{:S(2)}, u32[]{:S(2)}) async-start(bf16[64,8,4096]{2,1,0:T(8,128)(2,1)} %bitcast.65), calls=%async_computation.2 | async-start | bytes 8388608 | tf_op jit(solution)/shard_map/all_to_all | solution.py:25
  193.1 4.8 %copy-start.3 = (bf16[1,384,4096]{2,1,0:T(8,128)(2,1)S(1)}, bf16[1,384,4096]{2,1,0:T(8,128)(2,1)}, u32[]{:S(2)}) copy-start(bf16[1,384,4096]{2,1,0:T(8,128)(2,1)} %param.13) | copy-start | bytes 9437188
  193.1 4.8 %copy-start.9 = (f32[512,384]{1,0:T(8,128)S(1)}, f32[512,384]{1,0:T(8,128)}, u32[]{:S(2)}) copy-start(f32[512,384]{1,0:T(8,128)} %copy-done.8) | copy-start | bytes 2359300
  193.1 4.8 %copy-start.11 = (f32[512,384]{1,0:T(8,128)S(1)}, f32[512,384]{1,0:T(8,128)}, u32[]{:S(2)}) copy-start(f32[512,384]{1,0:T(8,128)} %copy-done.10) | copy-start | bytes 2359300
  197.9 4.3 %copy-start.7 = (bf16[1,4096,384]{2,1,0:T(8,128)(2,1)S(1)}, bf16[1,4096,384]{2,1,0:T(8,128)(2,1)}, u32[]{:S(2)}) copy-start(bf16[1,4096,384]{2,1,0:T(8,128)(2,1)} %param.11) | copy-start | bytes 9437188
  248.1 64.2 %all-to-all-start.3 = ((bf16[64,8,4096]{2,1,0:T(8,128)(2,1)}), bf16[64,8,4096]{2,1,0:T(8,128)(2,1)}, u32[]{:S(2)}, u32[]{:S(2)}) async-start(bf16[64,8,4096]{2,1,0:T(8,128)(2,1)} %bitcast.66), calls=%async_computation.3 | async-start | bytes 8388608 | tf_op jit(solution)/shard_map/all_to_all | solution.py:25
  257.3 4.9 %copy-start.17 = (bf16[512,384]{1,0:T(8,128)(2,1)S(1)}, bf16[512,384]{1,0:T(8,128)(2,1)}, u32[]{:S(2)}) copy-start(bf16[512,384]{1,0:T(8,128)(2,1)} %copy-done.16) | copy-start | bytes 1179652
  257.3 4.8 %copy-start.19 = (bf16[512,4096]{1,0:T(8,128)(2,1)S(1)}, bf16[512,4096]{1,0:T(8,128)(2,1)}, u32[]{:S(2)}) copy-start(bf16[512,4096]{1,0:T(8,128)(2,1)} %copy-done.18) | copy-start | bytes 12582916
  262.2 7.6 %copy-start.20 = (bf16[1024,4096]{1,0:T(8,128)(2,1)S(1)}, bf16[1024,4096]{1,0:T(8,128)(2,1)}, u32[]{:S(2)}) copy-start(bf16[1024,4096]{1,0:T(8,128)(2,1)} %constant_dynamic-update-slice_fusion) | copy-start | bytes 25165828
  284.8 27.5 %copy-start.22 = (pred[512,128]{1,0:T(8,128)(4,1)S(1)}, pred[512,128]{1,0:T(8,128)(4,1)}, u32[]{:S(2)}) copy-start(pred[512,128]{1,0:T(8,128)(4,1)} %copy-done.21) | copy-start | bytes 196612
  284.8 31.4 %copy-start.1 = (bf16[128,4096]{1,0:T(8,128)(2,1)S(1)}, bf16[128,4096]{1,0:T(8,128)(2,1)}, u32[]{:S(2)}) copy-start(bf16[128,4096]{1,0:T(8,128)(2,1)} %param.7) | copy-start | bytes 3145732

commit v2 on v1

--- a/solution.py
+++ b/solution.py
@@ -16,7 +16,9 @@
 
 
 def swap(value):
-    return lax.ppermute(value, "dp", [(0, 1), (1, 0)])
+    size = value.shape[0] // 4
+    parts = [value[size * i : size * (i + 1)] for i in range(4)]
+    return jnp.concatenate([lax.ppermute(part, "dp", [(0, 1), (1, 0)]) for part in parts])
 
 
 def exchange(value, experts):

time: 317 us -> 292 us (0.921); the launches traced: 316 us -> 286 us
  waiting for transfers between devices: 164 us -> 83.9 us
  local copies, waits for them, and re-layouts: 23.5 us -> 41.7 us
  starting transfers between devices: 38.2 us -> 52 us
  other arithmetic: 1.68 us -> 15.4 us
  matrix products: 38.5 us -> 42.3 us
    all_to_all x4, waiting for transfers between devices: 149 us -> 83.9 us  [exchange(): lax.all_to_all(parts, 'expert', split_axis=0, concat_axis=0, tiled=True)]
    ppermute x4 -> x16, waiting for transfers between devices: 14.9 us -> 0.04 us  [swap(): lax.ppermute(part, 'dp', [(0, 1), (1, 0)])]
    slice x1 -> x5, local copies, waits for them, and re-layouts: 0.18 us -> 14.9 us  [the longest x4 14.7 us: swap(): parts = [value[size * i:size * (i + 1)] for i in range(4)]]
    ppermute x4 -> x16, starting transfers between devices: 0.27 us -> 14.1 us  [swap(): lax.ppermute(part, 'dp', [(0, 1), (1, 0)])]
    concatenate x0 -> x4, other arithmetic: none -> 13.7 us  [swap(): jnp.concatenate([lax.ppermute(part, 'dp', [(0, 1), (1, 0)]) for part in p...]
    unnamed x50 -> x67, local copies, waits for them, and re-layouts: 18 us -> 22.9 us
    dot_general x8, matrix products: 38.5 us -> 42.3 us  [dot(): lax.dot_general(left, right, (dims, ((), ())), preferred_element_type=F32)]
    concatenate x1, local copies, waits for them, and re-layouts: 4.83 us -> 1.08 us  [local(): rows_all = jnp.concatenate([rows_own, rows_other])]
  transfers between devices with their start and end apart: 8 -> 20, of which waited for: 6 -> 3; matrix products, arithmetic and copies ran while one was open for 13% -> 28% of each run, Pallas kernels for 8% -> 17%
where the time goes in v2:
time: 292 us; the launch traced here: 286 us
  waiting for transfers between devices  83.9 us (29%)
  starting transfers between devices  52 us (18%)
  Pallas kernels  49.5 us (17%)
  matrix products  42.3 us (14%)
  local copies, waits for them, and re-layouts  41.7 us (14%)
  other arithmetic  15.4 us (5%)
    all_to_all x4, waiting for transfers between devices, exchange(): lax.all_to_all(parts, 'expert', split_axis=0, concat_axis=0, tiled=True)  83.9 us
    pallas_call x6, Pallas kernels, by_rows(): pl.pallas_call(kernel, grid=(rows // BLOCK,), in_specs=in_specs, out_spec...  49.5 us
    dot_general x8, matrix products, dot(): lax.dot_general(left, right, (dims, ((), ())), preferred_element_type=F32)  42.3 us
    all_to_all x4, starting transfers between devices, exchange(): lax.all_to_all(parts, 'expert', split_axis=0, concat_axis=0, tiled=True)  37.9 us
    unnamed x67, local copies, waits for them, and re-layouts  22.9 us
    slice x4, local copies, waits for them, and re-layouts, swap(): parts = [value[size * i:size * (i + 1)] for i in range(4)]  14.7 us
    ppermute x16, starting transfers between devices, swap(): lax.ppermute(part, 'dp', [(0, 1), (1, 0)])  14.1 us
    concatenate x4, other arithmetic, swap(): jnp.concatenate([lax.ppermute(part, 'dp', [(0, 1), (1, 0)]) for part in p...  13.7 us
  transfers between devices with their start and end apart: 20, of which 3 were waited for; matrix products, arithmetic and copies ran while one was open for 28% of the time, Pallas kernels for 17%

profile of v2, /device:TPU:0, one launch (start us, length us, event | category | flops | bytes accessed | tf_op | source)
XLA Modules:
  0.0 286.3 jit_solution(10468541901835171813)
XLA Ops:
  0.6 0.9 copy.32
  1.5 0.1 eq.72
  1.7 0.1 eq.68
  1.8 0.6 reduce-window.6
  2.4 0.2 slice_reduce_fusion
  2.7 0.1 fusion.17
  2.8 0.1 reduce_sum.21
  2.9 0.1 copy.35
  3.0 0.7 multiply_add_fusion
  3.7 0.1 fusion.12
  3.8 3.3 %fusion = bf16[64,8,4096]{2,1,0:T(8,128)(2,1)} fusion(pred[512,128]{1,0:T(8,128)(4,1)S(1)} %fusion.12, bf16[128,4096]{1,0:T(8,128)(2,1)S(1)} %copy-done), kind=kOutput, calls=%fused_computation.5 | convolution fusion | flops 538968064 | bytes 5308416 | tf_op jit(solution)/shard_map/dot_general | solution.py:15
  7.0 11.9 %all-to-all-start = ((bf16[64,8,4096]{2,1,0:T(8,128)(2,1)}), bf16[64,8,4096]{2,1,0:T(8,128)(2,1)}, u32[]{:S(2)}, u32[]{:S(2)}) async-start(bf16[64,8,4096]{2,1,0:T(8,128)(2,1)} %fusion), calls=%async_computation | async-start | bytes 8388608 | tf_op jit(solution)/shard_map/all_to_all | solution.py:27
  19.0 0.1 select_reduce_fusion
  19.1 3.2 %multiply_convert_fusion = bf16[512,4096]{1,0:T(8,128)(2,1)} fusion(pred[512,128]{1,0:T(8,128)(4,1)S(1)} %fusion.12, bf16[128,4096]{1,0:T(8,128)(2,1)S(1)} %copy-done.25, f32[512]{0:T(512)S(1)} %select_reduce_fusion), kind=kOutput, calls=%fused_computation | convolution fusion | flops 541065216 | bytes 5310464 | tf_op jit(solution)/shard_map/dot_general | solution.py:15
  22.3 51.3 %all-to-all-done = bf16[64,8,4096]{2,1,0:T(8,128)(2,1)} async-done(((bf16[64,8,4096]{2,1,0:T(8,128)(2,1)}), bf16[64,8,4096]{2,1,0:T(8,128)(2,1)}, u32[]{:S(2)}, u32[]{:S(2)}) %all-to-all-start) | async-done | bytes 4194336 | tf_op jit(solution)/shard_map/all_to_all | solution.py:27
  73.7 4.3 %fusion.25 = (bf16[128,4096]{1,0:T(8,128)(2,1)}, bf16[128,4096]{1,0:T(8,128)(2,1)}, bf16[128,4096]{1,0:T(8,128)(2,1)}, bf16[128,4096]{1,0:T(8,128)(2,1)}) fusion(bf16[512,4096]{1,0:T(8,128)(2,1)} %bitcast.2.rows_ref), kind=kLoop, calls=%fused_computation.61 | loop fusion | bytes 8388608 | tf_op jit(solution)/shard_map/slice | solution.py:20
  77.9 0.5 collective-permute-start.1
  78.5 0.5 collective-permute-start.3
  79.0 7.7 %all-to-all-start.1 = ((bf16[64,8,4096]{2,1,0:T(8,128)(2,1)}), bf16[64,8,4096]{2,1,0:T(8,128)(2,1)}, u32[]{:S(2)}, u32[]{:S(2)}) async-start(bf16[64,8,4096]{2,1,0:T(8,128)(2,1)} %bitcast.65), calls=%async_computation.1 | async-start | bytes 8388608 | tf_op jit(solution)/shard_map/all_to_all | solution.py:27
  86.7 3.8 %pad_maximum_fusion.rows_ref = bf16[512,4096]{1,0:T(8,128)(2,1)} fusion(bf16[128,4096]{1,0:T(8,128)(2,1)S(1)} %collective-permute-done.3, bf16[128,4096]{1,0:T(8,128)(2,1)S(1)} %collective-permute-done.2, bf16[128,4096]{1,0:T(8,128)(2,1)} %collective-permute-done.1, bf16[128,4096]{1,0:T(8,128)(2,1)S(1)} %collective-permute-done), kind=kLoop, calls=%fused_computation.11 | loop fusion | flops 16777216 | bytes 8388608 | tf_op jit(solution)/shard_map/concatenate | solution.py:21
  90.5 12.0 %shard_map.111 = (bf16[512,384]{1,0:T(8,128)(2,1)S(1)}, f32[512,384]{1,0:T(8,128)S(1)}, f32[512,384]{1,0:T(8,128)S(1)}, bf16[512,4096]{1,0:T(8,128)(2,1)}) custom-call(bf16[512,4096]{1,0:T(8,128)(2,1)} %pad_maximum_fusion.rows_ref, bf16[4096,384]{1,0:T(8,128)(2,1)S(1)} %bitcast.57, bf16[4096,384]{1,0:T(8,128)(2,1)} %bitcast.61, bf16[384,4096]{1,0:T(8,128)(2,1)} %bitcast.53), custom_call_target="tpu_custom_call" | custom-call | flops 1000 | bytes 1000 | tf_op jit(solution)/shard_map/pallas_call | solution.py:87
  102.5 3.4 %fusion.24 = (bf16[128,4096]{1,0:T(8,128)(2,1)S(1)}, bf16[128,4096]{1,0:T(8,128)(2,1)S(1)}, bf16[128,4096]{1,0:T(8,128)(2,1)S(1)}, bf16[128,4096]{1,0:T(8,128)(2,1)S(1)}) fusion(bf16[512,4096]{1,0:T(8,128)(2,1)} %get-tuple-element.31), kind=kLoop, calls=%fused_computation.60 | loop fusion | bytes 8388608 | tf_op jit(solution)/shard_map/slice | solution.py:20
  105.9 0.1 collective-permute-start.4
  106.0 0.5 collective-permute-start.5
  106.5 0.1 collective-permute-start.6
  106.6 0.7 collective-permute-start.7
  107.3 4.7 %constant_dynamic-update-slice_fusion.4 = bf16[1024,4096]{1,0:T(8,128)(2,1)} fusion(bf16[512,4096]{1,0:T(8,128)(2,1)} %bitcast.2.rows_ref), kind=kLoop, calls=%fused_computation.44 | loop fusion | bytes 8388608
  112.0 7.3 %shard_map.110 = (bf16[512,384]{1,0:T(8,128)(2,1)S(1)}, f32[512,384]{1,0:T(8,128)S(1)}, f32[512,384]{1,0:T(8,128)S(1)}) custom-call(bf16[512,4096]{1,0:T(8,128)(2,1)} %bitcast.2.rows_ref, bf16[4096,384]{1,0:T(8,128)(2,1)S(1)} %bitcast.58, bf16[4096,384]{1,0:T(8,128)(2,1)} %bitcast.62), custom_call_target="tpu_custom_call" | custom-call | flops 1000 | bytes 1000 | tf_op jit(solution)/shard_map/pallas_call | solution.py:87
  119.3 1.1 constant_dynamic-update-slice_fusion.3
  120.4 2.3 constant_dynamic-update-slice_fusion.2
  122.8 3.5 %pad_maximum_fusion.1.peer_ref = bf16[512,4096]{1,0:T(8,128)(2,1)} fusion(bf16[128,4096]{1,0:T(8,128)(2,1)} %collective-permute-done.7, bf16[128,4096]{1,0:T(8,128)(2,1)S(1)} %collective-permute-done.6, bf16[128,4096]{1,0:T(8,128)(2,1)S(1)} %collective-permute-done.5, bf16[128,4096]{1,0:T(8,128)(2,1)S(1)} %collective-permute-done.4), kind=kLoop, calls=%fused_computation.12 | loop fusion | flops 16777216 | bytes 8388608 | tf_op jit(solution)/shard_map/concatenate | solution.py:21
  126.2 5.5 %shard_map.112 = bf16[512,4096]{1,0:T(8,128)(2,1)} custom-call(bf16[512,384]{1,0:T(8,128)(2,1)S(1)} %get-tuple-element.30.hidden_ref, bf16[512,4096]{1,0:T(8,128)(2,1)} %pad_maximum_fusion.1.peer_ref, bf16[384,4096]{1,0:T(8,128)(2,1)S(1)} %bitcast.55), custom_call_target="tpu_custom_call" | custom-call | flops 1000 | bytes 1000 | tf_op jit(solution)/shard_map/pallas_call | solution.py:87
  131.7 10.1 %all-to-all-done.1 = bf16[64,8,4096]{2,1,0:T(8,128)(2,1)} async-done(((bf16[64,8,4096]{2,1,0:T(8,128)(2,1)}), bf16[64,8,4096]{2,1,0:T(8,128)(2,1)}, u32[]{:S(2)}, u32[]{:S(2)}) %all-to-all-start.1) | async-done | bytes 4194336 | tf_op jit(solution)/shard_map/all_to_all | solution.py:27
  141.8 4.4 %fusion.23 = (bf16[128,4096]{1,0:T(8,128)(2,1)}, bf16[128,4096]{1,0:T(8,128)(2,1)}, bf16[128,4096]{1,0:T(8,128)(2,1)}, bf16[128,4096]{1,0:T(8,128)(2,1)}) fusion(bf16[512,4096]{1,0:T(8,128)(2,1)} %bitcast.4.grads_ref), kind=kLoop, calls=%fused_computation.59 | loop fusion | bytes 8388608 | tf_op jit(solution)/shard_map/slice | solution.py:20
  146.2 0.5 collective-permute-start.11
  146.8 0.5 collective-permute-start.9
  147.3 1.1 constant_dynamic-update-slice_fusion.1
  148.4 1.1 constant_dynamic-update-slice_fusion
  149.5 7.7 %all-to-all-start.2 = ((bf16[64,8,4096]{2,1,0:T(8,128)(2,1)}), bf16[64,8,4096]{2,1,0:T(8,128)(2,1)}, u32[]{:S(2)}, u32[]{:S(2)}) async-start(bf16[64,8,4096]{2,1,0:T(8,128)(2,1)} %bitcast.66), calls=%async_computation.2 | async-start | bytes 8388608 | tf_op jit(solution)/shard_map/all_to_all | solution.py:27
  157.2 4.8 %constant_dynamic-update-slice_fusion.9 = bf16[1024,4096]{1,0:T(8,128)(2,1)} fusion(bf16[512,4096]{1,0:T(8,128)(2,1)} %bitcast.4.grads_ref), kind=kLoop, calls=%fused_computation.49 | loop fusion | bytes 8388608
  161.9 4.2 %shard_map.113 = (bf16[512,384]{1,0:T(8,128)(2,1)S(1)}, bf16[512,384]{1,0:T(8,128)(2,1)S(1)}) custom-call(bf16[512,4096]{1,0:T(8,128)(2,1)} %bitcast.4.grads_ref, f32[512,384]{1,0:T(8,128)S(1)} %copy-done.6, f32[512,384]{1,0:T(8,128)S(1)} %copy-done.8, bf16[384,4096]{1,0:T(8,128)(2,1)S(1)} %bitcast.56), custom_call_target="tpu_custom_call" | custom-call | flops 1000 | bytes 1000 | tf_op jit(solution)/shard_map/pallas_call | solution.py:87
  166.2 4.2 %pad_maximum_fusion.2.grads_ref = bf16[512,4096]{1,0:T(8,128)(2,1)} fusion(bf16[128,4096]{1,0:T(8,128)(2,1)} %collective-permute-done.11, bf16[128,4096]{1,0:T(8,128)(2,1)} %collective-permute-done.10, bf16[128,4096]{1,0:T(8,128)(2,1)} %collective-permute-done.9, bf16[128,4096]{1,0:T(8,128)(2,1)} %collective-permute-done.8), kind=kLoop, calls=%fused_computation.13 | loop fusion | flops 16777216 | bytes 8388608 | tf_op jit(solution)/shard_map/concatenate | solution.py:21
  170.4 0.7 copy-done.10
  171.1 0.4 copy-done.12
  171.5 11.9 %shard_map.114 = (bf16[512,384]{1,0:T(8,128)(2,1)S(1)}, bf16[512,384]{1,0:T(8,128)(2,1)S(1)}, bf16[512,4096]{1,0:T(8,128)(2,1)}) custom-call(bf16[512,4096]{1,0:T(8,128)(2,1)} %pad_maximum_fusion.2.grads_ref, f32[512,384]{1,0:T(8,128)S(1)} %copy-done.10, f32[512,384]{1,0:T(8,128)S(1)} %copy-done.12, bf16[4096,384]{1,0:T(8,128)(2,1)S(1)} %bitcast.59, ...), custom_call_target="tpu_custom_call" | custom-call | flops 1000 | bytes 1000 | tf_op jit(solution)/shard_map/pallas_call | solution.py:87
  183.4 2.6 fusion.22
  186.0 0.1 collective-permute-start.12
  186.1 0.5 collective-permute-start.13
  186.6 0.1 collective-permute-start.14
  186.7 10.0 %collective-permute-start.15 = (bf16[128,4096]{1,0:T(8,128)(2,1)S(1)}, bf16[128,4096]{1,0:T(8,128)(2,1)S(1)}, u32[]{:S(2)}, u32[]{:S(2)}) collective-permute-start(bf16[128,4096]{1,0:T(8,128)(2,1)S(1)} %get-tuple-element.52), channel_id=1, source_target_pairs={{0,64},{64,0},{1,65},{65,1},{2,66},{66,2},{3,67},{67,3},{4,68},{68... | collective-permute-start | bytes 3145736 | tf_op jit(solution)/shard_map/ppermute | solution.py:21
  196.8 2.3 constant_dynamic-update-slice_fusion.8
  199.1 2.3 constant_dynamic-update-slice_fusion.7
  201.4 2.3 constant_dynamic-update-slice_fusion.6
  203.6 2.4 constant_dynamic-update-slice_fusion.5
  206.0 2.3 pad_maximum_fusion.3.peer_ref
  208.3 8.7 %shard_map.115 = bf16[512,4096]{1,0:T(8,128)(2,1)} custom-call(bf16[512,384]{1,0:T(8,128)(2,1)S(1)} %get-tuple-element.35.gate_grad_ref, bf16[512,384]{1,0:T(8,128)(2,1)S(1)} %get-tuple-element.39.up_grad_ref, bf16[512,4096]{1,0:T(8,128)(2,1)} %pad_maximum_fusion.3.peer_ref, bf16[4096,384]{1,0:T(8,128)(2,1)S(1)} %bitcast.60, bf16[4096,384]{1,0:T(8,128)(2,1)} %bitcast.64), custom_call_target="tpu_custom_call" | custom-call | flops 1000 | bytes 1000 | tf_op jit(solution)/shard_map/pallas_call | solution.py:87
  217.0 10.7 %all-to-all-start.3 = ((bf16[64,8,4096]{2,1,0:T(8,128)(2,1)}), bf16[64,8,4096]{2,1,0:T(8,128)(2,1)}, u32[]{:S(2)}, u32[]{:S(2)}) async-start(bf16[64,8,4096]{2,1,0:T(8,128)(2,1)} %bitcast.67), calls=%async_computation.3 | async-start | bytes 8388608 | tf_op jit(solution)/shard_map/all_to_all | solution.py:27
  227.7 8.7 %convolution_convert_fusion.1 = bf16[384,4096]{1,0:T(8,128)(2,1)} fusion(bf16[1024,4096]{1,0:T(8,128)(2,1)} %constant_dynamic-update-slice_fusion.5, bf16[512,384]{1,0:T(8,128)(2,1)S(1)} %copy-done.18, bf16[512,384]{1,0:T(8,128)(2,1)S(1)} %get-tuple-element.30.hidden_ref), kind=kOutput, calls=%fused_computation.2 | convolution fusion | flops 3224371200 | bytes 12320768 | tf_op jit(solution)/shard_map/dot_general | solution.py:15
  236.4 10.1 %convolution_convert_fusion.2 = bf16[4096,384]{1,0:T(8,128)(2,1)} fusion(bf16[1024,4096]{1,0:T(8,128)(2,1)} %constant_dynamic-update-slice_fusion, bf16[512,384]{1,0:T(8,128)(2,1)S(1)} %get-tuple-element.40, bf16[512,384]{1,0:T(8,128)(2,1)S(1)} %copy-done.16), kind=kOutput, calls=%fused_computation.3 | convolution fusion | flops 3224371200 | bytes 12320768 | tf_op jit(solution)/shard_map/dot_general | solution.py:15
  246.5 6.0 %convolution_convert_fusion.3 = bf16[4096,384]{1,0:T(8,128)(2,1)} fusion(bf16[1024,4096]{1,0:T(8,128)(2,1)S(1)} %bitcast.69, bf16[512,384]{1,0:T(8,128)(2,1)S(1)} %get-tuple-element.38, bf16[512,384]{1,0:T(8,128)(2,1)S(1)} %copy-done.14), kind=kOutput, calls=%fused_computation.4 | convolution fusion | flops 3224371200 | bytes 12320768 | tf_op jit(solution)/shard_map/dot_general | solution.py:15
  252.6 2.9 %convolution_multiply_fusion.1 = f32[128,4096]{1,0:T(8,128)S(1)} fusion(bf16[512,4096]{1,0:T(8,128)(2,1)} %bitcast.11, f32[128]{0:T(128)S(1)} %get-tuple-element.70, s32[128]{0:T(128)S(1)} %get-tuple-element.68), kind=kOutput, calls=%fused_computation.8 | convolution fusion | flops 537460736 | bytes 6292480 | tf_op jit(solution)/shard_map/dot_general | solution.py:15
  255.5 4.1 %fusion.2 = bf16[128,4096]{1,0:T(8,128)(2,1)} fusion(f32[128,4096]{1,0:T(8,128)S(1)} %convolution_multiply_fusion.1, bf16[512,4096]{1,0:T(8,128)(2,1)} %bitcast.11, f32[128]{0:T(128)S(1)} %get-tuple-element.69, s32[128]{0:T(128)S(1)} %get-tuple-element.67), kind=kOutput, calls=%fused_computation.9 | convolution fusion | flops 538509312 | bytes 7341056 | tf_op jit(solution)/shard_map/dot_general | solution.py:15
  259.7 22.5 %all-to-all-done.3 = bf16[64,8,4096]{2,1,0:T(8,128)(2,1)} async-done(((bf16[64,8,4096]{2,1,0:T(8,128)(2,1)}), bf16[64,8,4096]{2,1,0:T(8,128)(2,1)}, u32[]{:S(2)}, u32[]{:S(2)}) %all-to-all-start.3) | async-done | bytes 4194336 | tf_op jit(solution)/shard_map/all_to_all | solution.py:27
  282.1 3.9 %convolution_convert_fusion.4 = bf16[128,4096]{1,0:T(8,128)(2,1)} fusion(pred[512,128]{1,0:T(8,128)(4,1)S(1)} %copy-done.24, bf16[512,4096]{1,0:T(8,128)(2,1)} %bitcast.15), kind=kOutput, calls=%fused_computation.10 | convolution fusion | flops 537395200 | bytes 5308416 | tf_op jit(solution)/shard_map/dot_general | solution.py:15
  (83 shorter events, 0.2 us)
Async XLA Ops:
  0.6 3.1 %copy-start = (bf16[128,4096]{1,0:T(8,128)(2,1)S(1)}, bf16[128,4096]{1,0:T(8,128)(2,1)}, u32[]{:S(2)}) copy-start(bf16[128,4096]{1,0:T(8,128)(2,1)} %param.7) | copy-start | bytes 3145732
  3.8 15.4 %copy-start.23 = (pred[512,128]{1,0:T(8,128)(4,1)}, pred[512,128]{1,0:T(8,128)(4,1)S(1)}, u32[]{:S(2)}) copy-start(pred[512,128]{1,0:T(8,128)(4,1)S(1)} %fusion.12) | copy-start | bytes 196612
  7.0 11.9 %copy-start.26 = (f32[128,2]{0,1:T(2,128)S(1)}, f32[128,2]{0,1:T(2,128)}, u32[]{:S(2)}) copy-start(f32[128,2]{0,1:T(2,128)} %param.10) | copy-start | bytes 3076
  7.0 12.1 %copy-start.25 = (bf16[128,4096]{1,0:T(8,128)(2,1)S(1)}, bf16[128,4096]{1,0:T(8,128)(2,1)}, u32[]{:S(2)}) copy-start(bf16[128,4096]{1,0:T(8,128)(2,1)} %param.8) | copy-start | bytes 3145732
  7.0 66.6 %all-to-all-start = ((bf16[64,8,4096]{2,1,0:T(8,128)(2,1)}), bf16[64,8,4096]{2,1,0:T(8,128)(2,1)}, u32[]{:S(2)}, u32[]{:S(2)}) async-start(bf16[64,8,4096]{2,1,0:T(8,128)(2,1)} %fusion), calls=%async_computation | async-start | bytes 8388608 | tf_op jit(solution)/shard_map/all_to_all | solution.py:27
  77.9 8.7 %collective-permute-start = (bf16[128,4096]{1,0:T(8,128)(2,1)}, bf16[128,4096]{1,0:T(8,128)(2,1)S(1)}, u32[]{:S(2)}, u32[]{:S(2)}) collective-permute-start(bf16[128,4096]{1,0:T(8,128)(2,1)} %get-tuple-element.66), channel_id=1, source_target_pairs={{0,64},{64,0},{1,65},{65,1},{2,66},{66,2},{3,67},{67,3},{4,68},{68... | collective-permute-start | bytes 3145736 | tf_op jit(solution)/shard_map/ppermute | solution.py:21
  77.9 8.7 %collective-permute-start.1 = (bf16[128,4096]{1,0:T(8,128)(2,1)}, bf16[128,4096]{1,0:T(8,128)(2,1)}, u32[]{:S(2)}, u32[]{:S(2)}) collective-permute-start(bf16[128,4096]{1,0:T(8,128)(2,1)} %get-tuple-element.65), channel_id=1, source_target_pairs={{0,64},{64,0},{1,65},{65,1},{2,66},{66,2},{3,67},{67,3},{4,68},{68... | collective-permute-start | bytes 3145736 | tf_op jit(solution)/shard_map/ppermute | solution.py:21
  78.4 8.3 %collective-permute-start.2 = (bf16[128,4096]{1,0:T(8,128)(2,1)}, bf16[128,4096]{1,0:T(8,128)(2,1)S(1)}, u32[]{:S(2)}, u32[]{:S(2)}) collective-permute-start(bf16[128,4096]{1,0:T(8,128)(2,1)} %get-tuple-element.64), channel_id=1, source_target_pairs={{0,64},{64,0},{1,65},{65,1},{2,66},{66,2},{3,67},{67,3},{4,68},{68... | collective-permute-start | bytes 3145736 | tf_op jit(solution)/shard_map/ppermute | solution.py:21
  78.5 8.3 %collective-permute-start.3 = (bf16[128,4096]{1,0:T(8,128)(2,1)}, bf16[128,4096]{1,0:T(8,128)(2,1)S(1)}, u32[]{:S(2)}, u32[]{:S(2)}) collective-permute-start(bf16[128,4096]{1,0:T(8,128)(2,1)} %get-tuple-element.63), channel_id=1, source_target_pairs={{0,64},{64,0},{1,65},{65,1},{2,66},{66,2},{3,67},{67,3},{4,68},{68... | collective-permute-start | bytes 3145736 | tf_op jit(solution)/shard_map/ppermute | solution.py:21
  79.0 62.9 %all-to-all-start.1 = ((bf16[64,8,4096]{2,1,0:T(8,128)(2,1)}), bf16[64,8,4096]{2,1,0:T(8,128)(2,1)}, u32[]{:S(2)}, u32[]{:S(2)}) async-start(bf16[64,8,4096]{2,1,0:T(8,128)(2,1)} %bitcast.65), calls=%async_computation.1 | async-start | bytes 8388608 | tf_op jit(solution)/shard_map/all_to_all | solution.py:27
  86.7 3.9 %copy-start.3 = (bf16[1,4096,384]{2,1,0:T(8,128)(2,1)S(1)}, bf16[1,4096,384]{2,1,0:T(8,128)(2,1)}, u32[]{:S(2)}) copy-start(bf16[1,4096,384]{2,1,0:T(8,128)(2,1)} %param.11) | copy-start | bytes 9437188
  86.7 3.8 %copy-start.19 = (bf16[128,4096]{1,0:T(8,128)(2,1)}, bf16[128,4096]{1,0:T(8,128)(2,1)S(1)}, u32[]{:S(2)}) copy-start(bf16[128,4096]{1,0:T(8,128)(2,1)S(1)} %collective-permute-done.2) | copy-start | bytes 3145732
  86.7 3.8 %copy-start.21 = (bf16[128,4096]{1,0:T(8,128)(2,1)}, bf16[128,4096]{1,0:T(8,128)(2,1)S(1)}, u32[]{:S(2)}) copy-start(bf16[128,4096]{1,0:T(8,128)(2,1)S(1)} %collective-permute-done.3) | copy-start | bytes 3145732
  102.5 3.4 %copy-start.9 = (f32[512,384]{1,0:T(8,128)}, f32[512,384]{1,0:T(8,128)S(1)}, u32[]{:S(2)}) copy-start(f32[512,384]{1,0:T(8,128)S(1)} %get-tuple-element.36.act_ref) | copy-start | bytes 2359300
  102.5 3.4 %copy-start.11 = (f32[512,384]{1,0:T(8,128)}, f32[512,384]{1,0:T(8,128)S(1)}, u32[]{:S(2)}) copy-start(f32[512,384]{1,0:T(8,128)S(1)} %get-tuple-element.37.slope_ref) | copy-start | bytes 2359300
  102.5 3.4 %copy-start.17 = (bf16[512,384]{1,0:T(8,128)(2,1)}, bf16[512,384]{1,0:T(8,128)(2,1)S(1)}, u32[]{:S(2)}) copy-start(bf16[512,384]{1,0:T(8,128)(2,1)S(1)} %get-tuple-element.41) | copy-start | bytes 1179652
  105.9 16.8 %collective-permute-start.4 = (bf16[128,4096]{1,0:T(8,128)(2,1)S(1)}, bf16[128,4096]{1,0:T(8,128)(2,1)S(1)}, u32[]{:S(2)}, u32[]{:S(2)}) collective-permute-start(bf16[128,4096]{1,0:T(8,128)(2,1)S(1)} %get-tuple-element.59), channel_id=1, source_target_pairs={{0,64},{64,0},{1,65},{65,1},{2,66},{66,2},{3,67},{67,3},{4,68},{68... | collective-permute-start | bytes 3145736 | tf_op jit(solution)/shard_map/ppermute | solution.py:21
  106.0 16.7 %collective-permute-start.5 = (bf16[128,4096]{1,0:T(8,128)(2,1)S(1)}, bf16[128,4096]{1,0:T(8,128)(2,1)S(1)}, u32[]{:S(2)}, u32[]{:S(2)}) collective-permute-start(bf16[128,4096]{1,0:T(8,128)(2,1)S(1)} %get-tuple-element.62), channel_id=1, source_target_pairs={{0,64},{64,0},{1,65},{65,1},{2,66},{66,2},{3,67},{67,3},{4,68},{68... | collective-permute-start | bytes 3145736 | tf_op jit(solution)/shard_map/ppermute | solution.py:21
  106.5 16.2 %collective-permute-start.6 = (bf16[128,4096]{1,0:T(8,128)(2,1)S(1)}, bf16[128,4096]{1,0:T(8,128)(2,1)S(1)}, u32[]{:S(2)}, u32[]{:S(2)}) collective-permute-start(bf16[128,4096]{1,0:T(8,128)(2,1)S(1)} %get-tuple-element.61), channel_id=1, source_target_pairs={{0,64},{64,0},{1,65},{65,1},{2,66},{66,2},{3,67},{67,3},{4,68},{68... | collective-permute-start | bytes 3145736 | tf_op jit(solution)/shard_map/ppermute | solution.py:21
  106.6 16.1 %collective-permute-start.7 = (bf16[128,4096]{1,0:T(8,128)(2,1)S(1)}, bf16[128,4096]{1,0:T(8,128)(2,1)}, u32[]{:S(2)}, u32[]{:S(2)}) collective-permute-start(bf16[128,4096]{1,0:T(8,128)(2,1)S(1)} %get-tuple-element.60), channel_id=1, source_target_pairs={{0,64},{64,0},{1,65},{65,1},{2,66},{66,2},{3,67},{67,3},{4,68},{68... | collective-permute-start | bytes 3145736 | tf_op jit(solution)/shard_map/ppermute | solution.py:21
  119.3 6.9 %copy-start.5 = (f32[512,384]{1,0:T(8,128)}, f32[512,384]{1,0:T(8,128)S(1)}, u32[]{:S(2)}) copy-start(f32[512,384]{1,0:T(8,128)S(1)} %get-tuple-element.33.act_ref) | copy-start | bytes 2359300
  119.3 6.9 %copy-start.7 = (f32[512,384]{1,0:T(8,128)}, f32[512,384]{1,0:T(8,128)S(1)}, u32[]{:S(2)}) copy-start(f32[512,384]{1,0:T(8,128)S(1)} %get-tuple-element.34.slope_ref) | copy-start | bytes 2359300
  122.7 3.5 %copy-start.2 = (bf16[1,384,4096]{2,1,0:T(8,128)(2,1)S(1)}, bf16[1,384,4096]{2,1,0:T(8,128)(2,1)}, u32[]{:S(2)}) copy-start(bf16[1,384,4096]{2,1,0:T(8,128)(2,1)} %param.13) | copy-start | bytes 9437188
  141.8 5.5 %copy-start.20 = (bf16[128,4096]{1,0:T(8,128)(2,1)S(1)}, bf16[128,4096]{1,0:T(8,128)(2,1)}, u32[]{:S(2)}) copy-start(bf16[128,4096]{1,0:T(8,128)(2,1)} %copy-done.19) | copy-start | bytes 3145732
  141.8 6.6 %copy-start.22 = (bf16[128,4096]{1,0:T(8,128)(2,1)S(1)}, bf16[128,4096]{1,0:T(8,128)(2,1)}, u32[]{:S(2)}) copy-start(bf16[128,4096]{1,0:T(8,128)(2,1)} %copy-done.21) | copy-start | bytes 3145732
  146.2 19.9 %collective-permute-start.10 = (bf16[128,4096]{1,0:T(8,128)(2,1)}, bf16[128,4096]{1,0:T(8,128)(2,1)}, u32[]{:S(2)}, u32[]{:S(2)}) collective-permute-start(bf16[128,4096]{1,0:T(8,128)(2,1)} %get-tuple-element.57), channel_id=1, source_target_pairs={{0,64},{64,0},{1,65},{65,1},{2,66},{66,2},{3,67},{67,3},{4,68},{68... | collective-permute-start | bytes 3145736 | tf_op jit(solution)/shard_map/ppermute | solution.py:21
  146.2 19.9 %collective-permute-start.11 = (bf16[128,4096]{1,0:T(8,128)(2,1)}, bf16[128,4096]{1,0:T(8,128)(2,1)}, u32[]{:S(2)}, u32[]{:S(2)}) collective-permute-start(bf16[128,4096]{1,0:T(8,128)(2,1)} %get-tuple-element.56), channel_id=1, source_target_pairs={{0,64},{64,0},{1,65},{65,1},{2,66},{66,2},{3,67},{67,3},{4,68},{68... | collective-permute-start | bytes 3145736 | tf_op jit(solution)/shard_map/ppermute | solution.py:21
  146.8 19.4 %collective-permute-start.8 = (bf16[128,4096]{1,0:T(8,128)(2,1)}, bf16[128,4096]{1,0:T(8,128)(2,1)}, u32[]{:S(2)}, u32[]{:S(2)}) collective-permute-start(bf16[128,4096]{1,0:T(8,128)(2,1)} %get-tuple-element.55), channel_id=1, source_target_pairs={{0,64},{64,0},{1,65},{65,1},{2,66},{66,2},{3,67},{67,3},{4,68},{68... | collective-permute-start | bytes 3145736 | tf_op jit(solution)/shard_map/ppermute | solution.py:21
  146.8 19.4 %collective-permute-start.9 = (bf16[128,4096]{1,0:T(8,128)(2,1)}, bf16[128,4096]{1,0:T(8,128)(2,1)}, u32[]{:S(2)}, u32[]{:S(2)}) collective-permute-start(bf16[128,4096]{1,0:T(8,128)(2,1)} %get-tuple-element.58), channel_id=1, source_target_pairs={{0,64},{64,0},{1,65},{65,1},{2,66},{66,2},{3,67},{67,3},{4,68},{68... | collective-permute-start | bytes 3145736 | tf_op jit(solution)/shard_map/ppermute | solution.py:21
  149.5 67.6 %all-to-all-start.2 = ((bf16[64,8,4096]{2,1,0:T(8,128)(2,1)}), bf16[64,8,4096]{2,1,0:T(8,128)(2,1)}, u32[]{:S(2)}, u32[]{:S(2)}) async-start(bf16[64,8,4096]{2,1,0:T(8,128)(2,1)} %bitcast.66), calls=%async_computation.2 | async-start | bytes 8388608 | tf_op jit(solution)/shard_map/all_to_all | solution.py:27
  157.1 4.8 %copy-start.6 = (f32[512,384]{1,0:T(8,128)S(1)}, f32[512,384]{1,0:T(8,128)}, u32[]{:S(2)}) copy-start(f32[512,384]{1,0:T(8,128)} %copy-done.5) | copy-start | bytes 2359300
  157.2 4.8 %copy-start.8 = (f32[512,384]{1,0:T(8,128)S(1)}, f32[512,384]{1,0:T(8,128)}, u32[]{:S(2)}) copy-start(f32[512,384]{1,0:T(8,128)} %copy-done.7) | copy-start | bytes 2359300
  166.1 42.2 %copy-start.13 = (bf16[512,384]{1,0:T(8,128)(2,1)}, bf16[512,384]{1,0:T(8,128)(2,1)S(1)}, u32[]{:S(2)}) copy-start(bf16[512,384]{1,0:T(8,128)(2,1)S(1)} %get-tuple-element.35.gate_grad_ref) | copy-start | bytes 1179652
  166.1 42.2 %copy-start.15 = (bf16[512,384]{1,0:T(8,128)(2,1)}, bf16[512,384]{1,0:T(8,128)(2,1)S(1)}, u32[]{:S(2)}) copy-start(bf16[512,384]{1,0:T(8,128)(2,1)S(1)} %get-tuple-element.39.up_grad_ref) | copy-start | bytes 1179652
  166.1 4.3 %copy-start.4 = (bf16[1,4096,384]{2,1,0:T(8,128)(2,1)S(1)}, bf16[1,4096,384]{2,1,0:T(8,128)(2,1)}, u32[]{:S(2)}) copy-start(bf16[1,4096,384]{2,1,0:T(8,128)(2,1)} %param.11) | copy-start | bytes 9437188
  166.1 5.0 %copy-start.10 = (f32[512,384]{1,0:T(8,128)S(1)}, f32[512,384]{1,0:T(8,128)}, u32[]{:S(2)}) copy-start(f32[512,384]{1,0:T(8,128)} %copy-done.9) | copy-start | bytes 2359300
  166.1 5.4 %copy-start.12 = (f32[512,384]{1,0:T(8,128)S(1)}, f32[512,384]{1,0:T(8,128)}, u32[]{:S(2)}) copy-start(f32[512,384]{1,0:T(8,128)} %copy-done.11) | copy-start | bytes 2359300
  186.0 20.0 %collective-permute-start.12 = (bf16[128,4096]{1,0:T(8,128)(2,1)S(1)}, bf16[128,4096]{1,0:T(8,128)(2,1)S(1)}, u32[]{:S(2)}, u32[]{:S(2)}) collective-permute-start(bf16[128,4096]{1,0:T(8,128)(2,1)S(1)} %get-tuple-element.51), channel_id=1, source_target_pairs={{0,64},{64,0},{1,65},{65,1},{2,66},{66,2},{3,67},{67,3},{4,68},{68... | collective-permute-start | bytes 3145736 | tf_op jit(solution)/shard_map/ppermute | solution.py:21
  186.1 19.9 %collective-permute-start.13 = (bf16[128,4096]{1,0:T(8,128)(2,1)S(1)}, bf16[128,4096]{1,0:T(8,128)(2,1)S(1)}, u32[]{:S(2)}, u32[]{:S(2)}) collective-permute-start(bf16[128,4096]{1,0:T(8,128)(2,1)S(1)} %get-tuple-element.54), channel_id=1, source_target_pairs={{0,64},{64,0},{1,65},{65,1},{2,66},{66,2},{3,67},{67,3},{4,68},{68... | collective-permute-start | bytes 3145736 | tf_op jit(solution)/shard_map/ppermute | solution.py:21
  186.6 19.4 %collective-permute-start.14 = (bf16[128,4096]{1,0:T(8,128)(2,1)S(1)}, bf16[128,4096]{1,0:T(8,128)(2,1)S(1)}, u32[]{:S(2)}, u32[]{:S(2)}) collective-permute-start(bf16[128,4096]{1,0:T(8,128)(2,1)S(1)} %get-tuple-element.53), channel_id=1, source_target_pairs={{0,64},{64,0},{1,65},{65,1},{2,66},{66,2},{3,67},{67,3},{4,68},{68... | collective-permute-start | bytes 3145736 | tf_op jit(solution)/shard_map/ppermute | solution.py:21
  186.7 19.3 %collective-permute-start.15 = (bf16[128,4096]{1,0:T(8,128)(2,1)S(1)}, bf16[128,4096]{1,0:T(8,128)(2,1)S(1)}, u32[]{:S(2)}, u32[]{:S(2)}) collective-permute-start(bf16[128,4096]{1,0:T(8,128)(2,1)S(1)} %get-tuple-element.52), channel_id=1, source_target_pairs={{0,64},{64,0},{1,65},{65,1},{2,66},{66,2},{3,67},{67,3},{4,68},{68... | collective-permute-start | bytes 3145736 | tf_op jit(solution)/shard_map/ppermute | solution.py:21
  217.0 10.7 %copy-start.18 = (bf16[512,384]{1,0:T(8,128)(2,1)S(1)}, bf16[512,384]{1,0:T(8,128)(2,1)}, u32[]{:S(2)}) copy-start(bf16[512,384]{1,0:T(8,128)(2,1)} %copy-done.17) | copy-start | bytes 1179652
  217.0 65.1 %all-to-all-start.3 = ((bf16[64,8,4096]{2,1,0:T(8,128)(2,1)}), bf16[64,8,4096]{2,1,0:T(8,128)(2,1)}, u32[]{:S(2)}, u32[]{:S(2)}) async-start(bf16[64,8,4096]{2,1,0:T(8,128)(2,1)} %bitcast.67), calls=%async_computation.3 | async-start | bytes 8388608 | tf_op jit(solution)/shard_map/all_to_all | solution.py:27
  227.7 8.7 %copy-start.16 = (bf16[512,384]{1,0:T(8,128)(2,1)S(1)}, bf16[512,384]{1,0:T(8,128)(2,1)}, u32[]{:S(2)}) copy-start(bf16[512,384]{1,0:T(8,128)(2,1)} %copy-done.15) | copy-start | bytes 1179652
  227.7 18.8 %slice-start = ((s8[8388608]{0:T(1024)(128)(4,1)}), s8[4194304]{0:T(1024)(128)(4,1)S(1)}, s32[]{:S(2)}) async-start(s8[8388608]{0:T(1024)(128)(4,1)} %bitcast.68), calls=%async_computation.4 | async-start | bytes 8388608
  236.4 10.1 %copy-start.14 = (bf16[512,384]{1,0:T(8,128)(2,1)S(1)}, bf16[512,384]{1,0:T(8,128)(2,1)}, u32[]{:S(2)}) copy-start(bf16[512,384]{1,0:T(8,128)(2,1)} %copy-done.13) | copy-start | bytes 1179652
  236.4 10.1 %slice-start.1 = ((s8[8388608]{0:T(1024)(128)(4,1)}), s8[4194304]{0:T(1024)(128)(4,1)S(1)}, s32[]{:S(2)}) async-start(s8[8388608]{0:T(1024)(128)(4,1)} %bitcast.68), calls=%async_computation.5 | async-start | bytes 8388608
  255.5 26.6 %copy-start.24 = (pred[512,128]{1,0:T(8,128)(4,1)S(1)}, pred[512,128]{1,0:T(8,128)(4,1)}, u32[]{:S(2)}) copy-start(pred[512,128]{1,0:T(8,128)(4,1)} %copy-done.23) | copy-start | bytes 196612
  255.5 30.5 %copy-start.1 = (bf16[128,4096]{1,0:T(8,128)(2,1)S(1)}, bf16[128,4096]{1,0:T(8,128)(2,1)}, u32[]{:S(2)}) copy-start(bf16[128,4096]{1,0:T(8,128)(2,1)} %param.7) | copy-start | bytes 3145732

commit v3 on v1

v3 whole, which is shorter than its diff:
```python
import functools

import jax
import jax.numpy as jnp
from jax import lax
from jax.experimental import pallas as pl
from jax.experimental.pallas import tpu as pltpu
from jax.sharding import PartitionSpec as P

HOT = 4
COLUMNS = 512
PARTS = 2
BF16 = jnp.bfloat16
F32 = jnp.float32
MIB = 1024 * 1024


def dot(left, right, dims):
    return lax.dot_general(left, right, (dims, ((), ())), preferred_element_type=F32)


def swap(value):
    return lax.ppermute(value, "dp", [(0, 1), (1, 0)])


def exchange(value, experts):
    rows, features = value.shape
    parts = value.reshape(experts, rows // experts, features)
    moved = lax.all_to_all(parts, "expert", split_axis=0, concat_axis=0, tiled=True)
    return moved.reshape(rows, features)


def call(kernel, args, outs, limit, grid=(), scratch=()):
    in_specs = [spec for _, spec in args]
    return pl.pallas_call(
        kernel,
        grid=grid,
        in_specs=in_specs,
        out_specs=[spec for _, _, spec in outs],
        out_shape=[jax.ShapeDtypeStruct(shape, kind) for shape, kind, _ in outs],
        scratch_shapes=scratch,
        compiler_params=pltpu.CompilerParams(vmem_limit_bytes=limit * MIB),
        cost_estimate=pl.CostEstimate(flops=1000, bytes_accessed=1000, transcendentals=0),
    )(*[arg for arg, _ in args])


def whole(arg):
    return arg, pl.BlockSpec(memory_space=pltpu.VMEM)


def fixed(arg):
    return arg, pl.BlockSpec(arg.shape, lambda i: (0, 0))


def across(arg):
    return arg, pl.BlockSpec((arg.shape[0], COLUMNS), lambda i: (0, i))


def out_whole(shape, kind):
    return shape, kind, pl.BlockSpec(memory_space=pltpu.VMEM)


def by_column(rows, columns, kind):
    return (rows, columns), kind, pl.BlockSpec((rows, COLUMNS), lambda i: (0, i))


def joined(refs):
    return jnp.concatenate([ref[...] for ref in refs], axis=0)


def hidden_parts(rows, gate_matrix, up_matrix):
    gate_pre = dot(rows, gate_matrix, ((1,), (0,)))
    up_pre = dot(rows, up_matrix, ((1,), (0,)))
    sig_gate = jax.nn.sigmoid(gate_pre)
    activated = gate_pre * sig_gate
    hidden = (activated * up_pre).astype(BF16)
    gate_slope = up_pre * sig_gate * (1.0 + gate_pre * (1.0 - sig_gate))
    return hidden, activated, gate_slope


def grad_parts(grads, act, slope, down_matrix):
    hidden_grad = dot(grads, down_matrix, ((1,), (1,)))
    return (hidden_grad * slope).astype(BF16), (hidden_grad * act).astype(BF16)


def input_parts(gate_grad, up_grad, gate_matrix, up_matrix):
    return dot(gate_grad, gate_matrix, ((1,), (1,))) + dot(up_grad, up_matrix, ((1,), (1,)))


def places(routing_ref, position_ref, experts, capacity):
    tok_rows, top_count = routing_ref.shape
    expert_ids = lax.broadcasted_iota(jnp.int32, (tok_rows, experts), 1)
    named = [routing_ref[:, column : column + 1] == expert_ids for column in range(top_count)]
    counts = sum(hit.astype(F32) for hit in named)
    earlier = lax.broadcasted_iota(jnp.int32, (tok_rows, tok_rows), 1) < lax.broadcasted_iota(
        jnp.int32, (tok_rows, tok_rows), 0
    )
    before = dot(earlier.astype(F32).astype(BF16), counts.astype(BF16), ((1,), (0,)))
    for column, hit in enumerate(named):
        slot = jnp.sum(jnp.where(hit, before, 0.0), axis=1, keepdims=True).astype(jnp.int32)
        position_ref[:, column : column + 1] = routing_ref[:, column : column + 1] * capacity + slot


def pick_matrix(position_ref, local_rows):
    tok_rows, top_count = position_ref.shape
    slots = lax.broadcasted_iota(jnp.int32, (tok_rows, local_rows), 1)
    return sum((position_ref[:, column : column + 1] == slots).astype(F32) for column in range(top_count)).astype(BF16)


def dispatch_kernel(routing_ref, tokens_ref, position_ref, out_ref, pick_ref, *, experts, capacity):
    @pl.when(pl.program_id(0) == 0)
    def _():
        places(routing_ref, position_ref, experts, capacity)
        pick_ref[...] = pick_matrix(position_ref, pick_ref.shape[1])

    out_ref[...] = dot(pick_ref[...], tokens_ref[...], ((0,), (0,))).astype(BF16)


def token_grad_kernel(position_ref, rows_ref, out_ref, pick_ref):
    @pl.when(pl.program_id(0) == 0)
    def _():
        pick_ref[...] = pick_matrix(position_ref, pick_ref.shape[1])

    out_ref[...] = dot(pick_ref[...], rows_ref[...], ((1,), (0,))).astype(BF16)


def combine_kernel(position_ref, weight_ref, rows_ref, out_ref):
    rows = rows_ref[...]
    tok_rows, top_count = position_ref.shape
    slots = lax.broadcasted_iota(jnp.int32, (tok_rows, rows.shape[0]), 1)
    total = jnp.zeros(out_ref.shape, F32)
    for column in range(top_count):
        pick = (position_ref[:, column : column + 1] == slots).astype(F32).astype(BF16)
        total += weight_ref[:, column : column + 1] * dot(pick, rows, ((1,), (0,)))
    out_ref[...] = total.astype(BF16)


def hidden_kernel(rows_ref, gate_ref, up_ref, hidden_ref, act_ref, slope_ref):
    hidden_ref[...], act_ref[...], slope_ref[...] = hidden_parts(rows_ref[...], gate_ref[...], up_ref[...])


def forward_kernel(rows_ref, gate_ref, up_ref, down_ref, hidden_ref, act_ref, slope_ref, *out_refs):
    hidden, act_ref[...], slope_ref[...] = hidden_parts(rows_ref[...], gate_ref[...], up_ref[...])
    hidden_ref[...] = hidden
    size = hidden.shape[0] // len(out_refs)
    for i, out_ref in enumerate(out_refs):
        out_ref[...] = dot(hidden[i * size : (i + 1) * size], down_ref[...], ((1,), (0,))).astype(BF16)


def out_kernel(hidden_ref, down_ref, *refs):
    peer_refs, out_ref = refs[:-1], refs[-1]
    size = hidden_ref.shape[0] // len(peer_refs)
    for i, peer_ref in enumerate(peer_refs):
        rows = slice(i * size, (i + 1) * size)
        total = dot(hidden_ref[rows], down_ref[...], ((1,), (0,))) + peer_ref[...].astype(F32)
        out_ref[rows] = total.astype(BF16)


def grad_kernel(grads_ref, act_ref, slope_ref, down_ref, gate_grad_ref, up_grad_ref):
    gate_grad_ref[...], up_grad_ref[...] = grad_parts(grads_ref[...], act_ref[...], slope_ref[...], down_ref[...])


def backward_kernel(grads_ref, act_ref, slope_ref, gate_ref, up_ref, down_ref, gate_grad_ref, up_grad_ref, *in_refs):
    gate_grad, up_grad = grad_parts(grads_ref[...], act_ref[...], slope_ref[...], down_ref[...])
    gate_grad_ref[...] = gate_grad
    up_grad_ref[...] = up_grad
    size = gate_grad.shape[0] // len(in_refs)
    for i, in_ref in enumerate(in_refs):
        rows = slice(i * size, (i + 1) * size)
        in_ref[...] = input_parts(gate_grad[rows], up_grad[rows], gate_ref[...], up_ref[...]).astype(BF16)


def input_kernel(gate_grad_ref, up_grad_ref, gate_ref, up_ref, *refs):
    peer_refs, out_ref = refs[:-1], refs[-1]
    size = gate_grad_ref.shape[0] // len(peer_refs)
    for i, peer_ref in enumerate(peer_refs):
        rows = slice(i * size, (i + 1) * size)
        total = input_parts(gate_grad_ref[rows], up_grad_ref[rows], gate_ref[...], up_ref[...])
        out_ref[rows] = (total + peer_ref[...].astype(F32)).astype(BF16)


def weight_kernel(*refs):
    rows, grads, hidden, gate_grad, up_grad = (refs[2 * i : 2 * i + 2] for i in range(5))
    gate_out, up_out, down_out = refs[10:]
    both = jnp.concatenate([joined(gate_grad), joined(up_grad)], axis=1)
    total = dot(joined(rows), both, ((0,), (0,)))
    width = gate_out.shape[1]
    gate_out[...] = total[:, :width].astype(BF16)
    up_out[...] = total[:, width:].astype(BF16)
    down_out[...] = dot(joined(hidden), joined(grads), ((0,), (0,))).astype(BF16)


def weight_grads(wide, kept):
    features = wide[0].shape[1]
    width = kept[0].shape[1]
    args = [(value, pl.BlockSpec((value.shape[0], COLUMNS), lambda i: (0, i))) for value in wide]
    args += [fixed(value) for value in kept]
    tall = ((features, width), BF16, pl.BlockSpec((COLUMNS, width), lambda i: (i, 0)))
    return call(weight_kernel, args, [tall, tall, by_column(width, features, BF16)], 48, grid=(features // COLUMNS,))


def local(tokens, cotangent, routing, combine_weights, w_gate, w_up, w_down):
    tok_rows, features = tokens.shape
    top_count = routing.shape[1]
    experts = lax.axis_size("expert")
    cold_count = experts - HOT
    hot_cap = 2 * tok_rows * top_count // experts
    cold_cap = (tok_rows * top_count - HOT * hot_cap + cold_count - 1) // cold_count
    capacity = max(hot_cap, cold_cap)
    local_rows = experts * capacity
    gate_matrix, up_matrix, down_matrix = w_gate[0], w_up[0], w_down[0]
    width = gate_matrix.shape[1]
    grid = (features // COLUMNS,)
    pick_scratch = [pltpu.VMEM((tok_rows, local_rows), BF16)]

    position, send_rows = call(
        functools.partial(dispatch_kernel, experts=experts, capacity=capacity),
        [fixed(routing), across(tokens)],
        [(routing.shape, jnp.int32, pl.BlockSpec(routing.shape, lambda i: (0, 0))), by_column(local_rows, features, BF16)],
        24,
        grid=grid,
        scratch=pick_scratch,
    )
    rows_own = exchange(send_rows, experts)
    targets = jnp.arange(local_rows, dtype=jnp.int32)
    selected = position[None, :, :] == targets[:, None, None]
    picker = jnp.any(selected, axis=2).astype(BF16)
    slot_weight = jnp.sum(jnp.where(selected, combine_weights[None, :, :], 0.0), axis=(1, 2))
    send_grads = (slot_weight[:, None] * dot(picker, cotangent, ((1,), (0,)))).astype(BF16)
    rows_own, send_grads = lax.optimization_barrier((rows_own, send_grads))
    grads_own = exchange(send_grads, experts)

    weights = [whole(matrix) for matrix in (gate_matrix, up_matrix, down_matrix)]
    kept = [out_whole((local_rows, width), kind) for kind in (BF16, F32, F32)]
    pair = [out_whole((local_rows, width), BF16)] * 2
    parts = [out_whole((local_rows // PARTS, features), BF16)] * PARTS
    send = [out_whole((local_rows, features), BF16)]

    rows_peer = swap(rows_own)
    hidden_own, act_own, slope_own = call(hidden_kernel, [whole(rows_own)] + weights[:2], kept, 32)
    hidden_peer, act_peer, slope_peer, *outs = call(forward_kernel, [whole(rows_peer)] + weights, kept + parts, 40)
    outs = [swap(out) for out in outs]
    (out_send,) = call(out_kernel, [whole(hidden_own)] + weights[2:] + [whole(out) for out in outs], send, 32)
    grads_own, out_send = lax.optimization_barrier((grads_own, out_send))
    out_back = exchange(out_send, experts)

    grads_peer = swap(grads_own)
    gate_own, up_own = call(
        grad_kernel, [whole(value) for value in (grads_own, act_own, slope_own)] + weights[2:], pair, 32
    )
    gate_peer, up_peer, *ins = call(
        backward_kernel, [whole(value) for value in (grads_peer, act_peer, slope_peer)] + weights, pair + parts, 40
    )
    ins = [swap(value) for value in ins]
    (input_send,) = call(
        input_kernel, [whole(gate_own), whole(up_own)] + weights[:2] + [whole(value) for value in ins], send, 32
    )
    out_back, input_send = lax.optimization_barrier((out_back, input_send))
    input_back = exchange(input_send, experts)

    wgrads = weight_grads(
        [rows_own, rows_peer, grads_own, grads_peer],
        [hidden_own, hidden_peer, gate_own, gate_peer, up_own, up_peer],
    )
    (combined,) = call(
        combine_kernel,
        [fixed(position), fixed(combine_weights), across(out_back)],
        [by_column(tok_rows, features, BF16)],
        24,
        grid=grid,
    )
    *wgrads, combined, input_back = lax.optimization_barrier((*wgrads, combined, input_back))
    (token_grad,) = call(
        token_grad_kernel,
        [fixed(position), across(input_back)],
        [by_column(tok_rows, features, BF16)],
        24,
        grid=grid,
        scratch=pick_scratch,
    )
    return combined, token_grad, wgrads[0][None], wgrads[1][None], wgrads[2][None]


def solution(mesh):
    in_specs = (
        P(("dp", "expert"), None),
        P(("dp", "expert"), None),
        P(("dp", "expert"), None),
        P(("dp", "expert"), None),
        P("expert", None, "dp"),
        P("expert", None, "dp"),
        P("expert", "dp", None),
    )
    out_specs = (
        P(("dp", "expert"), None),
        P(("dp", "expert"), None),
        P("expert", None, "dp"),
        P("expert", None, "dp"),
        P("expert", "dp", None),
    )
    return jax.shard_map(local, mesh=mesh, in_specs=in_specs, out_specs=out_specs, check_vma=False)
```

time: 317 us -> 276 us (0.87)
  matrix products: 38.5 us -> 3.17 us
  waiting for transfers between devices: 164 us -> 139 us
  Pallas kernels: 49.7 us -> 71 us
  local copies, waits for them, and re-layouts: 23.5 us -> 20.1 us
    dot_general x8 -> x1, matrix products: 38.5 us -> 3.17 us  [dot(): lax.dot_general(left, right, (dims, ((), ())), preferred_element_type=F32)]
    pallas_call x6 -> x10, Pallas kernels: 49.7 us -> 71 us  [call(): pl.pallas_call(kernel, grid=grid, in_specs=in_specs, out_specs=[spec for...]
    ppermute x4 -> x6, waiting for transfers between devices: 14.9 us -> 2.08 us  [swap(): return lax.ppermute(value, 'dp', [(0, 1), (1, 0)])]
    all_to_all x4, waiting for transfers between devices: 149 us -> 137 us  [exchange(): lax.all_to_all(parts, 'expert', split_axis=0, concat_axis=0, tiled=True)]
    concatenate x1 -> x0, local copies, waits for them, and re-layouts: 4.83 us -> none  [local(): rows_all = jnp.concatenate([rows_own, rows_other])]
    unnamed x50 -> x70, local copies, waits for them, and re-layouts: 18 us -> 20.1 us
  transfers between devices with their start and end apart: 8 -> 10, of which waited for: 6 -> 5; matrix products, arithmetic and copies ran while one was open for 13% -> 1% of each run, Pallas kernels for 8% -> 22%
where the time goes in v3:
time: 276 us; the launch traced here: 275 us
  waiting for transfers between devices  139 us (50%)
  Pallas kernels  71 us (26%)
  starting transfers between devices  40.8 us (15%)
  local copies, waits for them, and re-layouts  20.1 us (7%)
  matrix products  3.17 us (1%)
    all_to_all x4, waiting for transfers between devices, exchange(): lax.all_to_all(parts, 'expert', split_axis=0, concat_axis=0, tiled=True)  137 us
    pallas_call x10, Pallas kernels, call(): pl.pallas_call(kernel, grid=grid, in_specs=in_specs, out_specs=[spec for...  71 us
    all_to_all x4, starting transfers between devices, exchange(): lax.all_to_all(parts, 'expert', split_axis=0, concat_axis=0, tiled=True)  39.7 us
    unnamed x70, local copies, waits for them, and re-layouts  20.1 us
  transfers between devices with their start and end apart: 10, of which 5 were waited for; matrix products, arithmetic and copies ran while one was open for 1% of the time, Pallas kernels for 22%

profile of v3, /device:TPU:0, one launch (start us, length us, event | category | flops | bytes accessed | tf_op | source)
XLA Modules:
  0.0 275.0 jit_solution(11225266972259641019)
XLA Ops:
  0.6 0.0 copy-start
  0.6 0.9 copy.15.routing_ref
  1.5 1.2 copy-done.16
  2.7 3.4 %shard_map.110 = (s32[128,2]{1,0:T(8,128)S(1)}, bf16[512,4096]{1,0:T(8,128)(2,1)S(1)}) custom-call(s32[128,2]{1,0:T(8,128)S(1)} %copy.15.routing_ref, bf16[128,4096]{1,0:T(8,128)(2,1)S(1)} %copy-done.16), custom_call_target="tpu_custom_call" | custom-call | flops 1000 | bytes 1000 | tf_op jit(solution)/shard_map/pallas_call | solution.py:35
  6.1 0.0 copy-start.11
  6.1 0.0 copy-start.25
  6.1 2.0 copy-done.11
  8.2 11.9 %all-to-all-start = ((bf16[64,8,4096]{2,1,0:T(8,128)(2,1)}), bf16[64,8,4096]{2,1,0:T(8,128)(2,1)}, u32[]{:S(2)}, u32[]{:S(2)}) async-start(bf16[64,8,4096]{2,1,0:T(8,128)(2,1)} %bitcast.30), calls=%async_computation | async-start | bytes 8388608 | tf_op jit(solution)/shard_map/all_to_all | solution.py:29
  20.1 0.1 copy.16
  20.1 0.1 fusion
  20.2 0.1 select_reduce_fusion
  20.4 0.0 copy-done
  20.4 3.2 %multiply_convert_fusion = bf16[512,4096]{1,0:T(8,128)(2,1)} fusion(pred[512,128]{1,0:T(8,128)(4,1)S(1)} %fusion, bf16[128,4096]{1,0:T(8,128)(2,1)S(1)} %copy-done, f32[512]{0:T(512)S(1)} %select_reduce_fusion), kind=kOutput, calls=%fused_computation | convolution fusion | flops 541065216 | bytes 5310464 | tf_op jit(solution)/shard_map/dot_general | solution.py:19
  23.5 51.2 %all-to-all-done = bf16[64,8,4096]{2,1,0:T(8,128)(2,1)} async-done(((bf16[64,8,4096]{2,1,0:T(8,128)(2,1)}), bf16[64,8,4096]{2,1,0:T(8,128)(2,1)}, u32[]{:S(2)}, u32[]{:S(2)}) %all-to-all-start) | async-done | bytes 4194336 | tf_op jit(solution)/shard_map/all_to_all | solution.py:29
  74.8 0.0 collective-permute-start
  74.8 7.9 %all-to-all-start.1 = ((bf16[64,8,4096]{2,1,0:T(8,128)(2,1)}), bf16[64,8,4096]{2,1,0:T(8,128)(2,1)}, u32[]{:S(2)}, u32[]{:S(2)}) async-start(bf16[64,8,4096]{2,1,0:T(8,128)(2,1)} %bitcast.31), calls=%async_computation.1 | async-start | bytes 8388608 | tf_op jit(solution)/shard_map/all_to_all | solution.py:29
  82.7 0.0 collective-permute-done.rows_ref.refs_1_
  82.7 0.0 copy-start.7
  82.7 1.9 copy-done.7
  84.6 10.1 %shard_map.112 = (bf16[512,384]{1,0:T(8,128)(2,1)S(1)}, f32[512,384]{1,0:T(8,128)S(1)}, f32[512,384]{1,0:T(8,128)S(1)}, bf16[256,4096]{1,0:T(8,128)(2,1)S(1)}, bf16[256,4096]{1,0:T(8,128)(2,1)S(1)}) custom-call(bf16[512,4096]{1,0:T(8,128)(2,1)} %collective-permute-done.rows_ref.refs_1_, bf16[4096,384]{1,0:T(8,128)(2,1)S(1)} %bitcast.20, ...), custom_call_target="tpu_custom_call" | custom-call | flops 1000 | bytes 1000 | tf_op jit(solution)/shard_map/pallas_call | solution.py:35
  94.8 0.0 copy-start.21
  94.8 0.9 copy-done.21
  95.7 0.9 copy-done.23
  96.5 0.7 copy-done.27
  97.3 0.2 collective-permute-start.1
  97.5 0.3 collective-permute-start.2
  97.8 6.9 %shard_map.111 = (bf16[512,384]{1,0:T(8,128)(2,1)S(1)}, f32[512,384]{1,0:T(8,128)S(1)}, f32[512,384]{1,0:T(8,128)S(1)}) custom-call(bf16[512,4096]{1,0:T(8,128)(2,1)} %bitcast.1.rows_ref.refs_0_, bf16[4096,384]{1,0:T(8,128)(2,1)S(1)} %bitcast.21, bf16[4096,384]{1,0:T(8,128)(2,1)S(1)} %bitcast.25), custom_call_target="tpu_custom_call" | custom-call | flops 1000 | bytes 1000 | tf_op jit(solution)/shard_map/pallas_call | solution.py:35
  104.7 0.0 copy-start.17
  104.7 0.9 copy-done.17
  105.6 0.9 copy-done.19
  106.5 0.0 collective-permute-done.1.refs_0_
  106.5 0.0 collective-permute-done.2.refs_1_
  106.5 0.0 copy-done.2
  106.5 2.3 shard_map.113
  108.8 2.0 copy-done.9
  110.9 27.2 %all-to-all-done.1 = bf16[64,8,4096]{2,1,0:T(8,128)(2,1)} async-done(((bf16[64,8,4096]{2,1,0:T(8,128)(2,1)}), bf16[64,8,4096]{2,1,0:T(8,128)(2,1)}, u32[]{:S(2)}, u32[]{:S(2)}) %all-to-all-start.1) | async-done | bytes 4194336 | tf_op jit(solution)/shard_map/all_to_all | solution.py:29
  138.0 0.0 collective-permute-start.3
  138.0 10.0 %all-to-all-start.2 = ((bf16[64,8,4096]{2,1,0:T(8,128)(2,1)}), bf16[64,8,4096]{2,1,0:T(8,128)(2,1)}, u32[]{:S(2)}, u32[]{:S(2)}) async-start(bf16[64,8,4096]{2,1,0:T(8,128)(2,1)} %bitcast.28), calls=%async_computation.2 | async-start | bytes 8388608 | tf_op jit(solution)/shard_map/all_to_all | solution.py:29
  148.0 0.0 collective-permute-done.3.grads_ref.refs_3_
  148.1 0.0 copy-start.8
  148.1 1.9 copy-done.8
  149.9 1.1 copy-done.22
  151.1 1.1 copy-done.24
  152.2 10.0 %shard_map.115 = (bf16[512,384]{1,0:T(8,128)(2,1)S(1)}, bf16[512,384]{1,0:T(8,128)(2,1)S(1)}, bf16[256,4096]{1,0:T(8,128)(2,1)S(1)}, bf16[256,4096]{1,0:T(8,128)(2,1)S(1)}) custom-call(bf16[512,4096]{1,0:T(8,128)(2,1)} %collective-permute-done.3.grads_ref.refs_3_, f32[512,384]{1,0:T(8,128)S(1)} %copy-done.22, f32[512,384]{1,0:T(8,128)S(1)} %copy-done.24, ...), custom_call_target="tpu_custom_call" | custom-call | flops 1000 | bytes 1000 | tf_op jit(solution)/shard_map/pallas_call | solution.py:35
  162.2 0.0 copy-start.29
  162.2 0.0 copy-start.31
  162.3 0.3 collective-permute-start.4
  162.5 0.3 collective-permute-start.5
  162.9 4.5 %shard_map.114 = (bf16[512,384]{1,0:T(8,128)(2,1)S(1)}, bf16[512,384]{1,0:T(8,128)(2,1)S(1)}) custom-call(bf16[512,4096]{1,0:T(8,128)(2,1)} %bitcast.3.grads_ref.refs_2_, f32[512,384]{1,0:T(8,128)S(1)} %copy-done.18, f32[512,384]{1,0:T(8,128)S(1)} %copy-done.20, bf16[384,4096]{1,0:T(8,128)(2,1)S(1)} %bitcast.19), custom_call_target="tpu_custom_call" | custom-call | flops 1000 | bytes 1000 | tf_op jit(solution)/shard_map/pallas_call | solution.py:35
  167.4 0.0 collective-permute-done.4.refs_0_
  167.4 2.1 collective-permute-done.5.refs_1_
  169.5 4.5 %shard_map.117 = bf16[512,4096]{1,0:T(8,128)(2,1)S(1)} custom-call(bf16[512,384]{1,0:T(8,128)(2,1)S(1)} %get-tuple-element.46.refs_6_.gate_grad_ref, bf16[512,384]{1,0:T(8,128)(2,1)S(1)} %get-tuple-element.50.refs_8_.up_grad_ref, bf16[4096,384]{1,0:T(8,128)(2,1)S(1)} %bitcast.23, bf16[4096,384]{1,0:T(8,128)(2,1)S(1)} %bitcast.27, ...), custom_call_target="tpu_custom_call" | custom-call | flops 1000 | bytes 1000 | tf_op jit(solution)/shard_map/pallas_call | solution.py:35
  174.1 2.0 copy-done.10
  176.0 0.7 copy-done.12
  176.8 0.7 copy-done.14
  177.5 25.6 %all-to-all-done.2 = bf16[64,8,4096]{2,1,0:T(8,128)(2,1)} async-done(((bf16[64,8,4096]{2,1,0:T(8,128)(2,1)}), bf16[64,8,4096]{2,1,0:T(8,128)(2,1)}, u32[]{:S(2)}, u32[]{:S(2)}) %all-to-all-start.2) | async-done | bytes 4194336 | tf_op jit(solution)/shard_map/all_to_all | solution.py:29
  203.1 0.0 copy-start.32
  203.1 9.9 %all-to-all-start.3 = ((bf16[64,8,4096]{2,1,0:T(8,128)(2,1)}), bf16[64,8,4096]{2,1,0:T(8,128)(2,1)}, u32[]{:S(2)}, u32[]{:S(2)}) async-start(bf16[64,8,4096]{2,1,0:T(8,128)(2,1)} %bitcast.29), calls=%async_computation.3 | async-start | bytes 8388608 | tf_op jit(solution)/shard_map/all_to_all | solution.py:29
  213.0 0.1 copy.17.weight_ref
  213.2 0.0 copy-start.1
  213.2 15.3 %shard_map.116 = (bf16[4096,384]{1,0:T(8,128)(2,1)}, bf16[4096,384]{1,0:T(8,128)(2,1)}, bf16[384,4096]{1,0:T(8,128)(2,1)}) custom-call(bf16[512,4096]{1,0:T(8,128)(2,1)} %bitcast.1.rows_ref.refs_0_, bf16[512,4096]{1,0:T(8,128)(2,1)} %collective-permute-done.rows_ref.refs_1_, bf16[512,4096]{1,0:T(8,128)(2,1)} %bitcast.3.grads_ref.refs_2_, ...), custom_call_target="tpu_custom_call" | custom-call | flops 1000 | bytes 1000 | tf_op jit(solution)/shard_map/pallas_call | solution.py:35
  228.5 7.1 %shard_map.118 = bf16[128,4096]{1,0:T(8,128)(2,1)} custom-call(s32[128,2]{1,0:T(8,128)S(1)} %copy-done.26, f32[128,2]{1,0:T(8,128)S(1)} %copy.17.weight_ref, bf16[512,4096]{1,0:T(8,128)(2,1)} %bitcast.8.rows_ref), custom_call_target="tpu_custom_call" | custom-call | flops 1000 | bytes 1000 | tf_op jit(solution)/shard_map/pallas_call | solution.py:35
  235.6 32.6 %all-to-all-done.3 = bf16[64,8,4096]{2,1,0:T(8,128)(2,1)} async-done(((bf16[64,8,4096]{2,1,0:T(8,128)(2,1)}), bf16[64,8,4096]{2,1,0:T(8,128)(2,1)}, u32[]{:S(2)}, u32[]{:S(2)}) %all-to-all-start.3) | async-done | bytes 4194336 | tf_op jit(solution)/shard_map/all_to_all | solution.py:29
  268.2 6.8 %shard_map.119 = bf16[128,4096]{1,0:T(8,128)(2,1)} custom-call(s32[128,2]{1,0:T(8,128)S(1)} %copy-done.26, bf16[512,4096]{1,0:T(8,128)(2,1)} %bitcast.10.rows_ref), custom_call_target="tpu_custom_call" | custom-call | flops 1000 | bytes 1000 | tf_op jit(solution)/shard_map/pallas_call | solution.py:35
  (40 shorter events, 0.1 us)
Async XLA Ops:
  0.6 19.7 %copy-start = (bf16[128,4096]{1,0:T(8,128)(2,1)S(1)}, bf16[128,4096]{1,0:T(8,128)(2,1)}, u32[]{:S(2)}) copy-start(bf16[128,4096]{1,0:T(8,128)(2,1)} %param.8) | copy-start | bytes 3145732
  1.5 1.2 copy-start.16
  6.1 2.0 copy-start.11
  6.1 13.9 %copy-start.25 = (s32[128,2]{1,0:T(8,128)}, s32[128,2]{1,0:T(8,128)S(1)}, u32[]{:S(2)}) copy-start(s32[128,2]{1,0:T(8,128)S(1)} %get-tuple-element.36.position_ref) | copy-start | bytes 3076
  8.1 12.1 %copy-start.33 = (f32[128,2]{0,1:T(2,128)S(1)}, f32[128,2]{0,1:T(2,128)}, u32[]{:S(2)}) copy-start(f32[128,2]{0,1:T(2,128)} %param.10) | copy-start | bytes 3076
  8.2 66.6 %all-to-all-start = ((bf16[64,8,4096]{2,1,0:T(8,128)(2,1)}), bf16[64,8,4096]{2,1,0:T(8,128)(2,1)}, u32[]{:S(2)}, u32[]{:S(2)}) async-start(bf16[64,8,4096]{2,1,0:T(8,128)(2,1)} %bitcast.30), calls=%async_computation | async-start | bytes 8388608 | tf_op jit(solution)/shard_map/all_to_all | solution.py:29
  74.8 8.0 %collective-permute-start = (bf16[512,4096]{1,0:T(8,128)(2,1)}, bf16[512,4096]{1,0:T(8,128)(2,1)}, u32[]{:S(2)}, u32[]{:S(2)}) collective-permute-start(bf16[512,4096]{1,0:T(8,128)(2,1)} %bitcast.1.rows_ref.refs_0_), channel_id=1, source_target_pairs={{0,64},{64,0},{1,65},{65,1},{2,66},{66,2},{3,67},{67,3},{4,68},{68... | collective-permute-start | bytes 12582920 | tf_op jit(solution)/shard_map/ppermute | solution.py:23
  74.8 8.0 %copy-start.4 = (bf16[1,4096,384]{2,1,0:T(8,128)(2,1)S(1)}, bf16[1,4096,384]{2,1,0:T(8,128)(2,1)}, u32[]{:S(2)}) copy-start(bf16[1,4096,384]{2,1,0:T(8,128)(2,1)} %param.11) | copy-start | bytes 9437188
  74.8 63.3 %all-to-all-start.1 = ((bf16[64,8,4096]{2,1,0:T(8,128)(2,1)}), bf16[64,8,4096]{2,1,0:T(8,128)(2,1)}, u32[]{:S(2)}, u32[]{:S(2)}) async-start(bf16[64,8,4096]{2,1,0:T(8,128)(2,1)} %bitcast.31), calls=%async_computation.1 | async-start | bytes 8388608 | tf_op jit(solution)/shard_map/all_to_all | solution.py:29
  82.7 1.9 copy-start.7
  84.6 13.2 %copy-start.5 = (bf16[1,4096,384]{2,1,0:T(8,128)(2,1)S(1)}, bf16[1,4096,384]{2,1,0:T(8,128)(2,1)}, u32[]{:S(2)}) copy-start(bf16[1,4096,384]{2,1,0:T(8,128)(2,1)} %param.11) | copy-start | bytes 9437188
  94.8 0.9 copy-start.21
  95.7 0.9 copy-start.23
  96.5 0.7 copy-start.27
  97.3 9.2 %collective-permute-start.1 = (bf16[256,4096]{1,0:T(8,128)(2,1)S(1)}, bf16[256,4096]{1,0:T(8,128)(2,1)S(1)}, u32[]{:S(2)}, u32[]{:S(2)}) collective-permute-start(bf16[256,4096]{1,0:T(8,128)(2,1)S(1)} %get-tuple-element.40), channel_id=1, source_target_pairs={{0,64},{64,0},{1,65},{65,1},{2,66},{66,2},{3,67},{67,3},{4,68},{68... | collective-permute-start | bytes 6291464 | tf_op jit(solution)/shard_map/ppermute | solution.py:23
  97.5 9.0 %copy-start.2 = (bf16[1,384,4096]{2,1,0:T(8,128)(2,1)S(1)}, bf16[1,384,4096]{2,1,0:T(8,128)(2,1)}, u32[]{:S(2)}) copy-start(bf16[1,384,4096]{2,1,0:T(8,128)(2,1)} %param.13) | copy-start | bytes 9437188
  97.5 9.0 %collective-permute-start.2 = (bf16[256,4096]{1,0:T(8,128)(2,1)S(1)}, bf16[256,4096]{1,0:T(8,128)(2,1)S(1)}, u32[]{:S(2)}, u32[]{:S(2)}) collective-permute-start(bf16[256,4096]{1,0:T(8,128)(2,1)S(1)} %get-tuple-element.41), channel_id=1, source_target_pairs={{0,64},{64,0},{1,65},{65,1},{2,66},{66,2},{3,67},{67,3},{4,68},{68... | collective-permute-start | bytes 6291464 | tf_op jit(solution)/shard_map/ppermute | solution.py:23
  104.7 0.9 copy-start.17
  105.6 0.9 copy-start.19
  108.8 2.0 copy-start.9
  138.0 10.0 %collective-permute-start.3 = (bf16[512,4096]{1,0:T(8,128)(2,1)}, bf16[512,4096]{1,0:T(8,128)(2,1)}, u32[]{:S(2)}, u32[]{:S(2)}) collective-permute-start(bf16[512,4096]{1,0:T(8,128)(2,1)} %bitcast.3.grads_ref.refs_2_), channel_id=1, source_target_pairs={{0,64},{64,0},{1,65},{65,1},{2,66},{66,2},{3,67},{67,3},{4,68},{68... | collective-permute-start | bytes 12582920 | tf_op jit(solution)/shard_map/ppermute | solution.py:23
  138.0 10.0 %copy-start.6 = (bf16[1,4096,384]{2,1,0:T(8,128)(2,1)S(1)}, bf16[1,4096,384]{2,1,0:T(8,128)(2,1)}, u32[]{:S(2)}) copy-start(bf16[1,4096,384]{2,1,0:T(8,128)(2,1)} %param.11) | copy-start | bytes 9437188
  138.0 65.1 %all-to-all-start.2 = ((bf16[64,8,4096]{2,1,0:T(8,128)(2,1)}), bf16[64,8,4096]{2,1,0:T(8,128)(2,1)}, u32[]{:S(2)}, u32[]{:S(2)}) async-start(bf16[64,8,4096]{2,1,0:T(8,128)(2,1)} %bitcast.28), calls=%async_computation.2 | async-start | bytes 8388608 | tf_op jit(solution)/shard_map/all_to_all | solution.py:29
  148.1 1.9 copy-start.8
  149.9 1.1 copy-start.22
  151.1 1.1 copy-start.24
  152.2 10.6 %copy-start.3 = (bf16[1,384,4096]{2,1,0:T(8,128)(2,1)S(1)}, bf16[1,384,4096]{2,1,0:T(8,128)(2,1)}, u32[]{:S(2)}) copy-start(bf16[1,384,4096]{2,1,0:T(8,128)(2,1)} %param.13) | copy-start | bytes 9437188
  152.2 10.6 %copy-start.18 = (f32[512,384]{1,0:T(8,128)S(1)}, f32[512,384]{1,0:T(8,128)}, u32[]{:S(2)}) copy-start(f32[512,384]{1,0:T(8,128)} %copy-done.17) | copy-start | bytes 2359300
  152.2 10.6 %copy-start.20 = (f32[512,384]{1,0:T(8,128)S(1)}, f32[512,384]{1,0:T(8,128)}, u32[]{:S(2)}) copy-start(f32[512,384]{1,0:T(8,128)} %copy-done.19) | copy-start | bytes 2359300
  162.2 5.2 %copy-start.29 = (bf16[512,384]{1,0:T(8,128)(2,1)}, bf16[512,384]{1,0:T(8,128)(2,1)S(1)}, u32[]{:S(2)}) copy-start(bf16[512,384]{1,0:T(8,128)(2,1)S(1)} %get-tuple-element.49.refs_7_) | copy-start | bytes 1179652
  162.2 5.2 %copy-start.31 = (bf16[512,384]{1,0:T(8,128)(2,1)}, bf16[512,384]{1,0:T(8,128)(2,1)S(1)}, u32[]{:S(2)}) copy-start(bf16[512,384]{1,0:T(8,128)(2,1)S(1)} %get-tuple-element.51.refs_9_) | copy-start | bytes 1179652
  162.3 5.2 %collective-permute-start.4 = (bf16[256,4096]{1,0:T(8,128)(2,1)S(1)}, bf16[256,4096]{1,0:T(8,128)(2,1)S(1)}, u32[]{:S(2)}, u32[]{:S(2)}) collective-permute-start(bf16[256,4096]{1,0:T(8,128)(2,1)S(1)} %get-tuple-element.56), channel_id=1, source_target_pairs={{0,64},{64,0},{1,65},{65,1},{2,66},{66,2},{3,67},{67,3},{4,68},{68... | collective-permute-start | bytes 6291464 | tf_op jit(solution)/shard_map/ppermute | solution.py:23
  162.5 7.0 %collective-permute-start.5 = (bf16[256,4096]{1,0:T(8,128)(2,1)S(1)}, bf16[256,4096]{1,0:T(8,128)(2,1)S(1)}, u32[]{:S(2)}, u32[]{:S(2)}) collective-permute-start(bf16[256,4096]{1,0:T(8,128)(2,1)S(1)} %get-tuple-element.57), channel_id=1, source_target_pairs={{0,64},{64,0},{1,65},{65,1},{2,66},{66,2},{3,67},{67,3},{4,68},{68... | collective-permute-start | bytes 6291464 | tf_op jit(solution)/shard_map/ppermute | solution.py:23
  174.0 2.0 copy-start.10
  176.0 0.7 copy-start.12
  176.8 0.7 copy-start.14
  203.1 10.0 %copy-start.13 = (bf16[512,384]{1,0:T(8,128)(2,1)S(1)}, bf16[512,384]{1,0:T(8,128)(2,1)}, u32[]{:S(2)}) copy-start(bf16[512,384]{1,0:T(8,128)(2,1)} %copy-done.12) | copy-start | bytes 1179652
  203.1 10.0 %copy-start.15 = (bf16[512,384]{1,0:T(8,128)(2,1)S(1)}, bf16[512,384]{1,0:T(8,128)(2,1)}, u32[]{:S(2)}) copy-start(bf16[512,384]{1,0:T(8,128)(2,1)} %copy-done.14) | copy-start | bytes 1179652
  203.1 10.0 %copy-start.28 = (bf16[512,384]{1,0:T(8,128)(2,1)S(1)}, bf16[512,384]{1,0:T(8,128)(2,1)}, u32[]{:S(2)}) copy-start(bf16[512,384]{1,0:T(8,128)(2,1)} %copy-done.27) | copy-start | bytes 1179652
  203.1 10.1 %copy-start.30 = (bf16[512,384]{1,0:T(8,128)(2,1)S(1)}, bf16[512,384]{1,0:T(8,128)(2,1)}, u32[]{:S(2)}) copy-start(bf16[512,384]{1,0:T(8,128)(2,1)} %copy-done.29) | copy-start | bytes 1179652
  203.1 10.1 %copy-start.32 = (bf16[512,384]{1,0:T(8,128)(2,1)S(1)}, bf16[512,384]{1,0:T(8,128)(2,1)}, u32[]{:S(2)}) copy-start(bf16[512,384]{1,0:T(8,128)(2,1)} %copy-done.31) | copy-start | bytes 1179652
  203.1 65.1 %all-to-all-start.3 = ((bf16[64,8,4096]{2,1,0:T(8,128)(2,1)}), bf16[64,8,4096]{2,1,0:T(8,128)(2,1)}, u32[]{:S(2)}, u32[]{:S(2)}) async-start(bf16[64,8,4096]{2,1,0:T(8,128)(2,1)} %bitcast.29), calls=%async_computation.3 | async-start | bytes 8388608 | tf_op jit(solution)/shard_map/all_to_all | solution.py:29
  213.2 15.3 %copy-start.26 = (s32[128,2]{1,0:T(8,128)S(1)}, s32[128,2]{1,0:T(8,128)}, u32[]{:S(2)}) copy-start(s32[128,2]{1,0:T(8,128)} %copy-done.25) | copy-start | bytes 3076
  213.2 61.8 %copy-start.1 = (bf16[128,4096]{1,0:T(8,128)(2,1)S(1)}, bf16[128,4096]{1,0:T(8,128)(2,1)}, u32[]{:S(2)}) copy-start(bf16[128,4096]{1,0:T(8,128)(2,1)} %param.8) | copy-start | bytes 3145732

commit v4 on v3

--- a/solution.py
+++ b/solution.py
@@ -9,6 +9,7 @@
 
 HOT = 4
 COLUMNS = 512
+BROAD = 1024
 PARTS = 2
 BF16 = jnp.bfloat16
 F32 = jnp.float32
@@ -30,14 +31,14 @@
     return moved.reshape(rows, features)
 
 
-def call(kernel, args, outs, limit, grid=(), scratch=()):
+def call(kernel, args, outs, limit, grid=(), scratch=(), pinned=False):
     in_specs = [spec for _, spec in args]
     return pl.pallas_call(
         kernel,
         grid=grid,
         in_specs=in_specs,
         out_specs=[spec for _, _, spec in outs],
-        out_shape=[jax.ShapeDtypeStruct(shape, kind) for shape, kind, _ in outs],
+        out_shape=[(pltpu.HBM if pinned else jax.ShapeDtypeStruct)(shape, kind) for shape, kind, _ in outs],
         scratch_shapes=scratch,
         compiler_params=pltpu.CompilerParams(vmem_limit_bytes=limit * MIB),
         cost_estimate=pl.CostEstimate(flops=1000, bytes_accessed=1000, transcendentals=0),
@@ -52,16 +53,16 @@
     return arg, pl.BlockSpec(arg.shape, lambda i: (0, 0))
 
 
-def across(arg):
-    return arg, pl.BlockSpec((arg.shape[0], COLUMNS), lambda i: (0, i))
+def across(arg, columns):
+    return arg, pl.BlockSpec((arg.shape[0], columns), lambda i: (0, i))
 
 
 def out_whole(shape, kind):
     return shape, kind, pl.BlockSpec(memory_space=pltpu.VMEM)
 
 
-def by_column(rows, columns, kind):
-    return (rows, columns), kind, pl.BlockSpec((rows, COLUMNS), lambda i: (0, i))
+def by_column(rows, columns, kind, wide):
+    return (rows, columns), kind, pl.BlockSpec((rows, wide), lambda i: (0, i))
 
 
 def joined(refs):
@@ -88,32 +89,34 @@
 
 
 def places(routing_ref, position_ref, experts, capacity):
-    tok_rows, top_count = routing_ref.shape
-    expert_ids = lax.broadcasted_iota(jnp.int32, (tok_rows, experts), 1)
-    named = [routing_ref[:, column : column + 1] == expert_ids for column in range(top_count)]
+    top_count, tok_rows = routing_ref.shape
+    expert_ids = lax.broadcasted_iota(jnp.int32, (experts, tok_rows), 0)
+    named = [routing_ref[column : column + 1] == expert_ids for column in range(top_count)]
     counts = sum(hit.astype(F32) for hit in named)
-    earlier = lax.broadcasted_iota(jnp.int32, (tok_rows, tok_rows), 1) < lax.broadcasted_iota(
-        jnp.int32, (tok_rows, tok_rows), 0
-    )
-    before = dot(earlier.astype(F32).astype(BF16), counts.astype(BF16), ((1,), (0,)))
+    earlier = lax.broadcasted_iota(jnp.int32, (tok_rows, tok_rows), 0) < lax.broadcasted_iota(
+        jnp.int32, (tok_rows, tok_rows), 1
+    )
+    before = dot(counts.astype(BF16), earlier.astype(F32).astype(BF16), ((1,), (0,)))
     for column, hit in enumerate(named):
-        slot = jnp.sum(jnp.where(hit, before, 0.0), axis=1, keepdims=True).astype(jnp.int32)
-        position_ref[:, column : column + 1] = routing_ref[:, column : column + 1] * capacity + slot
+        slot = jnp.sum(jnp.where(hit, before, 0.0), axis=0, keepdims=True).astype(jnp.int32)
+        position_ref[column : column + 1] = routing_ref[column : column + 1] * capacity + slot
+
+
+def dispatch_kernel(routing_ref, tokens_ref, position_ref, out_ref, pick_ref, *, experts, capacity):
+    @pl.when(pl.program_id(0) == 0)
+    def _():
+        places(routing_ref, position_ref, experts, capacity)
+        slots = lax.broadcasted_iota(jnp.int32, pick_ref.shape, 0)
+        hits = [position_ref[column : column + 1] == slots for column in range(position_ref.shape[0])]
+        pick_ref[...] = sum(hit.astype(F32) for hit in hits).astype(BF16)
+
+    out_ref[...] = dot(pick_ref[...], tokens_ref[...], ((1,), (0,))).astype(BF16)
 
 
 def pick_matrix(position_ref, local_rows):
     tok_rows, top_count = position_ref.shape
     slots = lax.broadcasted_iota(jnp.int32, (tok_rows, local_rows), 1)
     return sum((position_ref[:, column : column + 1] == slots).astype(F32) for column in range(top_count)).astype(BF16)
-
-
-def dispatch_kernel(routing_ref, tokens_ref, position_ref, out_ref, pick_ref, *, experts, capacity):
-    @pl.when(pl.program_id(0) == 0)
-    def _():
-        places(routing_ref, position_ref, experts, capacity)
-        pick_ref[...] = pick_matrix(position_ref, pick_ref.shape[1])
-
-    out_ref[...] = dot(pick_ref[...], tokens_ref[...], ((0,), (0,))).astype(BF16)
 
 
 def token_grad_kernel(position_ref, rows_ref, out_ref, pick_ref):
@@ -196,7 +199,7 @@
     args = [(value, pl.BlockSpec((value.shape[0], COLUMNS), lambda i: (0, i))) for value in wide]
     args += [fixed(value) for value in kept]
     tall = ((features, width), BF16, pl.BlockSpec((COLUMNS, width), lambda i: (i, 0)))
-    return call(weight_kernel, args, [tall, tall, by_column(width, features, BF16)], 48, grid=(features // COLUMNS,))
+    return call(weight_kernel, args, [tall, tall, by_column(width, features, BF16, COLUMNS)], 48, grid=(features // COLUMNS,))
 
 
 def local(tokens, cotangent, routing, combine_weights, w_gate, w_up, w_down):
@@ -210,17 +213,20 @@
     local_rows = experts * capacity
     gate_matrix, up_matrix, down_matrix = w_gate[0], w_up[0], w_down[0]
     width = gate_matrix.shape[1]
-    grid = (features // COLUMNS,)
+    broad_grid = (features // BROAD,)
     pick_scratch = [pltpu.VMEM((tok_rows, local_rows), BF16)]
 
+    place_shape = (top_count, tok_rows)
     position, send_rows = call(
         functools.partial(dispatch_kernel, experts=experts, capacity=capacity),
-        [fixed(routing), across(tokens)],
-        [(routing.shape, jnp.int32, pl.BlockSpec(routing.shape, lambda i: (0, 0))), by_column(local_rows, features, BF16)],
+        [fixed(routing.T), across(tokens, BROAD)],
+        [(place_shape, jnp.int32, pl.BlockSpec(place_shape, lambda i: (0, 0))), by_column(local_rows, features, BF16, BROAD)],
         24,
-        grid=grid,
-        scratch=pick_scratch,
-    )
+        grid=broad_grid,
+        scratch=[pltpu.VMEM((local_rows, tok_rows), BF16)],
+        pinned=True,
+    )
+    position = position.T
     rows_own = exchange(send_rows, experts)
     targets = jnp.arange(local_rows, dtype=jnp.int32)
     selected = position[None, :, :] == targets[:, None, None]
@@ -264,18 +270,18 @@
     )
     (combined,) = call(
         combine_kernel,
-        [fixed(position), fixed(combine_weights), across(out_back)],
-        [by_column(tok_rows, features, BF16)],
+        [fixed(position), fixed(combine_weights), across(out_back, BROAD)],
+        [by_column(tok_rows, features, BF16, BROAD)],
         24,
-        grid=grid,
+        grid=broad_grid,
     )
     *wgrads, combined, input_back = lax.optimization_barrier((*wgrads, combined, input_back))
     (token_grad,) = call(
         token_grad_kernel,
-        [fixed(position), across(input_back)],
-        [by_column(tok_rows, features, BF16)],
+        [fixed(position), across(input_back, BROAD)],
+        [by_column(tok_rows, features, BF16, BROAD)],
         24,
-        grid=grid,
+        grid=broad_grid,
         scratch=pick_scratch,
     )
     return combined, token_grad, wgrads[0][None], wgrads[1][None], wgrads[2][None]

time: 276 us -> 272 us (0.986)
  Pallas kernels: 71 us -> 67.2 us
    pallas_call x10, Pallas kernels: 71 us -> 67.2 us  [call(): pl.pallas_call(kernel, grid=grid, in_specs=in_specs, out_specs=[spec for...]
    unnamed x70 -> x71, local copies, waits for them, and re-layouts: 20.1 us -> 17.9 us
where the time goes in v4:
time: 272 us; the launch traced here: 271 us
  waiting for transfers between devices  141 us (52%)
  Pallas kernels  67.2 us (25%)
  starting transfers between devices  40.6 us (15%)
  local copies, waits for them, and re-layouts  18.1 us (7%)
  matrix products  3.16 us (1%)
    all_to_all x4, waiting for transfers between devices, exchange(): lax.all_to_all(parts, 'expert', split_axis=0, concat_axis=0, tiled=True)  139 us
    pallas_call x10, Pallas kernels, call(): pl.pallas_call(kernel, grid=grid, in_specs=in_specs, out_specs=[spec for...  67.2 us
    all_to_all x4, starting transfers between devices, exchange(): lax.all_to_all(parts, 'expert', split_axis=0, concat_axis=0, tiled=True)  39.5 us
    unnamed x71, local copies, waits for them, and re-layouts  17.9 us
  transfers between devices with their start and end apart: 10, of which 5 were waited for; matrix products, arithmetic and copies ran while one was open for 1% of the time, Pallas kernels for 22%

profile of v4, /device:TPU:0, one launch (start us, length us, event | category | flops | bytes accessed | tf_op | source)
XLA Modules:
  0.0 270.9 jit_solution(14624551712028461833)
XLA Ops:
  0.6 0.0 copy-start
  0.6 0.0 copy-start.17
  0.7 1.3 copy-done.17
  2.0 0.7 copy-done.32
  2.6 3.8 %shard_map.110 = (s32[2,128]{1,0:T(2,128)}, bf16[512,4096]{1,0:T(8,128)(2,1)}) custom-call(s32[2,128]{1,0:T(2,128)S(1)} %bitcast.35, bf16[128,4096]{1,0:T(8,128)(2,1)S(1)} %copy-done.17), custom_call_target="tpu_custom_call" | custom-call | flops 1000 | bytes 1000 | tf_op jit(solution)/shard_map/pallas_call | solution.py:36
  6.4 11.9 %all-to-all-start = ((bf16[64,8,4096]{2,1,0:T(8,128)(2,1)}), bf16[64,8,4096]{2,1,0:T(8,128)(2,1)}, u32[]{:S(2)}, u32[]{:S(2)}) async-start(bf16[64,8,4096]{2,1,0:T(8,128)(2,1)} %bitcast.37), calls=%async_computation | async-start | bytes 8388608 | tf_op jit(solution)/shard_map/all_to_all | solution.py:30
  18.3 0.1 copy.15
  18.5 0.1 copy.16
  18.5 0.1 fusion
  18.6 0.1 select_reduce_fusion
  18.8 3.2 %multiply_convert_fusion = bf16[512,4096]{1,0:T(8,128)(2,1)} fusion(pred[512,128]{1,0:T(8,128)(4,1)S(1)} %fusion, bf16[128,4096]{1,0:T(8,128)(2,1)S(1)} %copy-done, f32[512]{0:T(512)S(1)} %select_reduce_fusion), kind=kOutput, calls=%fused_computation | convolution fusion | flops 541065216 | bytes 5310464 | tf_op jit(solution)/shard_map/dot_general | solution.py:20
  21.9 51.1 %all-to-all-done = bf16[64,8,4096]{2,1,0:T(8,128)(2,1)} async-done(((bf16[64,8,4096]{2,1,0:T(8,128)(2,1)}), bf16[64,8,4096]{2,1,0:T(8,128)(2,1)}, u32[]{:S(2)}, u32[]{:S(2)}) %all-to-all-start) | async-done | bytes 4194336 | tf_op jit(solution)/shard_map/all_to_all | solution.py:30
  73.0 0.0 collective-permute-start
  73.0 8.0 %all-to-all-start.1 = ((bf16[64,8,4096]{2,1,0:T(8,128)(2,1)}), bf16[64,8,4096]{2,1,0:T(8,128)(2,1)}, u32[]{:S(2)}, u32[]{:S(2)}) async-start(bf16[64,8,4096]{2,1,0:T(8,128)(2,1)} %bitcast.36), calls=%async_computation.1 | async-start | bytes 8388608 | tf_op jit(solution)/shard_map/all_to_all | solution.py:30
  81.0 0.0 collective-permute-done.rows_ref.refs_1_
  81.0 0.0 copy-done.4
  81.0 0.0 copy-start.7
  81.0 1.9 copy-done.7
  82.9 10.1 %shard_map.112 = (bf16[512,384]{1,0:T(8,128)(2,1)S(1)}, f32[512,384]{1,0:T(8,128)S(1)}, f32[512,384]{1,0:T(8,128)S(1)}, bf16[256,4096]{1,0:T(8,128)(2,1)S(1)}, bf16[256,4096]{1,0:T(8,128)(2,1)S(1)}) custom-call(bf16[512,4096]{1,0:T(8,128)(2,1)} %collective-permute-done.rows_ref.refs_1_, bf16[4096,384]{1,0:T(8,128)(2,1)S(1)} %bitcast.22, ...), custom_call_target="tpu_custom_call" | custom-call | flops 1000 | bytes 1000 | tf_op jit(solution)/shard_map/pallas_call | solution.py:36
  93.1 0.0 copy-start.22
  93.1 0.9 copy-done.22
  94.0 0.9 copy-done.24
  94.8 0.7 copy-done.26
  95.6 0.2 collective-permute-start.1
  95.8 0.3 collective-permute-start.2
  96.1 6.9 %shard_map.111 = (bf16[512,384]{1,0:T(8,128)(2,1)S(1)}, f32[512,384]{1,0:T(8,128)S(1)}, f32[512,384]{1,0:T(8,128)S(1)}) custom-call(bf16[512,4096]{1,0:T(8,128)(2,1)} %bitcast.2.rows_ref.refs_0_, bf16[4096,384]{1,0:T(8,128)(2,1)S(1)} %bitcast.23, bf16[4096,384]{1,0:T(8,128)(2,1)S(1)} %bitcast.27), custom_call_target="tpu_custom_call" | custom-call | flops 1000 | bytes 1000 | tf_op jit(solution)/shard_map/pallas_call | solution.py:36
  103.0 0.0 copy-start.18
  103.0 0.9 copy-done.18
  103.9 0.9 copy-done.20
  104.8 0.0 collective-permute-done.1.refs_0_
  104.8 0.0 collective-permute-done.2.refs_1_
  104.8 2.3 shard_map.113
  107.1 2.0 copy-done.9
  109.1 27.1 %all-to-all-done.1 = bf16[64,8,4096]{2,1,0:T(8,128)(2,1)} async-done(((bf16[64,8,4096]{2,1,0:T(8,128)(2,1)}), bf16[64,8,4096]{2,1,0:T(8,128)(2,1)}, u32[]{:S(2)}, u32[]{:S(2)}) %all-to-all-start.1) | async-done | bytes 4194336 | tf_op jit(solution)/shard_map/all_to_all | solution.py:30
  136.3 0.0 collective-permute-start.3
  136.3 9.7 %all-to-all-start.2 = ((bf16[64,8,4096]{2,1,0:T(8,128)(2,1)}), bf16[64,8,4096]{2,1,0:T(8,128)(2,1)}, u32[]{:S(2)}, u32[]{:S(2)}) async-start(bf16[64,8,4096]{2,1,0:T(8,128)(2,1)} %bitcast.30), calls=%async_computation.2 | async-start | bytes 8388608 | tf_op jit(solution)/shard_map/all_to_all | solution.py:30
  146.0 0.0 collective-permute-done.3.grads_ref.refs_3_
  146.1 0.0 copy-start.8
  146.1 1.9 copy-done.8
  148.0 1.1 copy-done.23
  149.1 1.1 copy-done.25
  150.2 10.0 %shard_map.115 = (bf16[512,384]{1,0:T(8,128)(2,1)S(1)}, bf16[512,384]{1,0:T(8,128)(2,1)S(1)}, bf16[256,4096]{1,0:T(8,128)(2,1)S(1)}, bf16[256,4096]{1,0:T(8,128)(2,1)S(1)}) custom-call(bf16[512,4096]{1,0:T(8,128)(2,1)} %collective-permute-done.3.grads_ref.refs_3_, f32[512,384]{1,0:T(8,128)S(1)} %copy-done.23, f32[512,384]{1,0:T(8,128)S(1)} %copy-done.25, ...), custom_call_target="tpu_custom_call" | custom-call | flops 1000 | bytes 1000 | tf_op jit(solution)/shard_map/pallas_call | solution.py:36
  160.2 0.0 copy-start.28
  160.3 0.0 copy-start.30
  160.3 0.3 collective-permute-start.4
  160.5 0.3 collective-permute-start.5
  160.9 0.0 copy-done.3
  160.9 0.0 copy-done.21
  160.9 4.5 %shard_map.114 = (bf16[512,384]{1,0:T(8,128)(2,1)S(1)}, bf16[512,384]{1,0:T(8,128)(2,1)S(1)}) custom-call(bf16[512,4096]{1,0:T(8,128)(2,1)} %bitcast.5.grads_ref.refs_2_, f32[512,384]{1,0:T(8,128)S(1)} %copy-done.19, f32[512,384]{1,0:T(8,128)S(1)} %copy-done.21, bf16[384,4096]{1,0:T(8,128)(2,1)S(1)} %bitcast.21), custom_call_target="tpu_custom_call" | custom-call | flops 1000 | bytes 1000 | tf_op jit(solution)/shard_map/pallas_call | solution.py:36
  165.4 0.0 collective-permute-done.4.refs_0_
  165.4 2.1 collective-permute-done.5.refs_1_
  167.5 4.5 %shard_map.117 = bf16[512,4096]{1,0:T(8,128)(2,1)S(1)} custom-call(bf16[512,384]{1,0:T(8,128)(2,1)S(1)} %get-tuple-element.46.refs_6_.gate_grad_ref, bf16[512,384]{1,0:T(8,128)(2,1)S(1)} %get-tuple-element.50.refs_8_.up_grad_ref, bf16[4096,384]{1,0:T(8,128)(2,1)S(1)} %bitcast.25, bf16[4096,384]{1,0:T(8,128)(2,1)S(1)} %bitcast.29, ...), custom_call_target="tpu_custom_call" | custom-call | flops 1000 | bytes 1000 | tf_op jit(solution)/shard_map/pallas_call | solution.py:36
  172.1 2.0 copy-done.10
  174.0 0.7 copy-done.11
  174.8 0.7 copy-done.13
  175.5 25.6 %all-to-all-done.2 = bf16[64,8,4096]{2,1,0:T(8,128)(2,1)} async-done(((bf16[64,8,4096]{2,1,0:T(8,128)(2,1)}), bf16[64,8,4096]{2,1,0:T(8,128)(2,1)}, u32[]{:S(2)}, u32[]{:S(2)}) %all-to-all-start.2) | async-done | bytes 4194336 | tf_op jit(solution)/shard_map/all_to_all | solution.py:30
  201.1 0.0 copy-start.31
  201.1 9.9 %all-to-all-start.3 = ((bf16[64,8,4096]{2,1,0:T(8,128)(2,1)}), bf16[64,8,4096]{2,1,0:T(8,128)(2,1)}, u32[]{:S(2)}, u32[]{:S(2)}) async-start(bf16[64,8,4096]{2,1,0:T(8,128)(2,1)} %bitcast.31), calls=%async_computation.3 | async-start | bytes 8388608 | tf_op jit(solution)/shard_map/all_to_all | solution.py:30
  211.0 0.1 copy.17.weight_ref
  211.2 0.0 copy-start.1
  211.2 15.3 %shard_map.116 = (bf16[4096,384]{1,0:T(8,128)(2,1)}, bf16[4096,384]{1,0:T(8,128)(2,1)}, bf16[384,4096]{1,0:T(8,128)(2,1)}) custom-call(bf16[512,4096]{1,0:T(8,128)(2,1)} %bitcast.2.rows_ref.refs_0_, bf16[512,4096]{1,0:T(8,128)(2,1)} %collective-permute-done.rows_ref.refs_1_, bf16[512,4096]{1,0:T(8,128)(2,1)} %bitcast.5.grads_ref.refs_2_, ...), custom_call_target="tpu_custom_call" | custom-call | flops 1000 | bytes 1000 | tf_op jit(solution)/shard_map/pallas_call | solution.py:36
  226.5 4.9 %shard_map.118 = bf16[128,4096]{1,0:T(8,128)(2,1)} custom-call(s32[128,2]{1,0:T(8,128)S(1)} %bitcast.33, f32[128,2]{1,0:T(8,128)S(1)} %copy.17.weight_ref, bf16[512,4096]{1,0:T(8,128)(2,1)} %bitcast.10.rows_ref), custom_call_target="tpu_custom_call" | custom-call | flops 1000 | bytes 1000 | tf_op jit(solution)/shard_map/pallas_call | solution.py:36
  231.5 34.8 %all-to-all-done.3 = bf16[64,8,4096]{2,1,0:T(8,128)(2,1)} async-done(((bf16[64,8,4096]{2,1,0:T(8,128)(2,1)}), bf16[64,8,4096]{2,1,0:T(8,128)(2,1)}, u32[]{:S(2)}, u32[]{:S(2)}) %all-to-all-start.3) | async-done | bytes 4194336 | tf_op jit(solution)/shard_map/all_to_all | solution.py:30
  266.2 4.7 %shard_map.119 = bf16[128,4096]{1,0:T(8,128)(2,1)} custom-call(s32[128,2]{1,0:T(8,128)S(1)} %bitcast.34, bf16[512,4096]{1,0:T(8,128)(2,1)} %bitcast.12.rows_ref), custom_call_target="tpu_custom_call" | custom-call | flops 1000 | bytes 1000 | tf_op jit(solution)/shard_map/pallas_call | solution.py:36
  (42 shorter events, 0.1 us)
Async XLA Ops:
  0.6 18.1 %copy-start = (bf16[128,4096]{1,0:T(8,128)(2,1)S(1)}, bf16[128,4096]{1,0:T(8,128)(2,1)}, u32[]{:S(2)}) copy-start(bf16[128,4096]{1,0:T(8,128)(2,1)} %param.8) | copy-start | bytes 3145732
  0.6 1.3 copy-start.17
  2.0 0.7 copy-start.32
  6.4 11.9 %copy-start.34 = (s32[2,128]{1,0:T(2,128)S(1)}, s32[2,128]{1,0:T(2,128)}, u32[]{:S(2)}) copy-start(s32[2,128]{1,0:T(2,128)} %get-tuple-element.36) | copy-start | bytes 3076
  6.4 12.2 %copy-start.33 = (f32[128,2]{0,1:T(2,128)S(1)}, f32[128,2]{0,1:T(2,128)}, u32[]{:S(2)}) copy-start(f32[128,2]{0,1:T(2,128)} %param.10) | copy-start | bytes 3076
  6.4 66.6 %all-to-all-start = ((bf16[64,8,4096]{2,1,0:T(8,128)(2,1)}), bf16[64,8,4096]{2,1,0:T(8,128)(2,1)}, u32[]{:S(2)}, u32[]{:S(2)}) async-start(bf16[64,8,4096]{2,1,0:T(8,128)(2,1)} %bitcast.37), calls=%async_computation | async-start | bytes 8388608 | tf_op jit(solution)/shard_map/all_to_all | solution.py:30
  18.5 54.6 %copy-start.15 = (s32[2,128]{0,1:T(8,128)}, s32[2,128]{0,1:T(8,128)S(1)}, u32[]{:S(2)}) copy-start(s32[2,128]{0,1:T(8,128)S(1)} %copy.15) | copy-start | bytes 3076
  73.0 8.0 %collective-permute-start = (bf16[512,4096]{1,0:T(8,128)(2,1)}, bf16[512,4096]{1,0:T(8,128)(2,1)}, u32[]{:S(2)}, u32[]{:S(2)}) collective-permute-start(bf16[512,4096]{1,0:T(8,128)(2,1)} %bitcast.2.rows_ref.refs_0_), channel_id=1, source_target_pairs={{0,64},{64,0},{1,65},{65,1},{2,66},{66,2},{3,67},{67,3},{4,68},{68... | collective-permute-start | bytes 12582920 | tf_op jit(solution)/shard_map/ppermute | solution.py:24
  73.0 8.0 %copy-start.4 = (bf16[1,4096,384]{2,1,0:T(8,128)(2,1)S(1)}, bf16[1,4096,384]{2,1,0:T(8,128)(2,1)}, u32[]{:S(2)}) copy-start(bf16[1,4096,384]{2,1,0:T(8,128)(2,1)} %param.11) | copy-start | bytes 9437188
  73.0 63.2 %all-to-all-start.1 = ((bf16[64,8,4096]{2,1,0:T(8,128)(2,1)}), bf16[64,8,4096]{2,1,0:T(8,128)(2,1)}, u32[]{:S(2)}, u32[]{:S(2)}) async-start(bf16[64,8,4096]{2,1,0:T(8,128)(2,1)} %bitcast.36), calls=%async_computation.1 | async-start | bytes 8388608 | tf_op jit(solution)/shard_map/all_to_all | solution.py:30
  81.0 1.9 copy-start.7
  82.9 13.2 %copy-start.5 = (bf16[1,4096,384]{2,1,0:T(8,128)(2,1)S(1)}, bf16[1,4096,384]{2,1,0:T(8,128)(2,1)}, u32[]{:S(2)}) copy-start(bf16[1,4096,384]{2,1,0:T(8,128)(2,1)} %param.11) | copy-start | bytes 9437188
  93.1 0.9 copy-start.22
  94.0 0.9 copy-start.24
  94.8 0.7 copy-start.26
  95.6 9.2 %collective-permute-start.1 = (bf16[256,4096]{1,0:T(8,128)(2,1)S(1)}, bf16[256,4096]{1,0:T(8,128)(2,1)S(1)}, u32[]{:S(2)}, u32[]{:S(2)}) collective-permute-start(bf16[256,4096]{1,0:T(8,128)(2,1)S(1)} %get-tuple-element.40), channel_id=1, source_target_pairs={{0,64},{64,0},{1,65},{65,1},{2,66},{66,2},{3,67},{67,3},{4,68},{68... | collective-permute-start | bytes 6291464 | tf_op jit(solution)/shard_map/ppermute | solution.py:24
  95.8 9.0 %copy-start.2 = (bf16[1,384,4096]{2,1,0:T(8,128)(2,1)S(1)}, bf16[1,384,4096]{2,1,0:T(8,128)(2,1)}, u32[]{:S(2)}) copy-start(bf16[1,384,4096]{2,1,0:T(8,128)(2,1)} %param.13) | copy-start | bytes 9437188
  95.8 9.0 %collective-permute-start.2 = (bf16[256,4096]{1,0:T(8,128)(2,1)S(1)}, bf16[256,4096]{1,0:T(8,128)(2,1)S(1)}, u32[]{:S(2)}, u32[]{:S(2)}) collective-permute-start(bf16[256,4096]{1,0:T(8,128)(2,1)S(1)} %get-tuple-element.41), channel_id=1, source_target_pairs={{0,64},{64,0},{1,65},{65,1},{2,66},{66,2},{3,67},{67,3},{4,68},{68... | collective-permute-start | bytes 6291464 | tf_op jit(solution)/shard_map/ppermute | solution.py:24
  103.0 0.9 copy-start.18
  103.9 0.9 copy-start.20
  107.1 2.0 copy-start.9
  136.3 9.8 %collective-permute-start.3 = (bf16[512,4096]{1,0:T(8,128)(2,1)}, bf16[512,4096]{1,0:T(8,128)(2,1)}, u32[]{:S(2)}, u32[]{:S(2)}) collective-permute-start(bf16[512,4096]{1,0:T(8,128)(2,1)} %bitcast.5.grads_ref.refs_2_), channel_id=1, source_target_pairs={{0,64},{64,0},{1,65},{65,1},{2,66},{66,2},{3,67},{67,3},{4,68},{68... | collective-permute-start | bytes 12582920 | tf_op jit(solution)/shard_map/ppermute | solution.py:24
  136.3 9.8 %copy-start.6 = (bf16[1,4096,384]{2,1,0:T(8,128)(2,1)S(1)}, bf16[1,4096,384]{2,1,0:T(8,128)(2,1)}, u32[]{:S(2)}) copy-start(bf16[1,4096,384]{2,1,0:T(8,128)(2,1)} %param.11) | copy-start | bytes 9437188
  136.3 64.8 %all-to-all-start.2 = ((bf16[64,8,4096]{2,1,0:T(8,128)(2,1)}), bf16[64,8,4096]{2,1,0:T(8,128)(2,1)}, u32[]{:S(2)}, u32[]{:S(2)}) async-start(bf16[64,8,4096]{2,1,0:T(8,128)(2,1)} %bitcast.30), calls=%async_computation.2 | async-start | bytes 8388608 | tf_op jit(solution)/shard_map/all_to_all | solution.py:30
  146.1 1.9 copy-start.8
  148.0 1.1 copy-start.23
  149.1 1.1 copy-start.25
  150.2 10.6 %copy-start.3 = (bf16[1,384,4096]{2,1,0:T(8,128)(2,1)S(1)}, bf16[1,384,4096]{2,1,0:T(8,128)(2,1)}, u32[]{:S(2)}) copy-start(bf16[1,384,4096]{2,1,0:T(8,128)(2,1)} %param.13) | copy-start | bytes 9437188
  150.2 10.6 %copy-start.19 = (f32[512,384]{1,0:T(8,128)S(1)}, f32[512,384]{1,0:T(8,128)}, u32[]{:S(2)}) copy-start(f32[512,384]{1,0:T(8,128)} %copy-done.18) | copy-start | bytes 2359300
  150.2 10.6 %copy-start.21 = (f32[512,384]{1,0:T(8,128)S(1)}, f32[512,384]{1,0:T(8,128)}, u32[]{:S(2)}) copy-start(f32[512,384]{1,0:T(8,128)} %copy-done.20) | copy-start | bytes 2359300
  160.2 5.2 %copy-start.28 = (bf16[512,384]{1,0:T(8,128)(2,1)}, bf16[512,384]{1,0:T(8,128)(2,1)S(1)}, u32[]{:S(2)}) copy-start(bf16[512,384]{1,0:T(8,128)(2,1)S(1)} %get-tuple-element.49.refs_7_) | copy-start | bytes 1179652
  160.3 5.2 %copy-start.30 = (bf16[512,384]{1,0:T(8,128)(2,1)}, bf16[512,384]{1,0:T(8,128)(2,1)S(1)}, u32[]{:S(2)}) copy-start(bf16[512,384]{1,0:T(8,128)(2,1)S(1)} %get-tuple-element.51.refs_9_) | copy-start | bytes 1179652
  160.3 5.2 %collective-permute-start.4 = (bf16[256,4096]{1,0:T(8,128)(2,1)S(1)}, bf16[256,4096]{1,0:T(8,128)(2,1)S(1)}, u32[]{:S(2)}, u32[]{:S(2)}) collective-permute-start(bf16[256,4096]{1,0:T(8,128)(2,1)S(1)} %get-tuple-element.56), channel_id=1, source_target_pairs={{0,64},{64,0},{1,65},{65,1},{2,66},{66,2},{3,67},{67,3},{4,68},{68... | collective-permute-start | bytes 6291464 | tf_op jit(solution)/shard_map/ppermute | solution.py:24
  160.5 7.0 %collective-permute-start.5 = (bf16[256,4096]{1,0:T(8,128)(2,1)S(1)}, bf16[256,4096]{1,0:T(8,128)(2,1)S(1)}, u32[]{:S(2)}, u32[]{:S(2)}) collective-permute-start(bf16[256,4096]{1,0:T(8,128)(2,1)S(1)} %get-tuple-element.57), channel_id=1, source_target_pairs={{0,64},{64,0},{1,65},{65,1},{2,66},{66,2},{3,67},{67,3},{4,68},{68... | collective-permute-start | bytes 6291464 | tf_op jit(solution)/shard_map/ppermute | solution.py:24
  172.1 2.0 copy-start.10
  174.0 0.7 copy-start.11
  174.8 0.7 copy-start.13
  201.1 10.0 %copy-start.12 = (bf16[512,384]{1,0:T(8,128)(2,1)S(1)}, bf16[512,384]{1,0:T(8,128)(2,1)}, u32[]{:S(2)}) copy-start(bf16[512,384]{1,0:T(8,128)(2,1)} %copy-done.11) | copy-start | bytes 1179652
  201.1 10.0 %copy-start.14 = (bf16[512,384]{1,0:T(8,128)(2,1)S(1)}, bf16[512,384]{1,0:T(8,128)(2,1)}, u32[]{:S(2)}) copy-start(bf16[512,384]{1,0:T(8,128)(2,1)} %copy-done.13) | copy-start | bytes 1179652
  201.1 10.0 %copy-start.27 = (bf16[512,384]{1,0:T(8,128)(2,1)S(1)}, bf16[512,384]{1,0:T(8,128)(2,1)}, u32[]{:S(2)}) copy-start(bf16[512,384]{1,0:T(8,128)(2,1)} %copy-done.26) | copy-start | bytes 1179652
  201.1 10.1 %copy-start.29 = (bf16[512,384]{1,0:T(8,128)(2,1)S(1)}, bf16[512,384]{1,0:T(8,128)(2,1)}, u32[]{:S(2)}) copy-start(bf16[512,384]{1,0:T(8,128)(2,1)} %copy-done.28) | copy-start | bytes 1179652
  201.1 10.1 %copy-start.31 = (bf16[512,384]{1,0:T(8,128)(2,1)S(1)}, bf16[512,384]{1,0:T(8,128)(2,1)}, u32[]{:S(2)}) copy-start(bf16[512,384]{1,0:T(8,128)(2,1)} %copy-done.30) | copy-start | bytes 1179652
  201.1 65.1 %all-to-all-start.3 = ((bf16[64,8,4096]{2,1,0:T(8,128)(2,1)}), bf16[64,8,4096]{2,1,0:T(8,128)(2,1)}, u32[]{:S(2)}, u32[]{:S(2)}) async-start(bf16[64,8,4096]{2,1,0:T(8,128)(2,1)} %bitcast.31), calls=%async_computation.3 | async-start | bytes 8388608 | tf_op jit(solution)/shard_map/all_to_all | solution.py:30
  211.2 15.3 %copy-start.16 = (s32[2,128]{0,1:T(8,128)S(1)}, s32[2,128]{0,1:T(8,128)}, u32[]{:S(2)}) copy-start(s32[2,128]{0,1:T(8,128)} %copy-done.15) | copy-start | bytes 3076
  211.2 59.7 %copy-start.1 = (bf16[128,4096]{1,0:T(8,128)(2,1)S(1)}, bf16[128,4096]{1,0:T(8,128)(2,1)}, u32[]{:S(2)}) copy-start(bf16[128,4096]{1,0:T(8,128)(2,1)} %param.8) | copy-start | bytes 3145732

commit v5 on v4

--- a/solution.py
+++ b/solution.py
@@ -9,7 +9,7 @@
 
 HOT = 4
 COLUMNS = 512
-BROAD = 1024
+BROAD = 2048
 PARTS = 2
 BF16 = jnp.bfloat16
 F32 = jnp.float32
@@ -45,6 +45,10 @@
     )(*[arg for arg, _ in args])
 
 
+def pin(arg):
+    return pltpu.with_memory_space_constraint(arg, pltpu.HBM)
+
+
 def whole(arg):
     return arg, pl.BlockSpec(memory_space=pltpu.VMEM)
 
@@ -102,40 +106,41 @@
         position_ref[column : column + 1] = routing_ref[column : column + 1] * capacity + slot
 
 
-def dispatch_kernel(routing_ref, tokens_ref, position_ref, out_ref, pick_ref, *, experts, capacity):
+def dispatch_kernel(
+    routing_ref, weight_ref, tokens_ref, cotangent_ref, position_ref, kept_ref, rows_ref, grads_ref, pick_ref, scale_ref, *, experts, capacity
+):
     @pl.when(pl.program_id(0) == 0)
     def _():
         places(routing_ref, position_ref, experts, capacity)
+        kept_ref[...] = weight_ref[...]
         slots = lax.broadcasted_iota(jnp.int32, pick_ref.shape, 0)
-        hits = [position_ref[column : column + 1] == slots for column in range(position_ref.shape[0])]
+        columns = range(position_ref.shape[0])
+        hits = [position_ref[column : column + 1] == slots for column in columns]
         pick_ref[...] = sum(hit.astype(F32) for hit in hits).astype(BF16)
-
-    out_ref[...] = dot(pick_ref[...], tokens_ref[...], ((1,), (0,))).astype(BF16)
-
-
-def pick_matrix(position_ref, local_rows):
+        scale = sum(jnp.where(hits[column], weight_ref[column : column + 1], 0.0) for column in columns)
+        scale_ref[...] = jnp.broadcast_to(jnp.sum(scale, axis=1, keepdims=True), scale_ref.shape)
+
+    rows_ref[...] = dot(pick_ref[...], tokens_ref[...], ((1,), (0,))).astype(BF16)
+    grads = dot(pick_ref[...], cotangent_ref[...], ((1,), (0,)))
+    grads_ref[...] = (scale_ref[:, :1] * grads).astype(BF16)
+
+
+def combine_kernel(position_ref, weight_ref, out_ref, input_ref, combined_ref, token_grad_ref, pick_ref):
     tok_rows, top_count = position_ref.shape
-    slots = lax.broadcasted_iota(jnp.int32, (tok_rows, local_rows), 1)
-    return sum((position_ref[:, column : column + 1] == slots).astype(F32) for column in range(top_count)).astype(BF16)
-
-
-def token_grad_kernel(position_ref, rows_ref, out_ref, pick_ref):
+
     @pl.when(pl.program_id(0) == 0)
     def _():
-        pick_ref[...] = pick_matrix(position_ref, pick_ref.shape[1])
-
-    out_ref[...] = dot(pick_ref[...], rows_ref[...], ((1,), (0,))).astype(BF16)
-
-
-def combine_kernel(position_ref, weight_ref, rows_ref, out_ref):
-    rows = rows_ref[...]
-    tok_rows, top_count = position_ref.shape
-    slots = lax.broadcasted_iota(jnp.int32, (tok_rows, rows.shape[0]), 1)
-    total = jnp.zeros(out_ref.shape, F32)
+        slots = lax.broadcasted_iota(jnp.int32, (tok_rows, pick_ref.shape[1]), 1)
+        picks = [(position_ref[:, column : column + 1] == slots).astype(F32) for column in range(top_count)]
+        for column, pick in enumerate(picks + [sum(picks)]):
+            pick_ref[column * tok_rows : (column + 1) * tok_rows] = pick.astype(BF16)
+
+    found = dot(pick_ref[: top_count * tok_rows], out_ref[...], ((1,), (0,)))
+    total = jnp.zeros(combined_ref.shape, F32)
     for column in range(top_count):
-        pick = (position_ref[:, column : column + 1] == slots).astype(F32).astype(BF16)
-        total += weight_ref[:, column : column + 1] * dot(pick, rows, ((1,), (0,)))
-    out_ref[...] = total.astype(BF16)
+        total += weight_ref[:, column : column + 1] * found[column * tok_rows : (column + 1) * tok_rows]
+    combined_ref[...] = total.astype(BF16)
+    token_grad_ref[...] = dot(pick_ref[top_count * tok_rows :], input_ref[...], ((1,), (0,))).astype(BF16)
 
 
 def hidden_kernel(rows_ref, gate_ref, up_ref, hidden_ref, act_ref, slope_ref):
@@ -214,26 +219,22 @@
     gate_matrix, up_matrix, down_matrix = w_gate[0], w_up[0], w_down[0]
     width = gate_matrix.shape[1]
     broad_grid = (features // BROAD,)
-    pick_scratch = [pltpu.VMEM((tok_rows, local_rows), BF16)]
-
     place_shape = (top_count, tok_rows)
-    position, send_rows = call(
+    sent = by_column(local_rows, features, BF16, BROAD)
+    position, route_weights, send_rows, send_grads = call(
         functools.partial(dispatch_kernel, experts=experts, capacity=capacity),
-        [fixed(routing.T), across(tokens, BROAD)],
-        [(place_shape, jnp.int32, pl.BlockSpec(place_shape, lambda i: (0, 0))), by_column(local_rows, features, BF16, BROAD)],
-        24,
+        [fixed(routing.T), fixed(combine_weights.T), across(pin(tokens), BROAD), across(pin(cotangent), BROAD)],
+        [(place_shape, kind, pl.BlockSpec(place_shape, lambda i: (0, 0))) for kind in (jnp.int32, F32)] + [sent, sent],
+        40,
         grid=broad_grid,
-        scratch=[pltpu.VMEM((local_rows, tok_rows), BF16)],
+        scratch=[pltpu.VMEM((local_rows, tok_rows), BF16), pltpu.VMEM((local_rows, 128), F32)],
         pinned=True,
     )
-    position = position.T
     rows_own = exchange(send_rows, experts)
-    targets = jnp.arange(local_rows, dtype=jnp.int32)
-    selected = position[None, :, :] == targets[:, None, None]
-    picker = jnp.any(selected, axis=2).astype(BF16)
-    slot_weight = jnp.sum(jnp.where(selected, combine_weights[None, :, :], 0.0), axis=(1, 2))
-    send_grads = (slot_weight[:, None] * dot(picker, cotangent, ((1,), (0,)))).astype(BF16)
-    rows_own, send_grads = lax.optimization_barrier((rows_own, send_grads))
+    rows_own, send_grads, position, route_weights = lax.optimization_barrier(
+        (rows_own, send_grads, position, route_weights)
+    )
+    position, route_weights = position.T, route_weights.T
     grads_own = exchange(send_grads, experts)
 
     weights = [whole(matrix) for matrix in (gate_matrix, up_matrix, down_matrix)]
@@ -261,28 +262,21 @@
     (input_send,) = call(
         input_kernel, [whole(gate_own), whole(up_own)] + weights[:2] + [whole(value) for value in ins], send, 32
     )
-    out_back, input_send = lax.optimization_barrier((out_back, input_send))
-    input_back = exchange(input_send, experts)
-
     wgrads = weight_grads(
         [rows_own, rows_peer, grads_own, grads_peer],
         [hidden_own, hidden_peer, gate_own, gate_peer, up_own, up_peer],
     )
-    (combined,) = call(
+    out_back, input_send, position, route_weights, *wgrads = lax.optimization_barrier(
+        (out_back, input_send, position, route_weights, *wgrads)
+    )
+    input_back = exchange(input_send, experts)
+    combined, token_grad = call(
         combine_kernel,
-        [fixed(position), fixed(combine_weights), across(out_back, BROAD)],
-        [by_column(tok_rows, features, BF16, BROAD)],
-        24,
+        [fixed(position), fixed(route_weights), across(out_back, BROAD), across(input_back, BROAD)],
+        [by_column(tok_rows, features, BF16, BROAD)] * 2,
+        40,
         grid=broad_grid,
-    )
-    *wgrads, combined, input_back = lax.optimization_barrier((*wgrads, combined, input_back))
-    (token_grad,) = call(
-        token_grad_kernel,
-        [fixed(position), across(input_back, BROAD)],
-        [by_column(tok_rows, features, BF16, BROAD)],
-        24,
-        grid=broad_grid,
-        scratch=pick_scratch,
+        scratch=[pltpu.VMEM(((top_count + 1) * tok_rows, local_rows), BF16)],
     )
     return combined, token_grad, wgrads[0][None], wgrads[1][None], wgrads[2][None]
 

time: 272 us -> 266 us (0.978)
  blocking collectives: 0 us -> 126 us
  waiting for transfers between devices: 141 us -> 30.3 us
  starting transfers between devices: 40.6 us -> 16.9 us
  local copies, waits for them, and re-layouts: 18.1 us -> 22.1 us
  matrix products: 3.16 us -> 0 us
    all_to_all x0 -> x2, blocking collectives: none -> 126 us  [exchange(): lax.all_to_all(parts, 'expert', split_axis=0, concat_axis=0, tiled=True)]
    all_to_all x4 -> x2, waiting for transfers between devices: 139 us -> 29.2 us  [exchange(): lax.all_to_all(parts, 'expert', split_axis=0, concat_axis=0, tiled=True)]
    all_to_all x4 -> x2, starting transfers between devices: 39.5 us -> 15.9 us  [exchange(): lax.all_to_all(parts, 'expert', split_axis=0, concat_axis=0, tiled=True)]
    dot_general x1 -> x0, matrix products: 3.16 us -> none  [dot(): lax.dot_general(left, right, (dims, ((), ())), preferred_element_type=F32)]
    unnamed x71 -> x62, local copies, waits for them, and re-layouts: 17.9 us -> 20.7 us
    pallas_call x10 -> x9, Pallas kernels: 67.2 us -> 68.5 us  [call(): pl.pallas_call(kernel, grid=grid, in_specs=in_specs, out_specs=[spec for...]
  transfers between devices with their start and end apart: 10 -> 8, of which waited for: 5 -> 3; matrix products, arithmetic and copies ran while one was open for 1% -> 1% of each run, Pallas kernels for 22% -> 22%
where the time goes in v5:
time: 266 us; the launch traced here: 265 us
  blocking collectives  126 us (47%)
  Pallas kernels  68.5 us (26%)
  waiting for transfers between devices  30.3 us (11%)
  local copies, waits for them, and re-layouts  22.1 us (8%)
  starting transfers between devices  16.9 us (6%)
    all_to_all x2, blocking collectives, exchange(): lax.all_to_all(parts, 'expert', split_axis=0, concat_axis=0, tiled=True)  126 us
    pallas_call x9, Pallas kernels, call(): pl.pallas_call(kernel, grid=grid, in_specs=in_specs, out_specs=[spec for...  68.5 us
    all_to_all x2, waiting for transfers between devices, exchange(): lax.all_to_all(parts, 'expert', split_axis=0, concat_axis=0, tiled=True)  29.2 us
    unnamed x62, local copies, waits for them, and re-layouts  20.7 us
    all_to_all x2, starting transfers between devices, exchange(): lax.all_to_all(parts, 'expert', split_axis=0, concat_axis=0, tiled=True)  15.9 us
  transfers between devices with their start and end apart: 8, of which 3 were waited for; matrix products, arithmetic and copies ran while one was open for 1% of the time, Pallas kernels for 22%

profile of v5, /device:TPU:0, one launch (start us, length us, event | category | flops | bytes accessed | tf_op | source)
XLA Modules:
  0.0 265.1 jit_solution(18247135879816272632)
XLA Ops:
  0.6 0.0 copy-start.27
  0.6 0.7 copy-done.27
  1.3 0.7 copy-done.28
  2.0 5.8 %shard_map.110 = (s32[2,128]{1,0:T(2,128)}, f32[2,128]{1,0:T(2,128)}, bf16[512,4096]{1,0:T(8,128)(2,1)}, bf16[512,4096]{1,0:T(8,128)(2,1)}) custom-call(s32[2,128]{1,0:T(2,128)S(1)} %bitcast.35, f32[2,128]{1,0:T(2,128)S(1)} %bitcast.36, bf16[128,4096]{1,0:T(8,128)(2,1)} %tokens_ref.1, bf16[128,4096]{1,0:T(8,128)(2,1)} %cotangent_ref.1), custom_call_target="tpu_custom_call" | custom-call | flops 1000 | bytes 1000 | tf_op jit(solution)/shard_map/pallas_call | solution.py:36
  7.8 64.2 %all_to_all.20 = bf16[64,8,4096]{2,1,0:T(8,128)(2,1)} all-to-all(bf16[64,8,4096]{2,1,0:T(8,128)(2,1)} %bitcast.38), channel_id=1, replica_groups=mesh['dp'=2,'expert'=64] {'expert'}, dimensions={0} | all-to-all | bytes 8388608 | tf_op jit(solution)/shard_map/all_to_all | solution.py:30
  71.9 0.0 collective-permute-start
  71.9 6.4 %all-to-all-start.1 = ((bf16[64,8,4096]{2,1,0:T(8,128)(2,1)}), bf16[64,8,4096]{2,1,0:T(8,128)(2,1)}, u32[]{:S(2)}, u32[]{:S(2)}) async-start(bf16[64,8,4096]{2,1,0:T(8,128)(2,1)} %bitcast.37), calls=%async_computation.1 | async-start | bytes 8388608 | tf_op jit(solution)/shard_map/all_to_all | solution.py:30
  78.3 1.1 collective-permute-done.rows_ref.refs_1_
  79.4 0.0 copy-done.2
  79.4 1.9 copy-done.6
  81.3 10.1 %shard_map.112 = (bf16[512,384]{1,0:T(8,128)(2,1)S(1)}, f32[512,384]{1,0:T(8,128)S(1)}, f32[512,384]{1,0:T(8,128)S(1)}, bf16[256,4096]{1,0:T(8,128)(2,1)S(1)}, bf16[256,4096]{1,0:T(8,128)(2,1)S(1)}) custom-call(bf16[512,4096]{1,0:T(8,128)(2,1)} %collective-permute-done.rows_ref.refs_1_, bf16[4096,384]{1,0:T(8,128)(2,1)S(1)} %bitcast.22, ...), custom_call_target="tpu_custom_call" | custom-call | flops 1000 | bytes 1000 | tf_op jit(solution)/shard_map/pallas_call | solution.py:36
  91.5 0.0 copy-start.15
  91.5 0.9 copy-done.15
  92.3 0.9 copy-done.17
  93.2 0.1 collective-permute-start.1
  93.4 0.4 collective-permute-start.2
  93.7 0.0 copy-done.3
  93.7 6.9 %shard_map.111 = (bf16[512,384]{1,0:T(8,128)(2,1)S(1)}, f32[512,384]{1,0:T(8,128)S(1)}, f32[512,384]{1,0:T(8,128)S(1)}) custom-call(bf16[512,4096]{1,0:T(8,128)(2,1)} %bitcast.3.rows_ref.refs_0_, bf16[4096,384]{1,0:T(8,128)(2,1)S(1)} %bitcast.23, bf16[4096,384]{1,0:T(8,128)(2,1)S(1)} %bitcast.27), custom_call_target="tpu_custom_call" | custom-call | flops 1000 | bytes 1000 | tf_op jit(solution)/shard_map/pallas_call | solution.py:36
  100.7 0.0 copy-done.19
  100.7 0.0 copy-start.11
  100.7 0.9 copy-done.11
  101.6 0.9 copy-done.13
  102.5 0.0 collective-permute-done.1.refs_0_
  102.5 0.0 collective-permute-done.2.refs_1_
  102.5 0.0 copy-done
  102.5 2.3 shard_map.113
  104.8 0.0 copy-start.9
  104.8 2.0 copy-done.9
  106.9 26.8 %all-to-all-done.1 = bf16[64,8,4096]{2,1,0:T(8,128)(2,1)} async-done(((bf16[64,8,4096]{2,1,0:T(8,128)(2,1)}), bf16[64,8,4096]{2,1,0:T(8,128)(2,1)}, u32[]{:S(2)}, u32[]{:S(2)}) %all-to-all-start.1) | async-done | bytes 4194336 | tf_op jit(solution)/shard_map/all_to_all | solution.py:30
  133.6 0.0 collective-permute-start.3
  133.6 9.5 %all-to-all-start.2 = ((bf16[64,8,4096]{2,1,0:T(8,128)(2,1)}), bf16[64,8,4096]{2,1,0:T(8,128)(2,1)}, u32[]{:S(2)}, u32[]{:S(2)}) async-start(bf16[64,8,4096]{2,1,0:T(8,128)(2,1)} %bitcast.30), calls=%async_computation.2 | async-start | bytes 8388608 | tf_op jit(solution)/shard_map/all_to_all | solution.py:30
  143.1 0.0 collective-permute-done.3.grads_ref.refs_3_
  143.1 0.0 copy-start.4
  143.1 1.9 copy-done.4
  145.0 1.9 copy-done.7
  146.9 1.1 copy-done.16
  148.0 1.1 copy-done.18
  149.2 11.9 %shard_map.115 = (bf16[512,384]{1,0:T(8,128)(2,1)S(1)}, bf16[512,384]{1,0:T(8,128)(2,1)S(1)}, bf16[256,4096]{1,0:T(8,128)(2,1)}, bf16[256,4096]{1,0:T(8,128)(2,1)}) custom-call(bf16[512,4096]{1,0:T(8,128)(2,1)} %collective-permute-done.3.grads_ref.refs_3_, f32[512,384]{1,0:T(8,128)S(1)} %copy-done.16, f32[512,384]{1,0:T(8,128)S(1)} %copy-done.18, ...), custom_call_target="tpu_custom_call" | custom-call | flops 1000 | bytes 1000 | tf_op jit(solution)/shard_map/pallas_call | solution.py:36
  161.0 0.7 copy-done.21
  161.8 0.7 copy-done.23
  162.5 0.2 collective-permute-start.4
  162.7 0.3 collective-permute-start.5
  163.0 0.0 copy-done.30
  163.0 0.7 copy.12
  163.8 0.0 copy-done.29
  163.8 0.7 copy.13
  164.5 0.0 copy-done.1
  164.5 1.1 copy-done.12
  165.6 1.1 copy-done.14
  166.8 4.6 %shard_map.114 = (bf16[512,384]{1,0:T(8,128)(2,1)S(1)}, bf16[512,384]{1,0:T(8,128)(2,1)S(1)}) custom-call(bf16[512,4096]{1,0:T(8,128)(2,1)} %bitcast.5.grads_ref.refs_2_, f32[512,384]{1,0:T(8,128)S(1)} %copy-done.12, f32[512,384]{1,0:T(8,128)S(1)} %copy-done.14, bf16[384,4096]{1,0:T(8,128)(2,1)S(1)} %bitcast.21), custom_call_target="tpu_custom_call" | custom-call | flops 1000 | bytes 1000 | tf_op jit(solution)/shard_map/pallas_call | solution.py:36
  171.4 0.0 copy-done.20
  171.4 0.0 copy-done.22
  171.4 0.0 copy-done.24
  171.4 0.0 copy-start.5
  171.5 0.0 copy-start.8
  171.5 15.4 %shard_map.117 = (bf16[4096,384]{1,0:T(8,128)(2,1)}, bf16[4096,384]{1,0:T(8,128)(2,1)}, bf16[384,4096]{1,0:T(8,128)(2,1)}) custom-call(bf16[512,4096]{1,0:T(8,128)(2,1)} %bitcast.3.rows_ref.refs_0_, bf16[512,4096]{1,0:T(8,128)(2,1)} %collective-permute-done.rows_ref.refs_1_, bf16[512,4096]{1,0:T(8,128)(2,1)} %bitcast.5.grads_ref.refs_2_, ...), custom_call_target="tpu_custom_call" | custom-call | flops 1000 | bytes 1000 | tf_op jit(solution)/shard_map/pallas_call | solution.py:36
  186.9 0.0 collective-permute-done.4.refs_0_
  186.9 0.0 collective-permute-done.5.refs_1_
  186.9 6.8 %shard_map.116 = bf16[512,4096]{1,0:T(8,128)(2,1)S(1)} custom-call(bf16[512,384]{1,0:T(8,128)(2,1)S(1)} %get-tuple-element.54.gate_grad_ref.refs_6_, bf16[512,384]{1,0:T(8,128)(2,1)S(1)} %get-tuple-element.55.up_grad_ref.refs_8_, bf16[4096,384]{1,0:T(8,128)(2,1)S(1)} %bitcast.25, bf16[4096,384]{1,0:T(8,128)(2,1)S(1)} %bitcast.29, ...), custom_call_target="tpu_custom_call" | custom-call | flops 1000 | bytes 1000 | tf_op jit(solution)/shard_map/pallas_call | solution.py:36
  193.7 2.0 copy-done.10
  195.8 2.4 all-to-all-done.2
  198.2 62.3 %all_to_all.21 = bf16[64,8,4096]{2,1,0:T(8,128)(2,1)S(1)} all-to-all(bf16[64,8,4096]{2,1,0:T(8,128)(2,1)} %bitcast.32), channel_id=1, replica_groups=mesh['dp'=2,'expert'=64] {'expert'}, dimensions={0} | all-to-all | bytes 8388608 | tf_op jit(solution)/shard_map/all_to_all | solution.py:30
  260.5 0.0 copy-done.25
  260.5 4.6 %shard_map.118 = (bf16[128,4096]{1,0:T(8,128)(2,1)}, bf16[128,4096]{1,0:T(8,128)(2,1)}) custom-call(s32[128,2]{1,0:T(8,128)S(1)} %bitcast.33, f32[128,2]{1,0:T(8,128)S(1)} %bitcast.34, bf16[512,4096]{1,0:T(8,128)(2,1)} %bitcast.10.out_ref, bf16[512,4096]{1,0:T(8,128)(2,1)S(1)} %bitcast.31), custom_call_target="tpu_custom_call" | custom-call | flops 1000 | bytes 1000 | tf_op jit(solution)/shard_map/pallas_call | solution.py:36
  (27 shorter events, 0.0 us)
Async XLA Ops:
  0.6 0.7 copy-start.27
  1.3 0.7 copy-start.28
  71.9 7.5 %collective-permute-start = (bf16[512,4096]{1,0:T(8,128)(2,1)}, bf16[512,4096]{1,0:T(8,128)(2,1)}, u32[]{:S(2)}, u32[]{:S(2)}) collective-permute-start(bf16[512,4096]{1,0:T(8,128)(2,1)} %bitcast.3.rows_ref.refs_0_), channel_id=1, source_target_pairs={{0,64},{64,0},{1,65},{65,1},{2,66},{66,2},{3,67},{67,3},{4,68},{68... | collective-permute-start | bytes 12582920 | tf_op jit(solution)/shard_map/ppermute | solution.py:24
  71.9 7.5 %copy-start.2 = (bf16[1,4096,384]{2,1,0:T(8,128)(2,1)S(1)}, bf16[1,4096,384]{2,1,0:T(8,128)(2,1)}, u32[]{:S(2)}) copy-start(bf16[1,4096,384]{2,1,0:T(8,128)(2,1)} %param.11) | copy-start | bytes 9437188
  71.9 61.7 %all-to-all-start.1 = ((bf16[64,8,4096]{2,1,0:T(8,128)(2,1)}), bf16[64,8,4096]{2,1,0:T(8,128)(2,1)}, u32[]{:S(2)}, u32[]{:S(2)}) async-start(bf16[64,8,4096]{2,1,0:T(8,128)(2,1)} %bitcast.37), calls=%async_computation.1 | async-start | bytes 8388608 | tf_op jit(solution)/shard_map/all_to_all | solution.py:30
  79.4 1.9 copy-start.6
  81.3 12.4 %copy-start.3 = (bf16[1,4096,384]{2,1,0:T(8,128)(2,1)S(1)}, bf16[1,4096,384]{2,1,0:T(8,128)(2,1)}, u32[]{:S(2)}) copy-start(bf16[1,4096,384]{2,1,0:T(8,128)(2,1)} %param.11) | copy-start | bytes 9437188
  91.5 0.9 copy-start.15
  92.3 0.9 copy-start.17
  93.2 7.5 %copy-start.19 = (bf16[512,384]{1,0:T(8,128)(2,1)}, bf16[512,384]{1,0:T(8,128)(2,1)S(1)}, u32[]{:S(2)}) copy-start(bf16[512,384]{1,0:T(8,128)(2,1)S(1)} %get-tuple-element.62.refs_5_) | copy-start | bytes 1179652
  93.2 9.2 %collective-permute-start.1 = (bf16[256,4096]{1,0:T(8,128)(2,1)S(1)}, bf16[256,4096]{1,0:T(8,128)(2,1)S(1)}, u32[]{:S(2)}, u32[]{:S(2)}) collective-permute-start(bf16[256,4096]{1,0:T(8,128)(2,1)S(1)} %get-tuple-element.48), channel_id=1, source_target_pairs={{0,64},{64,0},{1,65},{65,1},{2,66},{66,2},{3,67},{67,3},{4,68},{68... | collective-permute-start | bytes 6291464 | tf_op jit(solution)/shard_map/ppermute | solution.py:24
  93.4 9.1 %copy-start = (bf16[1,384,4096]{2,1,0:T(8,128)(2,1)S(1)}, bf16[1,384,4096]{2,1,0:T(8,128)(2,1)}, u32[]{:S(2)}) copy-start(bf16[1,384,4096]{2,1,0:T(8,128)(2,1)} %param.13) | copy-start | bytes 9437188
  93.4 9.1 %collective-permute-start.2 = (bf16[256,4096]{1,0:T(8,128)(2,1)S(1)}, bf16[256,4096]{1,0:T(8,128)(2,1)S(1)}, u32[]{:S(2)}, u32[]{:S(2)}) collective-permute-start(bf16[256,4096]{1,0:T(8,128)(2,1)S(1)} %get-tuple-element.49), channel_id=1, source_target_pairs={{0,64},{64,0},{1,65},{65,1},{2,66},{66,2},{3,67},{67,3},{4,68},{68... | collective-permute-start | bytes 6291464 | tf_op jit(solution)/shard_map/ppermute | solution.py:24
  100.7 0.9 copy-start.11
  101.6 0.9 copy-start.13
  104.8 2.0 copy-start.9
  133.6 9.5 %collective-permute-start.3 = (bf16[512,4096]{1,0:T(8,128)(2,1)}, bf16[512,4096]{1,0:T(8,128)(2,1)}, u32[]{:S(2)}, u32[]{:S(2)}) collective-permute-start(bf16[512,4096]{1,0:T(8,128)(2,1)} %bitcast.5.grads_ref.refs_2_), channel_id=1, source_target_pairs={{0,64},{64,0},{1,65},{65,1},{2,66},{66,2},{3,67},{67,3},{4,68},{68... | collective-permute-start | bytes 12582920 | tf_op jit(solution)/shard_map/ppermute | solution.py:24
  133.6 64.6 %all-to-all-start.2 = ((bf16[64,8,4096]{2,1,0:T(8,128)(2,1)}), bf16[64,8,4096]{2,1,0:T(8,128)(2,1)}, u32[]{:S(2)}, u32[]{:S(2)}) async-start(bf16[64,8,4096]{2,1,0:T(8,128)(2,1)} %bitcast.30), calls=%async_computation.2 | async-start | bytes 8388608 | tf_op jit(solution)/shard_map/all_to_all | solution.py:30
  143.1 1.9 copy-start.4
  145.0 1.9 copy-start.7
  146.9 1.1 copy-start.16
  148.0 1.1 copy-start.18
  149.2 13.9 %copy-start.30 = (s32[2,128]{1,0:T(2,128)S(1)}, s32[2,128]{1,0:T(2,128)}, u32[]{:S(2)}) copy-start(s32[2,128]{1,0:T(2,128)} %get-tuple-element.60) | copy-start | bytes 3076
  149.2 14.6 %copy-start.29 = (f32[2,128]{1,0:T(2,128)S(1)}, f32[2,128]{1,0:T(2,128)}, u32[]{:S(2)}) copy-start(f32[2,128]{1,0:T(2,128)} %get-tuple-element.61) | copy-start | bytes 3076
  149.2 15.3 %copy-start.1 = (bf16[1,384,4096]{2,1,0:T(8,128)(2,1)S(1)}, bf16[1,384,4096]{2,1,0:T(8,128)(2,1)}, u32[]{:S(2)}) copy-start(bf16[1,384,4096]{2,1,0:T(8,128)(2,1)} %param.13) | copy-start | bytes 9437188
  161.0 0.7 copy-start.21
  161.8 0.7 copy-start.23
  162.5 24.4 %collective-permute-start.4 = (bf16[256,4096]{1,0:T(8,128)(2,1)}, bf16[256,4096]{1,0:T(8,128)(2,1)}, u32[]{:S(2)}, u32[]{:S(2)}) collective-permute-start(bf16[256,4096]{1,0:T(8,128)(2,1)} %get-tuple-element.58), channel_id=1, source_target_pairs={{0,64},{64,0},{1,65},{65,1},{2,66},{66,2},{3,67},{67,3},{4,68},{68... | collective-permute-start | bytes 6291464 | tf_op jit(solution)/shard_map/ppermute | solution.py:24
  162.7 24.2 %collective-permute-start.5 = (bf16[256,4096]{1,0:T(8,128)(2,1)}, bf16[256,4096]{1,0:T(8,128)(2,1)}, u32[]{:S(2)}, u32[]{:S(2)}) collective-permute-start(bf16[256,4096]{1,0:T(8,128)(2,1)} %get-tuple-element.59), channel_id=1, source_target_pairs={{0,64},{64,0},{1,65},{65,1},{2,66},{66,2},{3,67},{67,3},{4,68},{68... | collective-permute-start | bytes 6291464 | tf_op jit(solution)/shard_map/ppermute | solution.py:24
  164.5 1.1 copy-start.12
  165.6 1.1 copy-start.14
  166.8 4.6 %copy-start.20 = (bf16[512,384]{1,0:T(8,128)(2,1)S(1)}, bf16[512,384]{1,0:T(8,128)(2,1)}, u32[]{:S(2)}) copy-start(bf16[512,384]{1,0:T(8,128)(2,1)} %copy-done.19) | copy-start | bytes 1179652
  166.8 4.6 %copy-start.22 = (bf16[512,384]{1,0:T(8,128)(2,1)S(1)}, bf16[512,384]{1,0:T(8,128)(2,1)}, u32[]{:S(2)}) copy-start(bf16[512,384]{1,0:T(8,128)(2,1)} %copy-done.21) | copy-start | bytes 1179652
  166.8 4.7 %copy-start.24 = (bf16[512,384]{1,0:T(8,128)(2,1)S(1)}, bf16[512,384]{1,0:T(8,128)(2,1)}, u32[]{:S(2)}) copy-start(bf16[512,384]{1,0:T(8,128)(2,1)} %copy-done.23) | copy-start | bytes 1179652
  171.4 15.5 %copy-start.5 = (bf16[1,4096,384]{2,1,0:T(8,128)(2,1)S(1)}, bf16[1,4096,384]{2,1,0:T(8,128)(2,1)}, u32[]{:S(2)}) copy-start(bf16[1,4096,384]{2,1,0:T(8,128)(2,1)} %param.11) | copy-start | bytes 9437188
  171.5 15.5 %copy-start.8 = (bf16[1,4096,384]{2,1,0:T(8,128)(2,1)S(1)}, bf16[1,4096,384]{2,1,0:T(8,128)(2,1)}, u32[]{:S(2)}) copy-start(bf16[1,4096,384]{2,1,0:T(8,128)(2,1)} %param.12) | copy-start | bytes 9437188
  193.7 2.0 copy-start.10
  198.2 62.3 %copy-start.25 = (s32[2,128]{0,1:T(8,128)S(1)}, s32[2,128]{0,1:T(8,128)}, u32[]{:S(2)}) copy-start(s32[2,128]{0,1:T(8,128)} %copy.12) | copy-start | bytes 3076
  198.2 62.3 %copy-start.26 = (f32[2,128]{0,1:T(8,128)S(1)}, f32[2,128]{0,1:T(8,128)}, u32[]{:S(2)}) copy-start(f32[2,128]{0,1:T(8,128)} %copy.13) | copy-start | bytes 3076

commit v6 on v5

--- a/solution.py
+++ b/solution.py
@@ -11,6 +11,7 @@
 COLUMNS = 512
 BROAD = 2048
 PARTS = 2
+STEPS = 4
 BF16 = jnp.bfloat16
 F32 = jnp.float32
 MIB = 1024 * 1024
@@ -61,8 +62,21 @@
     return arg, pl.BlockSpec((arg.shape[0], columns), lambda i: (0, i))
 
 
-def out_whole(shape, kind):
-    return shape, kind, pl.BlockSpec(memory_space=pltpu.VMEM)
+def by_rows(arg, steps):
+    return pin(arg), pl.BlockSpec((arg.shape[0] // steps, arg.shape[1]), lambda i: (i, 0))
+
+
+def out_rows(rows, columns, kind, steps):
+    return (rows, columns), kind, pl.BlockSpec((rows // steps, columns), lambda i: (i, 0))
+
+
+def peer_blocks(peers, steps):
+    each = steps // PARTS
+    blocks = []
+    for part, peer in enumerate(peers):
+        index = lambda i, part=part: (jnp.clip(i - part * each, 0, each - 1), 0)
+        blocks.append((peer, pl.BlockSpec((peer.shape[0] // each, peer.shape[1]), index)))
+    return blocks
 
 
 def by_column(rows, columns, kind, wide):
@@ -150,18 +164,22 @@
 def forward_kernel(rows_ref, gate_ref, up_ref, down_ref, hidden_ref, act_ref, slope_ref, *out_refs):
     hidden, act_ref[...], slope_ref[...] = hidden_parts(rows_ref[...], gate_ref[...], up_ref[...])
     hidden_ref[...] = hidden
-    size = hidden.shape[0] // len(out_refs)
+    out = dot(hidden, down_ref[...], ((1,), (0,))).astype(BF16)
     for i, out_ref in enumerate(out_refs):
-        out_ref[...] = dot(hidden[i * size : (i + 1) * size], down_ref[...], ((1,), (0,))).astype(BF16)
+
+        @pl.when(pl.program_id(0) == i)
+        def _():
+            out_ref[...] = out
+
+
+def peer_part(peer_refs):
+    return jnp.where(pl.program_id(0) < pl.num_programs(0) // PARTS, peer_refs[0][...], peer_refs[1][...]).astype(F32)
 
 
 def out_kernel(hidden_ref, down_ref, *refs):
-    peer_refs, out_ref = refs[:-1], refs[-1]
-    size = hidden_ref.shape[0] // len(peer_refs)
-    for i, peer_ref in enumerate(peer_refs):
-        rows = slice(i * size, (i + 1) * size)
-        total = dot(hidden_ref[rows], down_ref[...], ((1,), (0,))) + peer_ref[...].astype(F32)
-        out_ref[rows] = total.astype(BF16)
+    out_ref = refs[-1]
+    total = dot(hidden_ref[...], down_ref[...], ((1,), (0,)))
+    out_ref[...] = (total + peer_part(refs[:-1])).astype(BF16)
 
 
 def grad_kernel(grads_ref, act_ref, slope_ref, down_ref, gate_grad_ref, up_grad_ref):
@@ -172,19 +190,18 @@
     gate_grad, up_grad = grad_parts(grads_ref[...], act_ref[...], slope_ref[...], down_ref[...])
     gate_grad_ref[...] = gate_grad
     up_grad_ref[...] = up_grad
-    size = gate_grad.shape[0] // len(in_refs)
+    back = input_parts(gate_grad, up_grad, gate_ref[...], up_ref[...]).astype(BF16)
     for i, in_ref in enumerate(in_refs):
-        rows = slice(i * size, (i + 1) * size)
-        in_ref[...] = input_parts(gate_grad[rows], up_grad[rows], gate_ref[...], up_ref[...]).astype(BF16)
+
+        @pl.when(pl.program_id(0) == i)
+        def _():
+            in_ref[...] = back
 
 
 def input_kernel(gate_grad_ref, up_grad_ref, gate_ref, up_ref, *refs):
-    peer_refs, out_ref = refs[:-1], refs[-1]
-    size = gate_grad_ref.shape[0] // len(peer_refs)
-    for i, peer_ref in enumerate(peer_refs):
-        rows = slice(i * size, (i + 1) * size)
-        total = input_parts(gate_grad_ref[rows], up_grad_ref[rows], gate_ref[...], up_ref[...])
-        out_ref[rows] = (total + peer_ref[...].astype(F32)).astype(BF16)
+    out_ref = refs[-1]
+    total = input_parts(gate_grad_ref[...], up_grad_ref[...], gate_ref[...], up_ref[...])
+    out_ref[...] = (total + peer_part(refs[:-1])).astype(BF16)
 
 
 def weight_kernel(*refs):
@@ -201,8 +218,7 @@
 def weight_grads(wide, kept):
     features = wide[0].shape[1]
     width = kept[0].shape[1]
-    args = [(value, pl.BlockSpec((value.shape[0], COLUMNS), lambda i: (0, i))) for value in wide]
-    args += [fixed(value) for value in kept]
+    args = [across(pin(value), COLUMNS) for value in wide] + [fixed(pin(value)) for value in kept]
     tall = ((features, width), BF16, pl.BlockSpec((COLUMNS, width), lambda i: (i, 0)))
     return call(weight_kernel, args, [tall, tall, by_column(width, features, BF16, COLUMNS)], 48, grid=(features // COLUMNS,))
 
@@ -223,7 +239,7 @@
     sent = by_column(local_rows, features, BF16, BROAD)
     position, route_weights, send_rows, send_grads = call(
         functools.partial(dispatch_kernel, experts=experts, capacity=capacity),
-        [fixed(routing.T), fixed(combine_weights.T), across(pin(tokens), BROAD), across(pin(cotangent), BROAD)],
+        [fixed(pin(routing.T)), fixed(pin(combine_weights.T)), across(pin(tokens), BROAD), across(pin(cotangent), BROAD)],
         [(place_shape, kind, pl.BlockSpec(place_shape, lambda i: (0, 0))) for kind in (jnp.int32, F32)] + [sent, sent],
         40,
         grid=broad_grid,
@@ -238,29 +254,48 @@
     grads_own = exchange(send_grads, experts)
 
     weights = [whole(matrix) for matrix in (gate_matrix, up_matrix, down_matrix)]
-    kept = [out_whole((local_rows, width), kind) for kind in (BF16, F32, F32)]
-    pair = [out_whole((local_rows, width), BF16)] * 2
-    parts = [out_whole((local_rows // PARTS, features), BF16)] * PARTS
-    send = [out_whole((local_rows, features), BF16)]
+    kept = [out_rows(local_rows, width, kind, PARTS) for kind in (BF16, F32, F32)]
+    pair = [out_rows(local_rows, width, BF16, PARTS)] * 2
+    part = (local_rows // PARTS, features)
+    parts = [(part, BF16, pl.BlockSpec(part, lambda i: (0, 0)))] * PARTS
+    send = [out_rows(local_rows, features, BF16, STEPS)]
+    halves = dict(grid=(PARTS,), pinned=True)
+    steps = dict(grid=(STEPS,), pinned=True)
 
     rows_peer = swap(rows_own)
-    hidden_own, act_own, slope_own = call(hidden_kernel, [whole(rows_own)] + weights[:2], kept, 32)
-    hidden_peer, act_peer, slope_peer, *outs = call(forward_kernel, [whole(rows_peer)] + weights, kept + parts, 40)
+    hidden_own, act_own, slope_own = call(hidden_kernel, [by_rows(rows_own, PARTS)] + weights[:2], kept, 32, **halves)
+    hidden_peer, act_peer, slope_peer, *outs = call(
+        forward_kernel, [by_rows(rows_peer, PARTS)] + weights, kept + parts, 44, **halves
+    )
     outs = [swap(out) for out in outs]
-    (out_send,) = call(out_kernel, [whole(hidden_own)] + weights[2:] + [whole(out) for out in outs], send, 32)
+    (out_send,) = call(
+        out_kernel, [by_rows(hidden_own, STEPS)] + weights[2:] + peer_blocks(outs, STEPS), send, 32, **steps
+    )
     grads_own, out_send = lax.optimization_barrier((grads_own, out_send))
     out_back = exchange(out_send, experts)
 
     grads_peer = swap(grads_own)
     gate_own, up_own = call(
-        grad_kernel, [whole(value) for value in (grads_own, act_own, slope_own)] + weights[2:], pair, 32
+        grad_kernel,
+        [by_rows(value, PARTS) for value in (grads_own, act_own, slope_own)] + weights[2:],
+        pair,
+        32,
+        **halves,
     )
     gate_peer, up_peer, *ins = call(
-        backward_kernel, [whole(value) for value in (grads_peer, act_peer, slope_peer)] + weights, pair + parts, 40
+        backward_kernel,
+        [by_rows(value, PARTS) for value in (grads_peer, act_peer, slope_peer)] + weights,
+        pair + parts,
+        44,
+        **halves,
     )
     ins = [swap(value) for value in ins]
     (input_send,) = call(
-        input_kernel, [whole(gate_own), whole(up_own)] + weights[:2] + [whole(value) for value in ins], send, 32
+        input_kernel,
+        [by_rows(gate_own, STEPS), by_rows(up_own, STEPS)] + weights[:2] + peer_blocks(ins, STEPS),
+        send,
+        32,
+        **steps,
     )
     wgrads = weight_grads(
         [rows_own, rows_peer, grads_own, grads_peer],

time: 266 us -> 264 us (level)
  local copies, waits for them, and re-layouts: 22.1 us -> 7.8 us
  Pallas kernels: 68.5 us -> 78 us
  waiting for transfers between devices: 30.3 us -> 33.6 us
    unnamed x62 -> x18, local copies, waits for them, and re-layouts: 20.7 us -> 7.57 us
    pallas_call x9, Pallas kernels: 68.5 us -> 78 us  [call(): pl.pallas_call(kernel, grid=grid, in_specs=in_specs, out_specs=[spec for...]
    all_to_all x2, waiting for transfers between devices: 29.2 us -> 32.5 us  [exchange(): lax.all_to_all(parts, 'expert', split_axis=0, concat_axis=0, tiled=True)]
  transfers between devices with their start and end apart: 8 -> 8, of which waited for: 3 -> 3; matrix products, arithmetic and copies ran while one was open for 1% -> 0% of each run, Pallas kernels for 22% -> 26%
where the time goes in v6:
time: 264 us
  blocking collectives  126 us (48%)
  Pallas kernels  78 us (30%)
  waiting for transfers between devices  33.6 us (13%)
  starting transfers between devices  17.1 us (6%)
  local copies, waits for them, and re-layouts  7.8 us (3%)
    all_to_all x2, blocking collectives, exchange(): lax.all_to_all(parts, 'expert', split_axis=0, concat_axis=0, tiled=True)  126 us
    pallas_call x9, Pallas kernels, call(): pl.pallas_call(kernel, grid=grid, in_specs=in_specs, out_specs=[spec for...  78 us
    all_to_all x2, waiting for transfers between devices, exchange(): lax.all_to_all(parts, 'expert', split_axis=0, concat_axis=0, tiled=True)  32.5 us
    all_to_all x2, starting transfers between devices, exchange(): lax.all_to_all(parts, 'expert', split_axis=0, concat_axis=0, tiled=True)  15.9 us
    unnamed x18, local copies, waits for them, and re-layouts  7.57 us
  transfers between devices with their start and end apart: 8, of which 3 were waited for; matrix products, arithmetic and copies ran while one was open for 0% of the time, Pallas kernels for 26%

profile of v6, /device:TPU:0, one launch (start us, length us, event | category | flops | bytes accessed | tf_op | source)
XLA Modules:
  0.0 263.5 jit_solution(4345610854961606919)
XLA Ops:
  0.6 5.7 %shard_map.110 = (s32[2,128]{1,0:T(2,128)}, f32[2,128]{1,0:T(2,128)}, bf16[512,4096]{1,0:T(8,128)(2,1)}, bf16[512,4096]{1,0:T(8,128)(2,1)}) custom-call(s32[2,128]{1,0:T(2,128)} %bitcast.37, f32[2,128]{1,0:T(2,128)} %bitcast.38, bf16[128,4096]{1,0:T(8,128)(2,1)} %tokens_ref.1, bf16[128,4096]{1,0:T(8,128)(2,1)} %cotangent_ref.1), custom_call_target="tpu_custom_call" | custom-call | flops 1000 | bytes 1000 | tf_op jit(solution)/shard_map/pallas_call | solution.py:37
  6.3 64.2 %all_to_all.20 = bf16[64,8,4096]{2,1,0:T(8,128)(2,1)} all-to-all(bf16[64,8,4096]{2,1,0:T(8,128)(2,1)} %bitcast.36), channel_id=1, replica_groups=mesh['dp'=2,'expert'=64] {'expert'}, dimensions={0} | all-to-all | bytes 8388608 | tf_op jit(solution)/shard_map/all_to_all | solution.py:31
  70.5 0.0 collective-permute-start
  70.5 0.0 copy-start
  70.5 6.4 %all-to-all-start.1 = ((bf16[64,8,4096]{2,1,0:T(8,128)(2,1)}), bf16[64,8,4096]{2,1,0:T(8,128)(2,1)}, u32[]{:S(2)}, u32[]{:S(2)}) async-start(bf16[64,8,4096]{2,1,0:T(8,128)(2,1)} %bitcast.35), calls=%async_computation.1 | async-start | bytes 8388608 | tf_op jit(solution)/shard_map/all_to_all | solution.py:31
  76.9 1.1 collective-permute-done.rows_ref.refs_1_
  78.0 0.0 copy-done
  78.0 0.0 copy-start.1
  78.0 1.9 copy-done.1
  79.9 0.0 copy-start.4
  79.9 1.9 copy-done.4
  81.8 11.4 %shard_map.112 = (bf16[512,384]{1,0:T(8,128)(2,1)}, f32[512,384]{1,0:T(8,128)}, f32[512,384]{1,0:T(8,128)}, bf16[256,4096]{1,0:T(8,128)(2,1)}, bf16[256,4096]{1,0:T(8,128)(2,1)}) custom-call(bf16[512,4096]{1,0:T(8,128)(2,1)} %collective-permute-done.rows_ref.refs_1_, bf16[4096,384]{1,0:T(8,128)(2,1)S(1)} %bitcast.22, bf16[4096,384]{1,0:T(8,128)(2,1)S(1)} %bitcast.26, ...), custom_call_target="tpu_custom_call" | custom-call | flops 1000 | bytes 1000 | tf_op jit(solution)/shard_map/pallas_call | solution.py:37
  93.2 0.2 collective-permute-start.1
  93.4 0.4 collective-permute-start.2
  93.8 7.2 %shard_map.111 = (bf16[512,384]{1,0:T(8,128)(2,1)}, f32[512,384]{1,0:T(8,128)}, f32[512,384]{1,0:T(8,128)}) custom-call(bf16[512,4096]{1,0:T(8,128)(2,1)} %bitcast.3.rows_ref.refs_0_, bf16[4096,384]{1,0:T(8,128)(2,1)S(1)} %bitcast.23, bf16[4096,384]{1,0:T(8,128)(2,1)S(1)} %bitcast.27), custom_call_target="tpu_custom_call" | custom-call | flops 1000 | bytes 1000 | tf_op jit(solution)/shard_map/pallas_call | solution.py:37
  101.0 0.0 collective-permute-done.1.refs_0_
  101.0 0.0 collective-permute-done.2.refs_1_
  101.0 5.3 %shard_map.113 = bf16[512,4096]{1,0:T(8,128)(2,1)} custom-call(bf16[512,384]{1,0:T(8,128)(2,1)} %get-tuple-element.47.hidden_ref.refs_4_, bf16[384,4096]{1,0:T(8,128)(2,1)S(1)} %bitcast.19, bf16[256,4096]{1,0:T(8,128)(2,1)S(1)} %collective-permute-done.1.refs_0_, bf16[256,4096]{1,0:T(8,128)(2,1)S(1)} %collective-permute-done.2.refs_1_), custom_call_target="tpu_custom_call" | custom-call | flops 1000 | bytes 1000 | tf_op jit(solution)/shard_map/pallas_call | solution.py:37
  106.3 25.9 %all-to-all-done.1 = bf16[64,8,4096]{2,1,0:T(8,128)(2,1)} async-done(((bf16[64,8,4096]{2,1,0:T(8,128)(2,1)}), bf16[64,8,4096]{2,1,0:T(8,128)(2,1)}, u32[]{:S(2)}, u32[]{:S(2)}) %all-to-all-start.1) | async-done | bytes 4194336 | tf_op jit(solution)/shard_map/all_to_all | solution.py:31
  132.2 0.0 collective-permute-start.3
  132.2 9.5 %all-to-all-start.2 = ((bf16[64,8,4096]{2,1,0:T(8,128)(2,1)}), bf16[64,8,4096]{2,1,0:T(8,128)(2,1)}, u32[]{:S(2)}, u32[]{:S(2)}) async-start(bf16[64,8,4096]{2,1,0:T(8,128)(2,1)} %bitcast.33), calls=%async_computation.2 | async-start | bytes 8388608 | tf_op jit(solution)/shard_map/all_to_all | solution.py:31
  141.7 0.0 collective-permute-done.3.grads_ref.refs_3_
  141.7 0.0 copy-start.2
  141.7 1.9 copy-done.2
  143.6 0.0 copy-start.5
  143.6 1.9 copy-done.5
  145.5 0.0 copy-start.8
  145.5 0.0 copy-start.7
  145.5 11.4 %shard_map.115 = (bf16[512,384]{1,0:T(8,128)(2,1)}, bf16[512,384]{1,0:T(8,128)(2,1)}, bf16[256,4096]{1,0:T(8,128)(2,1)}, bf16[256,4096]{1,0:T(8,128)(2,1)}) custom-call(bf16[512,4096]{1,0:T(8,128)(2,1)} %collective-permute-done.3.grads_ref.refs_3_, f32[512,384]{1,0:T(8,128)} %get-tuple-element.56.act_ref, f32[512,384]{1,0:T(8,128)} %get-tuple-element.57.slope_ref, ...), custom_call_target="tpu_custom_call" | custom-call | flops 1000 | bytes 1000 | tf_op jit(solution)/shard_map/pallas_call | solution.py:37
  156.9 0.3 collective-permute-start.4
  157.2 0.3 collective-permute-start.5
  157.5 0.0 copy-done.8
  157.5 0.1 copy.12
  157.6 0.0 copy-done.7
  157.6 0.1 copy.13
  157.7 5.1 %shard_map.114 = (bf16[512,384]{1,0:T(8,128)(2,1)}, bf16[512,384]{1,0:T(8,128)(2,1)}) custom-call(bf16[512,4096]{1,0:T(8,128)(2,1)} %bitcast.5.grads_ref.refs_2_, f32[512,384]{1,0:T(8,128)} %get-tuple-element.52.act_ref, f32[512,384]{1,0:T(8,128)} %get-tuple-element.53.slope_ref, bf16[384,4096]{1,0:T(8,128)(2,1)S(1)} %bitcast.21), custom_call_target="tpu_custom_call" | custom-call | flops 1000 | bytes 1000 | tf_op jit(solution)/shard_map/pallas_call | solution.py:37
  162.8 0.0 copy-start.3
  162.8 0.0 copy-start.6
  162.8 16.2 %shard_map.117 = (bf16[4096,384]{1,0:T(8,128)(2,1)}, bf16[4096,384]{1,0:T(8,128)(2,1)}, bf16[384,4096]{1,0:T(8,128)(2,1)}) custom-call(bf16[512,4096]{1,0:T(8,128)(2,1)} %bitcast.3.rows_ref.refs_0_, bf16[512,4096]{1,0:T(8,128)(2,1)} %collective-permute-done.rows_ref.refs_1_, bf16[512,4096]{1,0:T(8,128)(2,1)} %bitcast.5.grads_ref.refs_2_, ...), custom_call_target="tpu_custom_call" | custom-call | flops 1000 | bytes 1000 | tf_op jit(solution)/shard_map/pallas_call | solution.py:37
  179.1 0.0 collective-permute-done.4.refs_0_
  179.1 0.0 collective-permute-done.5.refs_1_
  179.1 0.0 copy-done.3
  179.1 0.0 copy-done.6
  179.1 11.1 %shard_map.116 = bf16[512,4096]{1,0:T(8,128)(2,1)} custom-call(bf16[512,384]{1,0:T(8,128)(2,1)} %get-tuple-element.54.gate_grad_ref.refs_6_, bf16[512,384]{1,0:T(8,128)(2,1)} %get-tuple-element.55.up_grad_ref.refs_8_, bf16[4096,384]{1,0:T(8,128)(2,1)S(1)} %bitcast.25, bf16[4096,384]{1,0:T(8,128)(2,1)S(1)} %bitcast.29, ...), custom_call_target="tpu_custom_call" | custom-call | flops 1000 | bytes 1000 | tf_op jit(solution)/shard_map/pallas_call | solution.py:37
  190.1 6.6 %all-to-all-done.2 = bf16[64,8,4096]{2,1,0:T(8,128)(2,1)} async-done(((bf16[64,8,4096]{2,1,0:T(8,128)(2,1)}), bf16[64,8,4096]{2,1,0:T(8,128)(2,1)}, u32[]{:S(2)}, u32[]{:S(2)}) %all-to-all-start.2) | async-done | bytes 4194336 | tf_op jit(solution)/shard_map/all_to_all | solution.py:31
  196.8 62.2 %all_to_all.21 = bf16[64,8,4096]{2,1,0:T(8,128)(2,1)S(1)} all-to-all(bf16[64,8,4096]{2,1,0:T(8,128)(2,1)} %bitcast.34), channel_id=1, replica_groups=mesh['dp'=2,'expert'=64] {'expert'}, dimensions={0} | all-to-all | bytes 8388608 | tf_op jit(solution)/shard_map/all_to_all | solution.py:31
  259.0 4.6 %shard_map.118 = (bf16[128,4096]{1,0:T(8,128)(2,1)}, bf16[128,4096]{1,0:T(8,128)(2,1)}) custom-call(s32[128,2]{1,0:T(8,128)S(1)} %bitcast.31, f32[128,2]{1,0:T(8,128)S(1)} %bitcast.32, bf16[512,4096]{1,0:T(8,128)(2,1)} %bitcast.10.out_ref, bf16[512,4096]{1,0:T(8,128)(2,1)S(1)} %bitcast.30), custom_call_target="tpu_custom_call" | custom-call | flops 1000 | bytes 1000 | tf_op jit(solution)/shard_map/pallas_call | solution.py:37
Async XLA Ops:
  70.5 7.5 %collective-permute-start = (bf16[512,4096]{1,0:T(8,128)(2,1)}, bf16[512,4096]{1,0:T(8,128)(2,1)}, u32[]{:S(2)}, u32[]{:S(2)}) collective-permute-start(bf16[512,4096]{1,0:T(8,128)(2,1)} %bitcast.3.rows_ref.refs_0_), channel_id=1, source_target_pairs={{0,64},{64,0},{1,65},{65,1},{2,66},{66,2},{3,67},{67,3},{4,68},{68... | collective-permute-start | bytes 12582920 | tf_op jit(solution)/shard_map/ppermute | solution.py:25
  70.5 7.5 %copy-start = (bf16[1,384,4096]{2,1,0:T(8,128)(2,1)S(1)}, bf16[1,384,4096]{2,1,0:T(8,128)(2,1)}, u32[]{:S(2)}) copy-start(bf16[1,384,4096]{2,1,0:T(8,128)(2,1)} %param.13) | copy-start | bytes 9437188
  70.5 61.7 %all-to-all-start.1 = ((bf16[64,8,4096]{2,1,0:T(8,128)(2,1)}), bf16[64,8,4096]{2,1,0:T(8,128)(2,1)}, u32[]{:S(2)}, u32[]{:S(2)}) async-start(bf16[64,8,4096]{2,1,0:T(8,128)(2,1)} %bitcast.35), calls=%async_computation.1 | async-start | bytes 8388608 | tf_op jit(solution)/shard_map/all_to_all | solution.py:31
  78.0 1.9 copy-start.1
  79.9 1.9 copy-start.4
  93.2 7.8 %collective-permute-start.1 = (bf16[256,4096]{1,0:T(8,128)(2,1)}, bf16[256,4096]{1,0:T(8,128)(2,1)S(1)}, u32[]{:S(2)}, u32[]{:S(2)}) collective-permute-start(bf16[256,4096]{1,0:T(8,128)(2,1)} %get-tuple-element.48), channel_id=1, source_target_pairs={{0,64},{64,0},{1,65},{65,1},{2,66},{66,2},{3,67},{67,3},{4,68},{68... | collective-permute-start | bytes 6291464 | tf_op jit(solution)/shard_map/ppermute | solution.py:25
  93.4 7.6 %collective-permute-start.2 = (bf16[256,4096]{1,0:T(8,128)(2,1)}, bf16[256,4096]{1,0:T(8,128)(2,1)S(1)}, u32[]{:S(2)}, u32[]{:S(2)}) collective-permute-start(bf16[256,4096]{1,0:T(8,128)(2,1)} %get-tuple-element.49), channel_id=1, source_target_pairs={{0,64},{64,0},{1,65},{65,1},{2,66},{66,2},{3,67},{67,3},{4,68},{68... | collective-permute-start | bytes 6291464 | tf_op jit(solution)/shard_map/ppermute | solution.py:25
  132.2 9.5 %collective-permute-start.3 = (bf16[512,4096]{1,0:T(8,128)(2,1)}, bf16[512,4096]{1,0:T(8,128)(2,1)}, u32[]{:S(2)}, u32[]{:S(2)}) collective-permute-start(bf16[512,4096]{1,0:T(8,128)(2,1)} %bitcast.5.grads_ref.refs_2_), channel_id=1, source_target_pairs={{0,64},{64,0},{1,65},{65,1},{2,66},{66,2},{3,67},{67,3},{4,68},{68... | collective-permute-start | bytes 12582920 | tf_op jit(solution)/shard_map/ppermute | solution.py:25
  132.2 64.6 %all-to-all-start.2 = ((bf16[64,8,4096]{2,1,0:T(8,128)(2,1)}), bf16[64,8,4096]{2,1,0:T(8,128)(2,1)}, u32[]{:S(2)}, u32[]{:S(2)}) async-start(bf16[64,8,4096]{2,1,0:T(8,128)(2,1)} %bitcast.33), calls=%async_computation.2 | async-start | bytes 8388608 | tf_op jit(solution)/shard_map/all_to_all | solution.py:31
  141.7 1.9 copy-start.2
  143.6 1.9 copy-start.5
  145.5 12.0 %copy-start.8 = (s32[2,128]{1,0:T(2,128)S(1)}, s32[2,128]{1,0:T(2,128)}, u32[]{:S(2)}) copy-start(s32[2,128]{1,0:T(2,128)} %get-tuple-element.60) | copy-start | bytes 3076
  145.5 12.1 %copy-start.7 = (f32[2,128]{1,0:T(2,128)S(1)}, f32[2,128]{1,0:T(2,128)}, u32[]{:S(2)}) copy-start(f32[2,128]{1,0:T(2,128)} %get-tuple-element.61) | copy-start | bytes 3076
  156.9 22.2 %collective-permute-start.4 = (bf16[256,4096]{1,0:T(8,128)(2,1)}, bf16[256,4096]{1,0:T(8,128)(2,1)}, u32[]{:S(2)}, u32[]{:S(2)}) collective-permute-start(bf16[256,4096]{1,0:T(8,128)(2,1)} %get-tuple-element.58), channel_id=1, source_target_pairs={{0,64},{64,0},{1,65},{65,1},{2,66},{66,2},{3,67},{67,3},{4,68},{68... | collective-permute-start | bytes 6291464 | tf_op jit(solution)/shard_map/ppermute | solution.py:25
  157.2 21.9 %collective-permute-start.5 = (bf16[256,4096]{1,0:T(8,128)(2,1)}, bf16[256,4096]{1,0:T(8,128)(2,1)}, u32[]{:S(2)}, u32[]{:S(2)}) collective-permute-start(bf16[256,4096]{1,0:T(8,128)(2,1)} %get-tuple-element.59), channel_id=1, source_target_pairs={{0,64},{64,0},{1,65},{65,1},{2,66},{66,2},{3,67},{67,3},{4,68},{68... | collective-permute-start | bytes 6291464 | tf_op jit(solution)/shard_map/ppermute | solution.py:25
  162.8 16.3 %copy-start.3 = (bf16[1,4096,384]{2,1,0:T(8,128)(2,1)S(1)}, bf16[1,4096,384]{2,1,0:T(8,128)(2,1)}, u32[]{:S(2)}) copy-start(bf16[1,4096,384]{2,1,0:T(8,128)(2,1)} %param.11) | copy-start | bytes 9437188
  162.8 16.3 %copy-start.6 = (bf16[1,4096,384]{2,1,0:T(8,128)(2,1)S(1)}, bf16[1,4096,384]{2,1,0:T(8,128)(2,1)}, u32[]{:S(2)}) copy-start(bf16[1,4096,384]{2,1,0:T(8,128)(2,1)} %param.12) | copy-start | bytes 9437188

commit v7 on v6

--- a/solution.py
+++ b/solution.py
@@ -8,10 +8,10 @@
 from jax.sharding import PartitionSpec as P
 
 HOT = 4
-COLUMNS = 512
+COLUMNS = 1024
 BROAD = 2048
 PARTS = 2
-STEPS = 4
+STEPS = 2
 BF16 = jnp.bfloat16
 F32 = jnp.float32
 MIB = 1024 * 1024
@@ -52,6 +52,10 @@
 
 def whole(arg):
     return arg, pl.BlockSpec(memory_space=pltpu.VMEM)
+
+
+def resident(arg):
+    return pin(arg), pl.BlockSpec(arg.shape, lambda i: (0, 0), pipeline_mode=pl.Buffered(1))
 
 
 def fixed(arg):
@@ -254,6 +258,7 @@
     grads_own = exchange(send_grads, experts)
 
     weights = [whole(matrix) for matrix in (gate_matrix, up_matrix, down_matrix)]
+    own_weights = [resident(matrix) for matrix in (gate_matrix, up_matrix, down_matrix)]
     kept = [out_rows(local_rows, width, kind, PARTS) for kind in (BF16, F32, F32)]
     pair = [out_rows(local_rows, width, BF16, PARTS)] * 2
     part = (local_rows // PARTS, features)
@@ -284,7 +289,7 @@
     )
     gate_peer, up_peer, *ins = call(
         backward_kernel,
-        [by_rows(value, PARTS) for value in (grads_peer, act_peer, slope_peer)] + weights,
+        [by_rows(value, PARTS) for value in (grads_peer, act_peer, slope_peer)] + own_weights,
         pair + parts,
         44,
         **halves,

time: 264 us -> 264 us (level)
  waiting for transfers between devices: 33.6 us -> 38.3 us
  local copies, waits for them, and re-layouts: 7.8 us -> 4.03 us
    all_to_all x2, waiting for transfers between devices: 32.5 us -> 37.2 us  [exchange(): lax.all_to_all(parts, 'expert', split_axis=0, concat_axis=0, tiled=True)]
    unnamed x18 -> x16, local copies, waits for them, and re-layouts: 7.57 us -> 3.8 us
  transfers between devices with their start and end apart: 8 -> 8, of which waited for: 3 -> 3; matrix products, arithmetic and copies ran while one was open for 0% -> 0% of each run, Pallas kernels for 26% -> 25%
where the time goes in v7:
time: 264 us
  blocking collectives  126 us (48%)
  Pallas kernels  77.1 us (29%)
  waiting for transfers between devices  38.3 us (15%)
  starting transfers between devices  17.3 us (7%)
  local copies, waits for them, and re-layouts  4.03 us (2%)
    all_to_all x2, blocking collectives, exchange(): lax.all_to_all(parts, 'expert', split_axis=0, concat_axis=0, tiled=True)  126 us
    pallas_call x9, Pallas kernels, call(): pl.pallas_call(kernel, grid=grid, in_specs=in_specs, out_specs=[spec for...  77.1 us
    all_to_all x2, waiting for transfers between devices, exchange(): lax.all_to_all(parts, 'expert', split_axis=0, concat_axis=0, tiled=True)  37.2 us
    all_to_all x2, starting transfers between devices, exchange(): lax.all_to_all(parts, 'expert', split_axis=0, concat_axis=0, tiled=True)  16.1 us
  transfers between devices with their start and end apart: 8, of which 3 were waited for; matrix products, arithmetic and copies ran while one was open for 0% of the time, Pallas kernels for 25%

profile of v7, /device:TPU:0, one launch (start us, length us, event | category | flops | bytes accessed | tf_op | source)
XLA Modules:
  0.0 263.8 jit_solution(7653455107100488077)
XLA Ops:
  0.6 5.8 %shard_map.110 = (s32[2,128]{1,0:T(2,128)}, f32[2,128]{1,0:T(2,128)}, bf16[512,4096]{1,0:T(8,128)(2,1)}, bf16[512,4096]{1,0:T(8,128)(2,1)}) custom-call(s32[2,128]{1,0:T(2,128)} %bitcast.37, f32[2,128]{1,0:T(2,128)} %bitcast.38, bf16[128,4096]{1,0:T(8,128)(2,1)} %tokens_ref.1, bf16[128,4096]{1,0:T(8,128)(2,1)} %cotangent_ref.1), custom_call_target="tpu_custom_call" | custom-call | flops 1000 | bytes 1000 | tf_op jit(solution)/shard_map/pallas_call | solution.py:37
  6.4 64.2 %all_to_all.20 = bf16[64,8,4096]{2,1,0:T(8,128)(2,1)} all-to-all(bf16[64,8,4096]{2,1,0:T(8,128)(2,1)} %bitcast.36), channel_id=1, replica_groups=mesh['dp'=2,'expert'=64] {'expert'}, dimensions={0} | all-to-all | bytes 8388608 | tf_op jit(solution)/shard_map/all_to_all | solution.py:31
  70.6 0.0 collective-permute-start
  70.6 0.0 copy-start
  70.6 6.4 %all-to-all-start.1 = ((bf16[64,8,4096]{2,1,0:T(8,128)(2,1)}), bf16[64,8,4096]{2,1,0:T(8,128)(2,1)}, u32[]{:S(2)}, u32[]{:S(2)}) async-start(bf16[64,8,4096]{2,1,0:T(8,128)(2,1)} %bitcast.35), calls=%async_computation.1 | async-start | bytes 8388608 | tf_op jit(solution)/shard_map/all_to_all | solution.py:31
  77.0 1.1 collective-permute-done.rows_ref.refs_1_
  78.1 0.0 copy-done
  78.1 0.0 copy-start.2
  78.1 1.9 copy-done.2
  80.0 0.0 copy-start.4
  80.0 1.9 copy-done.4
  81.9 11.4 %shard_map.112 = (bf16[512,384]{1,0:T(8,128)(2,1)}, f32[512,384]{1,0:T(8,128)}, f32[512,384]{1,0:T(8,128)}, bf16[256,4096]{1,0:T(8,128)(2,1)}, bf16[256,4096]{1,0:T(8,128)(2,1)}) custom-call(bf16[512,4096]{1,0:T(8,128)(2,1)} %collective-permute-done.rows_ref.refs_1_, bf16[4096,384]{1,0:T(8,128)(2,1)S(1)} %bitcast.23, bf16[4096,384]{1,0:T(8,128)(2,1)S(1)} %bitcast.27, ...), custom_call_target="tpu_custom_call" | custom-call | flops 1000 | bytes 1000 | tf_op jit(solution)/shard_map/pallas_call | solution.py:37
  93.3 0.2 collective-permute-start.1
  93.5 0.4 collective-permute-start.2
  93.9 7.2 %shard_map.111 = (bf16[512,384]{1,0:T(8,128)(2,1)}, f32[512,384]{1,0:T(8,128)}, f32[512,384]{1,0:T(8,128)}) custom-call(bf16[512,4096]{1,0:T(8,128)(2,1)} %bitcast.3.rows_ref.refs_0_, bf16[4096,384]{1,0:T(8,128)(2,1)S(1)} %bitcast.24, bf16[4096,384]{1,0:T(8,128)(2,1)S(1)} %bitcast.28), custom_call_target="tpu_custom_call" | custom-call | flops 1000 | bytes 1000 | tf_op jit(solution)/shard_map/pallas_call | solution.py:37
  101.1 0.0 collective-permute-done.1.refs_0_
  101.1 0.0 collective-permute-done.2.refs_1_
  101.1 4.8 %shard_map.113 = bf16[512,4096]{1,0:T(8,128)(2,1)} custom-call(bf16[512,384]{1,0:T(8,128)(2,1)} %get-tuple-element.47.hidden_ref.refs_4_, bf16[384,4096]{1,0:T(8,128)(2,1)S(1)} %bitcast.20, bf16[256,4096]{1,0:T(8,128)(2,1)S(1)} %collective-permute-done.1.refs_0_, bf16[256,4096]{1,0:T(8,128)(2,1)S(1)} %collective-permute-done.2.refs_1_), custom_call_target="tpu_custom_call" | custom-call | flops 1000 | bytes 1000 | tf_op jit(solution)/shard_map/pallas_call | solution.py:37
  105.9 26.4 %all-to-all-done.1 = bf16[64,8,4096]{2,1,0:T(8,128)(2,1)} async-done(((bf16[64,8,4096]{2,1,0:T(8,128)(2,1)}), bf16[64,8,4096]{2,1,0:T(8,128)(2,1)}, u32[]{:S(2)}, u32[]{:S(2)}) %all-to-all-start.1) | async-done | bytes 4194336 | tf_op jit(solution)/shard_map/all_to_all | solution.py:31
  132.3 0.0 collective-permute-start.3
  132.3 9.7 %all-to-all-start.2 = ((bf16[64,8,4096]{2,1,0:T(8,128)(2,1)}), bf16[64,8,4096]{2,1,0:T(8,128)(2,1)}, u32[]{:S(2)}, u32[]{:S(2)}) async-start(bf16[64,8,4096]{2,1,0:T(8,128)(2,1)} %bitcast.33), calls=%async_computation.2 | async-start | bytes 8388608 | tf_op jit(solution)/shard_map/all_to_all | solution.py:31
  142.0 0.0 collective-permute-done.3.grads_ref.refs_3_
  142.0 0.0 copy-start.7
  142.0 0.0 copy-start.6
  142.0 0.0 copy-start.1
  142.0 14.5 %shard_map.115 = (bf16[512,384]{1,0:T(8,128)(2,1)}, bf16[512,384]{1,0:T(8,128)(2,1)}, bf16[256,4096]{1,0:T(8,128)(2,1)}, bf16[256,4096]{1,0:T(8,128)(2,1)}) custom-call(bf16[512,4096]{1,0:T(8,128)(2,1)} %collective-permute-done.3.grads_ref.refs_3_, f32[512,384]{1,0:T(8,128)} %get-tuple-element.56.act_ref, f32[512,384]{1,0:T(8,128)} %get-tuple-element.57.slope_ref, ...), custom_call_target="tpu_custom_call" | custom-call | flops 1000 | bytes 1000 | tf_op jit(solution)/shard_map/pallas_call | solution.py:37
  156.5 0.3 collective-permute-start.4
  156.8 0.3 collective-permute-start.5
  157.1 0.0 copy-done.7
  157.1 0.1 copy.12
  157.2 0.0 copy-done.6
  157.2 0.1 copy.13
  157.4 0.0 copy-done.1
  157.4 5.1 %shard_map.114 = (bf16[512,384]{1,0:T(8,128)(2,1)}, bf16[512,384]{1,0:T(8,128)(2,1)}) custom-call(bf16[512,4096]{1,0:T(8,128)(2,1)} %bitcast.5.grads_ref.refs_2_, f32[512,384]{1,0:T(8,128)} %get-tuple-element.52.act_ref, f32[512,384]{1,0:T(8,128)} %get-tuple-element.53.slope_ref, bf16[384,4096]{1,0:T(8,128)(2,1)S(1)} %bitcast.21), custom_call_target="tpu_custom_call" | custom-call | flops 1000 | bytes 1000 | tf_op jit(solution)/shard_map/pallas_call | solution.py:37
  162.5 0.0 copy-start.3
  162.5 0.0 copy-start.5
  162.5 15.1 %shard_map.117 = (bf16[4096,384]{1,0:T(8,128)(2,1)}, bf16[4096,384]{1,0:T(8,128)(2,1)}, bf16[384,4096]{1,0:T(8,128)(2,1)}) custom-call(bf16[512,4096]{1,0:T(8,128)(2,1)} %bitcast.3.rows_ref.refs_0_, bf16[512,4096]{1,0:T(8,128)(2,1)} %collective-permute-done.rows_ref.refs_1_, bf16[512,4096]{1,0:T(8,128)(2,1)} %bitcast.5.grads_ref.refs_2_, ...), custom_call_target="tpu_custom_call" | custom-call | flops 1000 | bytes 1000 | tf_op jit(solution)/shard_map/pallas_call | solution.py:37
  177.5 0.0 collective-permute-done.4.refs_0_
  177.5 0.0 collective-permute-done.5.refs_1_
  177.5 0.0 copy-done.3
  177.6 0.0 copy-done.5
  177.6 8.6 %shard_map.116 = bf16[512,4096]{1,0:T(8,128)(2,1)} custom-call(bf16[512,384]{1,0:T(8,128)(2,1)} %get-tuple-element.54.gate_grad_ref.refs_6_, bf16[512,384]{1,0:T(8,128)(2,1)} %get-tuple-element.55.up_grad_ref.refs_8_, bf16[4096,384]{1,0:T(8,128)(2,1)S(1)} %bitcast.25, bf16[4096,384]{1,0:T(8,128)(2,1)S(1)} %bitcast.29, ...), custom_call_target="tpu_custom_call" | custom-call | flops 1000 | bytes 1000 | tf_op jit(solution)/shard_map/pallas_call | solution.py:37
  186.2 10.9 %all-to-all-done.2 = bf16[64,8,4096]{2,1,0:T(8,128)(2,1)} async-done(((bf16[64,8,4096]{2,1,0:T(8,128)(2,1)}), bf16[64,8,4096]{2,1,0:T(8,128)(2,1)}, u32[]{:S(2)}, u32[]{:S(2)}) %all-to-all-start.2) | async-done | bytes 4194336 | tf_op jit(solution)/shard_map/all_to_all | solution.py:31
  197.0 62.2 %all_to_all.21 = bf16[64,8,4096]{2,1,0:T(8,128)(2,1)S(1)} all-to-all(bf16[64,8,4096]{2,1,0:T(8,128)(2,1)} %bitcast.34), channel_id=1, replica_groups=mesh['dp'=2,'expert'=64] {'expert'}, dimensions={0} | all-to-all | bytes 8388608 | tf_op jit(solution)/shard_map/all_to_all | solution.py:31
  259.2 4.6 %shard_map.118 = (bf16[128,4096]{1,0:T(8,128)(2,1)}, bf16[128,4096]{1,0:T(8,128)(2,1)}) custom-call(s32[128,2]{1,0:T(8,128)S(1)} %bitcast.31, f32[128,2]{1,0:T(8,128)S(1)} %bitcast.32, bf16[512,4096]{1,0:T(8,128)(2,1)} %bitcast.10.out_ref, bf16[512,4096]{1,0:T(8,128)(2,1)S(1)} %bitcast.30), custom_call_target="tpu_custom_call" | custom-call | flops 1000 | bytes 1000 | tf_op jit(solution)/shard_map/pallas_call | solution.py:37
Async XLA Ops:
  70.6 7.5 %collective-permute-start = (bf16[512,4096]{1,0:T(8,128)(2,1)}, bf16[512,4096]{1,0:T(8,128)(2,1)}, u32[]{:S(2)}, u32[]{:S(2)}) collective-permute-start(bf16[512,4096]{1,0:T(8,128)(2,1)} %bitcast.3.rows_ref.refs_0_), channel_id=1, source_target_pairs={{0,64},{64,0},{1,65},{65,1},{2,66},{66,2},{3,67},{67,3},{4,68},{68... | collective-permute-start | bytes 12582920 | tf_op jit(solution)/shard_map/ppermute | solution.py:25
  70.6 7.5 %copy-start = (bf16[1,384,4096]{2,1,0:T(8,128)(2,1)S(1)}, bf16[1,384,4096]{2,1,0:T(8,128)(2,1)}, u32[]{:S(2)}) copy-start(bf16[1,384,4096]{2,1,0:T(8,128)(2,1)} %param.13) | copy-start | bytes 9437188
  70.6 61.7 %all-to-all-start.1 = ((bf16[64,8,4096]{2,1,0:T(8,128)(2,1)}), bf16[64,8,4096]{2,1,0:T(8,128)(2,1)}, u32[]{:S(2)}, u32[]{:S(2)}) async-start(bf16[64,8,4096]{2,1,0:T(8,128)(2,1)} %bitcast.35), calls=%async_computation.1 | async-start | bytes 8388608 | tf_op jit(solution)/shard_map/all_to_all | solution.py:31
  78.1 1.9 copy-start.2
  80.0 1.9 copy-start.4
  93.3 7.8 %collective-permute-start.1 = (bf16[256,4096]{1,0:T(8,128)(2,1)}, bf16[256,4096]{1,0:T(8,128)(2,1)S(1)}, u32[]{:S(2)}, u32[]{:S(2)}) collective-permute-start(bf16[256,4096]{1,0:T(8,128)(2,1)} %get-tuple-element.48), channel_id=1, source_target_pairs={{0,64},{64,0},{1,65},{65,1},{2,66},{66,2},{3,67},{67,3},{4,68},{68... | collective-permute-start | bytes 6291464 | tf_op jit(solution)/shard_map/ppermute | solution.py:25
  93.5 7.6 %collective-permute-start.2 = (bf16[256,4096]{1,0:T(8,128)(2,1)}, bf16[256,4096]{1,0:T(8,128)(2,1)S(1)}, u32[]{:S(2)}, u32[]{:S(2)}) collective-permute-start(bf16[256,4096]{1,0:T(8,128)(2,1)} %get-tuple-element.49), channel_id=1, source_target_pairs={{0,64},{64,0},{1,65},{65,1},{2,66},{66,2},{3,67},{67,3},{4,68},{68... | collective-permute-start | bytes 6291464 | tf_op jit(solution)/shard_map/ppermute | solution.py:25
  132.3 9.7 %collective-permute-start.3 = (bf16[512,4096]{1,0:T(8,128)(2,1)}, bf16[512,4096]{1,0:T(8,128)(2,1)}, u32[]{:S(2)}, u32[]{:S(2)}) collective-permute-start(bf16[512,4096]{1,0:T(8,128)(2,1)} %bitcast.5.grads_ref.refs_2_), channel_id=1, source_target_pairs={{0,64},{64,0},{1,65},{65,1},{2,66},{66,2},{3,67},{67,3},{4,68},{68... | collective-permute-start | bytes 12582920 | tf_op jit(solution)/shard_map/ppermute | solution.py:25
  132.3 64.7 %all-to-all-start.2 = ((bf16[64,8,4096]{2,1,0:T(8,128)(2,1)}), bf16[64,8,4096]{2,1,0:T(8,128)(2,1)}, u32[]{:S(2)}, u32[]{:S(2)}) async-start(bf16[64,8,4096]{2,1,0:T(8,128)(2,1)} %bitcast.33), calls=%async_computation.2 | async-start | bytes 8388608 | tf_op jit(solution)/shard_map/all_to_all | solution.py:31
  142.0 15.2 %copy-start.7 = (s32[2,128]{1,0:T(2,128)S(1)}, s32[2,128]{1,0:T(2,128)}, u32[]{:S(2)}) copy-start(s32[2,128]{1,0:T(2,128)} %get-tuple-element.60) | copy-start | bytes 3076
  142.0 15.3 %copy-start.6 = (f32[2,128]{1,0:T(2,128)S(1)}, f32[2,128]{1,0:T(2,128)}, u32[]{:S(2)}) copy-start(f32[2,128]{1,0:T(2,128)} %get-tuple-element.61) | copy-start | bytes 3076
  142.0 15.4 %copy-start.1 = (bf16[1,384,4096]{2,1,0:T(8,128)(2,1)S(1)}, bf16[1,384,4096]{2,1,0:T(8,128)(2,1)}, u32[]{:S(2)}) copy-start(bf16[1,384,4096]{2,1,0:T(8,128)(2,1)} %param.13) | copy-start | bytes 9437188
  156.5 21.0 %collective-permute-start.4 = (bf16[256,4096]{1,0:T(8,128)(2,1)}, bf16[256,4096]{1,0:T(8,128)(2,1)}, u32[]{:S(2)}, u32[]{:S(2)}) collective-permute-start(bf16[256,4096]{1,0:T(8,128)(2,1)} %get-tuple-element.58), channel_id=1, source_target_pairs={{0,64},{64,0},{1,65},{65,1},{2,66},{66,2},{3,67},{67,3},{4,68},{68... | collective-permute-start | bytes 6291464 | tf_op jit(solution)/shard_map/ppermute | solution.py:25
  156.8 20.7 %collective-permute-start.5 = (bf16[256,4096]{1,0:T(8,128)(2,1)}, bf16[256,4096]{1,0:T(8,128)(2,1)}, u32[]{:S(2)}, u32[]{:S(2)}) collective-permute-start(bf16[256,4096]{1,0:T(8,128)(2,1)} %get-tuple-element.59), channel_id=1, source_target_pairs={{0,64},{64,0},{1,65},{65,1},{2,66},{66,2},{3,67},{67,3},{4,68},{68... | collective-permute-start | bytes 6291464 | tf_op jit(solution)/shard_map/ppermute | solution.py:25
  162.5 15.1 %copy-start.3 = (bf16[1,4096,384]{2,1,0:T(8,128)(2,1)S(1)}, bf16[1,4096,384]{2,1,0:T(8,128)(2,1)}, u32[]{:S(2)}) copy-start(bf16[1,4096,384]{2,1,0:T(8,128)(2,1)} %param.11) | copy-start | bytes 9437188
  162.5 15.1 %copy-start.5 = (bf16[1,4096,384]{2,1,0:T(8,128)(2,1)S(1)}, bf16[1,4096,384]{2,1,0:T(8,128)(2,1)}, u32[]{:S(2)}) copy-start(bf16[1,4096,384]{2,1,0:T(8,128)(2,1)} %param.12) | copy-start | bytes 9437188

commit v8 on v7

--- a/solution.py
+++ b/solution.py
@@ -39,7 +39,10 @@
         grid=grid,
         in_specs=in_specs,
         out_specs=[spec for _, _, spec in outs],
-        out_shape=[(pltpu.HBM if pinned else jax.ShapeDtypeStruct)(shape, kind) for shape, kind, _ in outs],
+        out_shape=[
+            (pltpu.HBM if pinned and spec.memory_space is None else jax.ShapeDtypeStruct)(shape, kind)
+            for shape, kind, spec in outs
+        ],
         scratch_shapes=scratch,
         compiler_params=pltpu.CompilerParams(vmem_limit_bytes=limit * MIB),
         cost_estimate=pl.CostEstimate(flops=1000, bytes_accessed=1000, transcendentals=0),
@@ -138,7 +141,9 @@
         scale = sum(jnp.where(hits[column], weight_ref[column : column + 1], 0.0) for column in columns)
         scale_ref[...] = jnp.broadcast_to(jnp.sum(scale, axis=1, keepdims=True), scale_ref.shape)
 
-    rows_ref[...] = dot(pick_ref[...], tokens_ref[...], ((1,), (0,))).astype(BF16)
+    columns = tokens_ref.shape[1]
+    here = pl.ds(pl.multiple_of(pl.program_id(0) * columns, columns), columns)
+    rows_ref[:, here] = dot(pick_ref[...], tokens_ref[...], ((1,), (0,))).astype(BF16)
     grads = dot(pick_ref[...], cotangent_ref[...], ((1,), (0,)))
     grads_ref[...] = (scale_ref[:, :1] * grads).astype(BF16)
 
@@ -244,7 +249,7 @@
     position, route_weights, send_rows, send_grads = call(
         functools.partial(dispatch_kernel, experts=experts, capacity=capacity),
         [fixed(pin(routing.T)), fixed(pin(combine_weights.T)), across(pin(tokens), BROAD), across(pin(cotangent), BROAD)],
-        [(place_shape, kind, pl.BlockSpec(place_shape, lambda i: (0, 0))) for kind in (jnp.int32, F32)] + [sent, sent],
+        [(place_shape, kind, pl.BlockSpec(place_shape, lambda i: (0, 0))) for kind in (jnp.int32, F32)] + [((local_rows, features), BF16, pl.BlockSpec(memory_space=pltpu.VMEM)), sent],
         40,
         grid=broad_grid,
         scratch=[pltpu.VMEM((local_rows, tok_rows), BF16), pltpu.VMEM((local_rows, 128), F32)],

time: 264 us -> 264 us (level)
  no operation moved by 1% of the time
where the time goes in v8:
time: 264 us; the launch traced here: 263 us
  blocking collectives  126 us (48%)
  Pallas kernels  76.8 us (29%)
  waiting for transfers between devices  38.3 us (15%)
  starting transfers between devices  17.3 us (7%)
  local copies, waits for them, and re-layouts  4.03 us (2%)
    all_to_all x2, blocking collectives, exchange(): lax.all_to_all(parts, 'expert', split_axis=0, concat_axis=0, tiled=True)  126 us
    pallas_call x9, Pallas kernels, call(): pl.pallas_call(kernel, grid=grid, in_specs=in_specs, out_specs=[spec for...  76.8 us
    all_to_all x2, waiting for transfers between devices, exchange(): lax.all_to_all(parts, 'expert', split_axis=0, concat_axis=0, tiled=True)  37.2 us
    all_to_all x2, starting transfers between devices, exchange(): lax.all_to_all(parts, 'expert', split_axis=0, concat_axis=0, tiled=True)  16.1 us
  transfers between devices with their start and end apart: 8, of which 3 were waited for; matrix products, arithmetic and copies ran while one was open for 0% of the time, Pallas kernels for 25%

profile of v8, /device:TPU:0, one launch (start us, length us, event | category | flops | bytes accessed | tf_op | source)
XLA Modules:
  0.0 263.3 jit_solution(1884668931323809900)
XLA Ops:
  0.6 5.5 %shard_map.110 = (s32[2,128]{1,0:T(2,128)}, f32[2,128]{1,0:T(2,128)}, bf16[512,4096]{1,0:T(8,128)(2,1)S(1)}, bf16[512,4096]{1,0:T(8,128)(2,1)}) custom-call(s32[2,128]{1,0:T(2,128)} %bitcast.37, f32[2,128]{1,0:T(2,128)} %bitcast.38, bf16[128,4096]{1,0:T(8,128)(2,1)} %tokens_ref.1, bf16[128,4096]{1,0:T(8,128)(2,1)} %cotangent_ref.1), custom_call_target="tpu_custom_call" | custom-call | flops 1000 | bytes 1000 | tf_op jit(solution)/shard_map/pallas_call | solution.py:37
  6.1 63.9 %all_to_all.20 = bf16[64,8,4096]{2,1,0:T(8,128)(2,1)} all-to-all(bf16[64,8,4096]{2,1,0:T(8,128)(2,1)S(1)} %bitcast.31), channel_id=1, replica_groups=mesh['dp'=2,'expert'=64] {'expert'}, dimensions={0} | all-to-all | bytes 8388608 | tf_op jit(solution)/shard_map/all_to_all | solution.py:31
  70.1 0.0 collective-permute-start
  70.1 0.0 copy-start
  70.1 6.4 %all-to-all-start.1 = ((bf16[64,8,4096]{2,1,0:T(8,128)(2,1)}), bf16[64,8,4096]{2,1,0:T(8,128)(2,1)}, u32[]{:S(2)}, u32[]{:S(2)}) async-start(bf16[64,8,4096]{2,1,0:T(8,128)(2,1)} %bitcast.36), calls=%async_computation.1 | async-start | bytes 8388608 | tf_op jit(solution)/shard_map/all_to_all | solution.py:31
  76.5 1.1 collective-permute-done.rows_ref.refs_1_
  77.6 0.0 copy-done
  77.6 0.0 copy-start.2
  77.6 1.9 copy-done.2
  79.5 0.0 copy-start.4
  79.5 1.9 copy-done.4
  81.4 11.4 %shard_map.112 = (bf16[512,384]{1,0:T(8,128)(2,1)}, f32[512,384]{1,0:T(8,128)}, f32[512,384]{1,0:T(8,128)}, bf16[256,4096]{1,0:T(8,128)(2,1)}, bf16[256,4096]{1,0:T(8,128)(2,1)}) custom-call(bf16[512,4096]{1,0:T(8,128)(2,1)} %collective-permute-done.rows_ref.refs_1_, bf16[4096,384]{1,0:T(8,128)(2,1)S(1)} %bitcast.23, bf16[4096,384]{1,0:T(8,128)(2,1)S(1)} %bitcast.27, ...), custom_call_target="tpu_custom_call" | custom-call | flops 1000 | bytes 1000 | tf_op jit(solution)/shard_map/pallas_call | solution.py:37
  92.8 0.2 collective-permute-start.1
  93.0 0.4 collective-permute-start.2
  93.4 7.2 %shard_map.111 = (bf16[512,384]{1,0:T(8,128)(2,1)}, f32[512,384]{1,0:T(8,128)}, f32[512,384]{1,0:T(8,128)}) custom-call(bf16[512,4096]{1,0:T(8,128)(2,1)} %bitcast.3.rows_ref.refs_0_, bf16[4096,384]{1,0:T(8,128)(2,1)S(1)} %bitcast.24, bf16[4096,384]{1,0:T(8,128)(2,1)S(1)} %bitcast.28), custom_call_target="tpu_custom_call" | custom-call | flops 1000 | bytes 1000 | tf_op jit(solution)/shard_map/pallas_call | solution.py:37
  100.6 0.0 collective-permute-done.1.refs_0_
  100.6 0.0 collective-permute-done.2.refs_1_
  100.6 4.8 %shard_map.113 = bf16[512,4096]{1,0:T(8,128)(2,1)} custom-call(bf16[512,384]{1,0:T(8,128)(2,1)} %get-tuple-element.47.hidden_ref.refs_4_, bf16[384,4096]{1,0:T(8,128)(2,1)S(1)} %bitcast.20, bf16[256,4096]{1,0:T(8,128)(2,1)S(1)} %collective-permute-done.1.refs_0_, bf16[256,4096]{1,0:T(8,128)(2,1)S(1)} %collective-permute-done.2.refs_1_), custom_call_target="tpu_custom_call" | custom-call | flops 1000 | bytes 1000 | tf_op jit(solution)/shard_map/pallas_call | solution.py:37
  105.4 26.4 %all-to-all-done.1 = bf16[64,8,4096]{2,1,0:T(8,128)(2,1)} async-done(((bf16[64,8,4096]{2,1,0:T(8,128)(2,1)}), bf16[64,8,4096]{2,1,0:T(8,128)(2,1)}, u32[]{:S(2)}, u32[]{:S(2)}) %all-to-all-start.1) | async-done | bytes 4194336 | tf_op jit(solution)/shard_map/all_to_all | solution.py:31
  131.8 0.0 collective-permute-start.3
  131.8 9.7 %all-to-all-start.2 = ((bf16[64,8,4096]{2,1,0:T(8,128)(2,1)}), bf16[64,8,4096]{2,1,0:T(8,128)(2,1)}, u32[]{:S(2)}, u32[]{:S(2)}) async-start(bf16[64,8,4096]{2,1,0:T(8,128)(2,1)} %bitcast.34), calls=%async_computation.2 | async-start | bytes 8388608 | tf_op jit(solution)/shard_map/all_to_all | solution.py:31
  141.5 0.0 collective-permute-done.3.grads_ref.refs_3_
  141.5 0.0 copy-start.7
  141.5 0.0 copy-start.6
  141.5 0.0 copy-start.1
  141.5 14.5 %shard_map.115 = (bf16[512,384]{1,0:T(8,128)(2,1)}, bf16[512,384]{1,0:T(8,128)(2,1)}, bf16[256,4096]{1,0:T(8,128)(2,1)}, bf16[256,4096]{1,0:T(8,128)(2,1)}) custom-call(bf16[512,4096]{1,0:T(8,128)(2,1)} %collective-permute-done.3.grads_ref.refs_3_, f32[512,384]{1,0:T(8,128)} %get-tuple-element.56.act_ref, f32[512,384]{1,0:T(8,128)} %get-tuple-element.57.slope_ref, ...), custom_call_target="tpu_custom_call" | custom-call | flops 1000 | bytes 1000 | tf_op jit(solution)/shard_map/pallas_call | solution.py:37
  156.0 0.3 collective-permute-start.4
  156.3 0.3 collective-permute-start.5
  156.6 0.0 copy-done.7
  156.6 0.1 copy.12
  156.7 0.0 copy-done.6
  156.7 0.1 copy.13
  156.9 0.0 copy-done.1
  156.9 5.1 %shard_map.114 = (bf16[512,384]{1,0:T(8,128)(2,1)}, bf16[512,384]{1,0:T(8,128)(2,1)}) custom-call(bf16[512,4096]{1,0:T(8,128)(2,1)} %bitcast.5.grads_ref.refs_2_, f32[512,384]{1,0:T(8,128)} %get-tuple-element.52.act_ref, f32[512,384]{1,0:T(8,128)} %get-tuple-element.53.slope_ref, bf16[384,4096]{1,0:T(8,128)(2,1)S(1)} %bitcast.21), custom_call_target="tpu_custom_call" | custom-call | flops 1000 | bytes 1000 | tf_op jit(solution)/shard_map/pallas_call | solution.py:37
  162.0 0.0 copy-start.3
  162.0 0.0 copy-start.5
  162.0 15.1 %shard_map.117 = (bf16[4096,384]{1,0:T(8,128)(2,1)}, bf16[4096,384]{1,0:T(8,128)(2,1)}, bf16[384,4096]{1,0:T(8,128)(2,1)}) custom-call(bf16[512,4096]{1,0:T(8,128)(2,1)} %bitcast.3.rows_ref.refs_0_, bf16[512,4096]{1,0:T(8,128)(2,1)} %collective-permute-done.rows_ref.refs_1_, bf16[512,4096]{1,0:T(8,128)(2,1)} %bitcast.5.grads_ref.refs_2_, ...), custom_call_target="tpu_custom_call" | custom-call | flops 1000 | bytes 1000 | tf_op jit(solution)/shard_map/pallas_call | solution.py:37
  177.1 0.0 collective-permute-done.4.refs_0_
  177.1 0.0 collective-permute-done.5.refs_1_
  177.1 0.0 copy-done.3
  177.1 0.0 copy-done.5
  177.1 8.6 %shard_map.116 = bf16[512,4096]{1,0:T(8,128)(2,1)} custom-call(bf16[512,384]{1,0:T(8,128)(2,1)} %get-tuple-element.54.gate_grad_ref.refs_6_, bf16[512,384]{1,0:T(8,128)(2,1)} %get-tuple-element.55.up_grad_ref.refs_8_, bf16[4096,384]{1,0:T(8,128)(2,1)S(1)} %bitcast.25, bf16[4096,384]{1,0:T(8,128)(2,1)S(1)} %bitcast.29, ...), custom_call_target="tpu_custom_call" | custom-call | flops 1000 | bytes 1000 | tf_op jit(solution)/shard_map/pallas_call | solution.py:37
  185.7 10.9 %all-to-all-done.2 = bf16[64,8,4096]{2,1,0:T(8,128)(2,1)} async-done(((bf16[64,8,4096]{2,1,0:T(8,128)(2,1)}), bf16[64,8,4096]{2,1,0:T(8,128)(2,1)}, u32[]{:S(2)}, u32[]{:S(2)}) %all-to-all-start.2) | async-done | bytes 4194336 | tf_op jit(solution)/shard_map/all_to_all | solution.py:31
  196.5 62.2 %all_to_all.21 = bf16[64,8,4096]{2,1,0:T(8,128)(2,1)S(1)} all-to-all(bf16[64,8,4096]{2,1,0:T(8,128)(2,1)} %bitcast.35), channel_id=1, replica_groups=mesh['dp'=2,'expert'=64] {'expert'}, dimensions={0} | all-to-all | bytes 8388608 | tf_op jit(solution)/shard_map/all_to_all | solution.py:31
  258.8 4.6 %shard_map.118 = (bf16[128,4096]{1,0:T(8,128)(2,1)}, bf16[128,4096]{1,0:T(8,128)(2,1)}) custom-call(s32[128,2]{1,0:T(8,128)S(1)} %bitcast.32, f32[128,2]{1,0:T(8,128)S(1)} %bitcast.33, bf16[512,4096]{1,0:T(8,128)(2,1)} %bitcast.10.out_ref, bf16[512,4096]{1,0:T(8,128)(2,1)S(1)} %bitcast.30), custom_call_target="tpu_custom_call" | custom-call | flops 1000 | bytes 1000 | tf_op jit(solution)/shard_map/pallas_call | solution.py:37
Async XLA Ops:
  70.1 7.5 %collective-permute-start = (bf16[512,4096]{1,0:T(8,128)(2,1)}, bf16[512,4096]{1,0:T(8,128)(2,1)}, u32[]{:S(2)}, u32[]{:S(2)}) collective-permute-start(bf16[512,4096]{1,0:T(8,128)(2,1)} %bitcast.3.rows_ref.refs_0_), channel_id=1, source_target_pairs={{0,64},{64,0},{1,65},{65,1},{2,66},{66,2},{3,67},{67,3},{4,68},{68... | collective-permute-start | bytes 12582920 | tf_op jit(solution)/shard_map/ppermute | solution.py:25
  70.1 7.5 %copy-start = (bf16[1,384,4096]{2,1,0:T(8,128)(2,1)S(1)}, bf16[1,384,4096]{2,1,0:T(8,128)(2,1)}, u32[]{:S(2)}) copy-start(bf16[1,384,4096]{2,1,0:T(8,128)(2,1)} %param.13) | copy-start | bytes 9437188
  70.1 61.7 %all-to-all-start.1 = ((bf16[64,8,4096]{2,1,0:T(8,128)(2,1)}), bf16[64,8,4096]{2,1,0:T(8,128)(2,1)}, u32[]{:S(2)}, u32[]{:S(2)}) async-start(bf16[64,8,4096]{2,1,0:T(8,128)(2,1)} %bitcast.36), calls=%async_computation.1 | async-start | bytes 8388608 | tf_op jit(solution)/shard_map/all_to_all | solution.py:31
  77.6 1.9 copy-start.2
  79.5 1.9 copy-start.4
  92.8 7.8 %collective-permute-start.1 = (bf16[256,4096]{1,0:T(8,128)(2,1)}, bf16[256,4096]{1,0:T(8,128)(2,1)S(1)}, u32[]{:S(2)}, u32[]{:S(2)}) collective-permute-start(bf16[256,4096]{1,0:T(8,128)(2,1)} %get-tuple-element.48), channel_id=1, source_target_pairs={{0,64},{64,0},{1,65},{65,1},{2,66},{66,2},{3,67},{67,3},{4,68},{68... | collective-permute-start | bytes 6291464 | tf_op jit(solution)/shard_map/ppermute | solution.py:25
  93.0 7.6 %collective-permute-start.2 = (bf16[256,4096]{1,0:T(8,128)(2,1)}, bf16[256,4096]{1,0:T(8,128)(2,1)S(1)}, u32[]{:S(2)}, u32[]{:S(2)}) collective-permute-start(bf16[256,4096]{1,0:T(8,128)(2,1)} %get-tuple-element.49), channel_id=1, source_target_pairs={{0,64},{64,0},{1,65},{65,1},{2,66},{66,2},{3,67},{67,3},{4,68},{68... | collective-permute-start | bytes 6291464 | tf_op jit(solution)/shard_map/ppermute | solution.py:25
  131.8 9.7 %collective-permute-start.3 = (bf16[512,4096]{1,0:T(8,128)(2,1)}, bf16[512,4096]{1,0:T(8,128)(2,1)}, u32[]{:S(2)}, u32[]{:S(2)}) collective-permute-start(bf16[512,4096]{1,0:T(8,128)(2,1)} %bitcast.5.grads_ref.refs_2_), channel_id=1, source_target_pairs={{0,64},{64,0},{1,65},{65,1},{2,66},{66,2},{3,67},{67,3},{4,68},{68... | collective-permute-start | bytes 12582920 | tf_op jit(solution)/shard_map/ppermute | solution.py:25
  131.8 64.7 %all-to-all-start.2 = ((bf16[64,8,4096]{2,1,0:T(8,128)(2,1)}), bf16[64,8,4096]{2,1,0:T(8,128)(2,1)}, u32[]{:S(2)}, u32[]{:S(2)}) async-start(bf16[64,8,4096]{2,1,0:T(8,128)(2,1)} %bitcast.34), calls=%async_computation.2 | async-start | bytes 8388608 | tf_op jit(solution)/shard_map/all_to_all | solution.py:31
  141.5 15.1 %copy-start.7 = (s32[2,128]{1,0:T(2,128)S(1)}, s32[2,128]{1,0:T(2,128)}, u32[]{:S(2)}) copy-start(s32[2,128]{1,0:T(2,128)} %get-tuple-element.60) | copy-start | bytes 3076
  141.5 15.2 %copy-start.6 = (f32[2,128]{1,0:T(2,128)S(1)}, f32[2,128]{1,0:T(2,128)}, u32[]{:S(2)}) copy-start(f32[2,128]{1,0:T(2,128)} %get-tuple-element.61) | copy-start | bytes 3076
  141.5 15.4 %copy-start.1 = (bf16[1,384,4096]{2,1,0:T(8,128)(2,1)S(1)}, bf16[1,384,4096]{2,1,0:T(8,128)(2,1)}, u32[]{:S(2)}) copy-start(bf16[1,384,4096]{2,1,0:T(8,128)(2,1)} %param.13) | copy-start | bytes 9437188
  156.0 21.0 %collective-permute-start.4 = (bf16[256,4096]{1,0:T(8,128)(2,1)}, bf16[256,4096]{1,0:T(8,128)(2,1)}, u32[]{:S(2)}, u32[]{:S(2)}) collective-permute-start(bf16[256,4096]{1,0:T(8,128)(2,1)} %get-tuple-element.58), channel_id=1, source_target_pairs={{0,64},{64,0},{1,65},{65,1},{2,66},{66,2},{3,67},{67,3},{4,68},{68... | collective-permute-start | bytes 6291464 | tf_op jit(solution)/shard_map/ppermute | solution.py:25
  156.3 20.7 %collective-permute-start.5 = (bf16[256,4096]{1,0:T(8,128)(2,1)}, bf16[256,4096]{1,0:T(8,128)(2,1)}, u32[]{:S(2)}, u32[]{:S(2)}) collective-permute-start(bf16[256,4096]{1,0:T(8,128)(2,1)} %get-tuple-element.59), channel_id=1, source_target_pairs={{0,64},{64,0},{1,65},{65,1},{2,66},{66,2},{3,67},{67,3},{4,68},{68... | collective-permute-start | bytes 6291464 | tf_op jit(solution)/shard_map/ppermute | solution.py:25
  162.0 15.1 %copy-start.3 = (bf16[1,4096,384]{2,1,0:T(8,128)(2,1)S(1)}, bf16[1,4096,384]{2,1,0:T(8,128)(2,1)}, u32[]{:S(2)}) copy-start(bf16[1,4096,384]{2,1,0:T(8,128)(2,1)} %param.11) | copy-start | bytes 9437188
  162.0 15.1 %copy-start.5 = (bf16[1,4096,384]{2,1,0:T(8,128)(2,1)S(1)}, bf16[1,4096,384]{2,1,0:T(8,128)(2,1)}, u32[]{:S(2)}) copy-start(bf16[1,4096,384]{2,1,0:T(8,128)(2,1)} %param.12) | copy-start | bytes 9437188

commit v9 on v8

--- a/solution.py
+++ b/solution.py
@@ -210,7 +210,8 @@
 def input_kernel(gate_grad_ref, up_grad_ref, gate_ref, up_ref, *refs):
     out_ref = refs[-1]
     total = input_parts(gate_grad_ref[...], up_grad_ref[...], gate_ref[...], up_ref[...])
-    out_ref[...] = (total + peer_part(refs[:-1])).astype(BF16)
+    rows = total.shape[0]
+    out_ref[pl.ds(pl.multiple_of(pl.program_id(0) * rows, rows), rows)] = (total + peer_part(refs[:-1])).astype(BF16)
 
 
 def weight_kernel(*refs):
@@ -303,7 +304,7 @@
     (input_send,) = call(
         input_kernel,
         [by_rows(gate_own, STEPS), by_rows(up_own, STEPS)] + weights[:2] + peer_blocks(ins, STEPS),
-        send,
+        [((local_rows, features), BF16, pl.BlockSpec(memory_space=pltpu.VMEM))],
         32,
         **steps,
     )

time: 264 us -> 264 us (level)
    unnamed x16 -> x18, local copies, waits for them, and re-layouts: 3.8 us -> 5.78 us
where the time goes in v9:
time: 264 us; the launch traced here: 263 us
  blocking collectives  126 us (48%)
  Pallas kernels  75.4 us (29%)
  waiting for transfers between devices  37.7 us (14%)
  starting transfers between devices  17.3 us (7%)
  local copies, waits for them, and re-layouts  6.01 us (2%)
    all_to_all x2, blocking collectives, exchange(): lax.all_to_all(parts, 'expert', split_axis=0, concat_axis=0, tiled=True)  126 us
    pallas_call x9, Pallas kernels, call(): pl.pallas_call(kernel, grid=grid, in_specs=in_specs, out_specs=[spec for...  75.4 us
    all_to_all x2, waiting for transfers between devices, exchange(): lax.all_to_all(parts, 'expert', split_axis=0, concat_axis=0, tiled=True)  36.6 us
    all_to_all x2, starting transfers between devices, exchange(): lax.all_to_all(parts, 'expert', split_axis=0, concat_axis=0, tiled=True)  16.1 us
    unnamed x18, local copies, waits for them, and re-layouts  5.78 us
  transfers between devices with their start and end apart: 8, of which 3 were waited for; matrix products, arithmetic and copies ran while one was open for 0% of the time, Pallas kernels for 25%

profile of v9, /device:TPU:0, one launch (start us, length us, event | category | flops | bytes accessed | tf_op | source)
XLA Modules:
  0.0 263.2 jit_solution(6340730737823640099)
XLA Ops:
  0.6 5.4 %shard_map.110 = (s32[2,128]{1,0:T(2,128)}, f32[2,128]{1,0:T(2,128)}, bf16[512,4096]{1,0:T(8,128)(2,1)S(1)}, bf16[512,4096]{1,0:T(8,128)(2,1)}) custom-call(s32[2,128]{1,0:T(2,128)} %bitcast.37, f32[2,128]{1,0:T(2,128)} %bitcast.38, bf16[128,4096]{1,0:T(8,128)(2,1)} %tokens_ref.1, bf16[128,4096]{1,0:T(8,128)(2,1)} %cotangent_ref.1), custom_call_target="tpu_custom_call" | custom-call | flops 1000 | bytes 1000 | tf_op jit(solution)/shard_map/pallas_call | solution.py:37
  6.0 63.9 %all_to_all.20 = bf16[64,8,4096]{2,1,0:T(8,128)(2,1)} all-to-all(bf16[64,8,4096]{2,1,0:T(8,128)(2,1)S(1)} %bitcast.32), channel_id=1, replica_groups=mesh['dp'=2,'expert'=64] {'expert'}, dimensions={0} | all-to-all | bytes 8388608 | tf_op jit(solution)/shard_map/all_to_all | solution.py:31
  70.0 0.0 collective-permute-start
  70.0 0.0 copy-start
  70.0 6.4 %all-to-all-start.1 = ((bf16[64,8,4096]{2,1,0:T(8,128)(2,1)}), bf16[64,8,4096]{2,1,0:T(8,128)(2,1)}, u32[]{:S(2)}, u32[]{:S(2)}) async-start(bf16[64,8,4096]{2,1,0:T(8,128)(2,1)} %bitcast.36), calls=%async_computation.1 | async-start | bytes 8388608 | tf_op jit(solution)/shard_map/all_to_all | solution.py:31
  76.4 1.1 collective-permute-done.rows_ref.refs_1_
  77.5 0.0 copy-done
  77.5 0.0 copy-start.2
  77.5 1.9 copy-done.2
  79.4 0.0 copy-start.4
  79.4 1.9 copy-done.4
  81.3 11.4 %shard_map.112 = (bf16[512,384]{1,0:T(8,128)(2,1)}, f32[512,384]{1,0:T(8,128)}, f32[512,384]{1,0:T(8,128)}, bf16[256,4096]{1,0:T(8,128)(2,1)}, bf16[256,4096]{1,0:T(8,128)(2,1)}) custom-call(bf16[512,4096]{1,0:T(8,128)(2,1)} %collective-permute-done.rows_ref.refs_1_, bf16[4096,384]{1,0:T(8,128)(2,1)S(1)} %bitcast.23, bf16[4096,384]{1,0:T(8,128)(2,1)S(1)} %bitcast.27, ...), custom_call_target="tpu_custom_call" | custom-call | flops 1000 | bytes 1000 | tf_op jit(solution)/shard_map/pallas_call | solution.py:37
  92.7 0.2 collective-permute-start.1
  92.9 0.4 collective-permute-start.2
  93.3 7.2 %shard_map.111 = (bf16[512,384]{1,0:T(8,128)(2,1)}, f32[512,384]{1,0:T(8,128)}, f32[512,384]{1,0:T(8,128)}) custom-call(bf16[512,4096]{1,0:T(8,128)(2,1)} %bitcast.3.rows_ref.refs_0_, bf16[4096,384]{1,0:T(8,128)(2,1)S(1)} %bitcast.24, bf16[4096,384]{1,0:T(8,128)(2,1)S(1)} %bitcast.28), custom_call_target="tpu_custom_call" | custom-call | flops 1000 | bytes 1000 | tf_op jit(solution)/shard_map/pallas_call | solution.py:37
  100.5 0.0 collective-permute-done.1.refs_0_
  100.5 0.0 collective-permute-done.2.refs_1_
  100.5 4.8 %shard_map.113 = bf16[512,4096]{1,0:T(8,128)(2,1)} custom-call(bf16[512,384]{1,0:T(8,128)(2,1)} %get-tuple-element.47.hidden_ref.refs_4_, bf16[384,4096]{1,0:T(8,128)(2,1)S(1)} %bitcast.20, bf16[256,4096]{1,0:T(8,128)(2,1)S(1)} %collective-permute-done.1.refs_0_, bf16[256,4096]{1,0:T(8,128)(2,1)S(1)} %collective-permute-done.2.refs_1_), custom_call_target="tpu_custom_call" | custom-call | flops 1000 | bytes 1000 | tf_op jit(solution)/shard_map/pallas_call | solution.py:37
  105.3 26.4 %all-to-all-done.1 = bf16[64,8,4096]{2,1,0:T(8,128)(2,1)} async-done(((bf16[64,8,4096]{2,1,0:T(8,128)(2,1)}), bf16[64,8,4096]{2,1,0:T(8,128)(2,1)}, u32[]{:S(2)}, u32[]{:S(2)}) %all-to-all-start.1) | async-done | bytes 4194336 | tf_op jit(solution)/shard_map/all_to_all | solution.py:31
  131.7 0.0 collective-permute-start.3
  131.7 9.7 %all-to-all-start.2 = ((bf16[64,8,4096]{2,1,0:T(8,128)(2,1)}), bf16[64,8,4096]{2,1,0:T(8,128)(2,1)}, u32[]{:S(2)}, u32[]{:S(2)}) async-start(bf16[64,8,4096]{2,1,0:T(8,128)(2,1)} %bitcast.35), calls=%async_computation.2 | async-start | bytes 8388608 | tf_op jit(solution)/shard_map/all_to_all | solution.py:31
  141.4 0.0 collective-permute-done.3.grads_ref.refs_3_
  141.4 0.0 copy-start.8
  141.4 0.0 copy-start.7
  141.4 0.0 copy-start.1
  141.4 14.5 %shard_map.115 = (bf16[512,384]{1,0:T(8,128)(2,1)}, bf16[512,384]{1,0:T(8,128)(2,1)}, bf16[256,4096]{1,0:T(8,128)(2,1)}, bf16[256,4096]{1,0:T(8,128)(2,1)}) custom-call(bf16[512,4096]{1,0:T(8,128)(2,1)} %collective-permute-done.3.grads_ref.refs_3_, f32[512,384]{1,0:T(8,128)} %get-tuple-element.56.act_ref, f32[512,384]{1,0:T(8,128)} %get-tuple-element.57.slope_ref, ...), custom_call_target="tpu_custom_call" | custom-call | flops 1000 | bytes 1000 | tf_op jit(solution)/shard_map/pallas_call | solution.py:37
  155.9 0.3 collective-permute-start.4
  156.2 0.3 collective-permute-start.5
  156.5 0.0 copy-done.8
  156.5 0.1 copy.12
  156.6 0.0 copy-done.7
  156.6 0.1 copy.13
  156.8 0.0 copy-done.1
  156.8 5.1 %shard_map.114 = (bf16[512,384]{1,0:T(8,128)(2,1)}, bf16[512,384]{1,0:T(8,128)(2,1)}) custom-call(bf16[512,4096]{1,0:T(8,128)(2,1)} %bitcast.5.grads_ref.refs_2_, f32[512,384]{1,0:T(8,128)} %get-tuple-element.52.act_ref, f32[512,384]{1,0:T(8,128)} %get-tuple-element.53.slope_ref, bf16[384,4096]{1,0:T(8,128)(2,1)S(1)} %bitcast.21), custom_call_target="tpu_custom_call" | custom-call | flops 1000 | bytes 1000 | tf_op jit(solution)/shard_map/pallas_call | solution.py:37
  161.9 0.0 copy-start.3
  161.9 0.0 copy-start.5
  161.9 15.1 %shard_map.117 = (bf16[4096,384]{1,0:T(8,128)(2,1)}, bf16[4096,384]{1,0:T(8,128)(2,1)}, bf16[384,4096]{1,0:T(8,128)(2,1)}) custom-call(bf16[512,4096]{1,0:T(8,128)(2,1)} %bitcast.3.rows_ref.refs_0_, bf16[512,4096]{1,0:T(8,128)(2,1)} %collective-permute-done.rows_ref.refs_1_, bf16[512,4096]{1,0:T(8,128)(2,1)} %bitcast.5.grads_ref.refs_2_, ...), custom_call_target="tpu_custom_call" | custom-call | flops 1000 | bytes 1000 | tf_op jit(solution)/shard_map/pallas_call | solution.py:37
  177.0 0.0 collective-permute-done.4.refs_0_
  177.0 0.0 collective-permute-done.5.refs_1_
  177.0 0.0 copy-done.3
  177.0 0.0 copy-done.5
  177.0 7.3 %shard_map.116 = bf16[512,4096]{1,0:T(8,128)(2,1)S(1)} custom-call(bf16[512,384]{1,0:T(8,128)(2,1)} %get-tuple-element.54.gate_grad_ref.refs_6_, bf16[512,384]{1,0:T(8,128)(2,1)} %get-tuple-element.55.up_grad_ref.refs_8_, bf16[4096,384]{1,0:T(8,128)(2,1)S(1)} %bitcast.25, bf16[4096,384]{1,0:T(8,128)(2,1)S(1)} %bitcast.29, ...), custom_call_target="tpu_custom_call" | custom-call | flops 1000 | bytes 1000 | tf_op jit(solution)/shard_map/pallas_call | solution.py:37
  184.2 0.0 copy-start.6
  184.3 2.0 copy-done.6
  186.2 10.2 %all-to-all-done.2 = bf16[64,8,4096]{2,1,0:T(8,128)(2,1)} async-done(((bf16[64,8,4096]{2,1,0:T(8,128)(2,1)}), bf16[64,8,4096]{2,1,0:T(8,128)(2,1)}, u32[]{:S(2)}, u32[]{:S(2)}) %all-to-all-start.2) | async-done | bytes 4194336 | tf_op jit(solution)/shard_map/all_to_all | solution.py:31
  196.4 62.2 %all_to_all.21 = bf16[64,8,4096]{2,1,0:T(8,128)(2,1)S(1)} all-to-all(bf16[64,8,4096]{2,1,0:T(8,128)(2,1)} %bitcast.31), channel_id=1, replica_groups=mesh['dp'=2,'expert'=64] {'expert'}, dimensions={0} | all-to-all | bytes 8388608 | tf_op jit(solution)/shard_map/all_to_all | solution.py:31
  258.7 4.6 %shard_map.118 = (bf16[128,4096]{1,0:T(8,128)(2,1)}, bf16[128,4096]{1,0:T(8,128)(2,1)}) custom-call(s32[128,2]{1,0:T(8,128)S(1)} %bitcast.33, f32[128,2]{1,0:T(8,128)S(1)} %bitcast.34, bf16[512,4096]{1,0:T(8,128)(2,1)} %bitcast.10.out_ref, bf16[512,4096]{1,0:T(8,128)(2,1)S(1)} %bitcast.30), custom_call_target="tpu_custom_call" | custom-call | flops 1000 | bytes 1000 | tf_op jit(solution)/shard_map/pallas_call | solution.py:37
Async XLA Ops:
  70.0 7.5 %collective-permute-start = (bf16[512,4096]{1,0:T(8,128)(2,1)}, bf16[512,4096]{1,0:T(8,128)(2,1)}, u32[]{:S(2)}, u32[]{:S(2)}) collective-permute-start(bf16[512,4096]{1,0:T(8,128)(2,1)} %bitcast.3.rows_ref.refs_0_), channel_id=1, source_target_pairs={{0,64},{64,0},{1,65},{65,1},{2,66},{66,2},{3,67},{67,3},{4,68},{68... | collective-permute-start | bytes 12582920 | tf_op jit(solution)/shard_map/ppermute | solution.py:25
  70.0 7.5 %copy-start = (bf16[1,384,4096]{2,1,0:T(8,128)(2,1)S(1)}, bf16[1,384,4096]{2,1,0:T(8,128)(2,1)}, u32[]{:S(2)}) copy-start(bf16[1,384,4096]{2,1,0:T(8,128)(2,1)} %param.13) | copy-start | bytes 9437188
  70.0 61.7 %all-to-all-start.1 = ((bf16[64,8,4096]{2,1,0:T(8,128)(2,1)}), bf16[64,8,4096]{2,1,0:T(8,128)(2,1)}, u32[]{:S(2)}, u32[]{:S(2)}) async-start(bf16[64,8,4096]{2,1,0:T(8,128)(2,1)} %bitcast.36), calls=%async_computation.1 | async-start | bytes 8388608 | tf_op jit(solution)/shard_map/all_to_all | solution.py:31
  77.5 1.9 copy-start.2
  79.4 1.9 copy-start.4
  92.7 7.8 %collective-permute-start.1 = (bf16[256,4096]{1,0:T(8,128)(2,1)}, bf16[256,4096]{1,0:T(8,128)(2,1)S(1)}, u32[]{:S(2)}, u32[]{:S(2)}) collective-permute-start(bf16[256,4096]{1,0:T(8,128)(2,1)} %get-tuple-element.48), channel_id=1, source_target_pairs={{0,64},{64,0},{1,65},{65,1},{2,66},{66,2},{3,67},{67,3},{4,68},{68... | collective-permute-start | bytes 6291464 | tf_op jit(solution)/shard_map/ppermute | solution.py:25
  92.9 7.6 %collective-permute-start.2 = (bf16[256,4096]{1,0:T(8,128)(2,1)}, bf16[256,4096]{1,0:T(8,128)(2,1)S(1)}, u32[]{:S(2)}, u32[]{:S(2)}) collective-permute-start(bf16[256,4096]{1,0:T(8,128)(2,1)} %get-tuple-element.49), channel_id=1, source_target_pairs={{0,64},{64,0},{1,65},{65,1},{2,66},{66,2},{3,67},{67,3},{4,68},{68... | collective-permute-start | bytes 6291464 | tf_op jit(solution)/shard_map/ppermute | solution.py:25
  131.7 9.7 %collective-permute-start.3 = (bf16[512,4096]{1,0:T(8,128)(2,1)}, bf16[512,4096]{1,0:T(8,128)(2,1)}, u32[]{:S(2)}, u32[]{:S(2)}) collective-permute-start(bf16[512,4096]{1,0:T(8,128)(2,1)} %bitcast.5.grads_ref.refs_2_), channel_id=1, source_target_pairs={{0,64},{64,0},{1,65},{65,1},{2,66},{66,2},{3,67},{67,3},{4,68},{68... | collective-permute-start | bytes 12582920 | tf_op jit(solution)/shard_map/ppermute | solution.py:25
  131.7 64.7 %all-to-all-start.2 = ((bf16[64,8,4096]{2,1,0:T(8,128)(2,1)}), bf16[64,8,4096]{2,1,0:T(8,128)(2,1)}, u32[]{:S(2)}, u32[]{:S(2)}) async-start(bf16[64,8,4096]{2,1,0:T(8,128)(2,1)} %bitcast.35), calls=%async_computation.2 | async-start | bytes 8388608 | tf_op jit(solution)/shard_map/all_to_all | solution.py:31
  141.4 15.1 %copy-start.8 = (s32[2,128]{1,0:T(2,128)S(1)}, s32[2,128]{1,0:T(2,128)}, u32[]{:S(2)}) copy-start(s32[2,128]{1,0:T(2,128)} %get-tuple-element.60) | copy-start | bytes 3076
  141.4 15.2 %copy-start.7 = (f32[2,128]{1,0:T(2,128)S(1)}, f32[2,128]{1,0:T(2,128)}, u32[]{:S(2)}) copy-start(f32[2,128]{1,0:T(2,128)} %get-tuple-element.61) | copy-start | bytes 3076
  141.4 15.4 %copy-start.1 = (bf16[1,384,4096]{2,1,0:T(8,128)(2,1)S(1)}, bf16[1,384,4096]{2,1,0:T(8,128)(2,1)}, u32[]{:S(2)}) copy-start(bf16[1,384,4096]{2,1,0:T(8,128)(2,1)} %param.13) | copy-start | bytes 9437188
  155.9 21.0 %collective-permute-start.4 = (bf16[256,4096]{1,0:T(8,128)(2,1)}, bf16[256,4096]{1,0:T(8,128)(2,1)}, u32[]{:S(2)}, u32[]{:S(2)}) collective-permute-start(bf16[256,4096]{1,0:T(8,128)(2,1)} %get-tuple-element.58), channel_id=1, source_target_pairs={{0,64},{64,0},{1,65},{65,1},{2,66},{66,2},{3,67},{67,3},{4,68},{68... | collective-permute-start | bytes 6291464 | tf_op jit(solution)/shard_map/ppermute | solution.py:25
  156.2 20.8 %collective-permute-start.5 = (bf16[256,4096]{1,0:T(8,128)(2,1)}, bf16[256,4096]{1,0:T(8,128)(2,1)}, u32[]{:S(2)}, u32[]{:S(2)}) collective-permute-start(bf16[256,4096]{1,0:T(8,128)(2,1)} %get-tuple-element.59), channel_id=1, source_target_pairs={{0,64},{64,0},{1,65},{65,1},{2,66},{66,2},{3,67},{67,3},{4,68},{68... | collective-permute-start | bytes 6291464 | tf_op jit(solution)/shard_map/ppermute | solution.py:25
  161.9 15.1 %copy-start.3 = (bf16[1,4096,384]{2,1,0:T(8,128)(2,1)S(1)}, bf16[1,4096,384]{2,1,0:T(8,128)(2,1)}, u32[]{:S(2)}) copy-start(bf16[1,4096,384]{2,1,0:T(8,128)(2,1)} %param.11) | copy-start | bytes 9437188
  161.9 15.1 %copy-start.5 = (bf16[1,4096,384]{2,1,0:T(8,128)(2,1)S(1)}, bf16[1,4096,384]{2,1,0:T(8,128)(2,1)}, u32[]{:S(2)}) copy-start(bf16[1,4096,384]{2,1,0:T(8,128)(2,1)} %param.12) | copy-start | bytes 9437188
  184.2 2.0 copy-start.6
